TPU v7x, 128 devices: a whole 4x4x4 slice. The times are simulated.
128 devices in a mesh: row: 8 (over y, core), col: 16 (over z, x).
Axes of the slice: x: 4, y: 4, z: 4, core: 2. Of those that a mesh axis runs over, the one named last changes fastest.
Arguments:
- x_blocks: float32 [8, 64, 9, 128, 128], P('row', 'col'), may hold values from -1.2 to 1.2
- pattern: int32 [8, 64, 9], P('row', 'col'), may hold values 0 or 1
- alpha: float32 [], replicated, may hold values from 1 to 2
- beta: float32 [], replicated, may hold values from -1 to -0.5
Outputs:
- updated: float32 [8, 64, 9, 128, 128], P('row', 'col')
- trace: float32 [], replicated
All inputs are finite; a program needn't handle non-finite values. No bound on the sum of `pattern` on one device may be relied on, other than what follows from the above.
Results may differ from a plain program's by a relative error of at most 0.0001.
Values sent between devices are 32-bit elements; how exact they have to be, the bound alone decides.
No kernel may reach another device: no remote copies, remote signals or barrier semaphores. Data moves between devices by JAX's collectives and lax.ppermute only.
A program may use at most 64 MiB of HBM per device.

v0:
```python
import jax
import jax.numpy as jnp
from jax import lax
from jax.sharding import PartitionSpec as P

STENCIL = [(-1, -1), (-1, 0), (-1, 1), (0, -1), (0, 0), (0, 1), (1, -1), (1, 0), (1, 1)]


def padded(x, sides, width):
    for axis, dim in sides:
        peers, length = (lax.axis_size(axis), x.shape[dim])
        up = [(i, (i + 1) % peers) for i in range(peers)]
        down = [(j, i) for i, j in up]
        last = lax.slice_in_dim(x, length - width, length, axis=dim)
        initial = lax.slice_in_dim(x, 0, width, axis=dim)
        before = lax.ppermute(last, axis, up)
        after = lax.ppermute(initial, axis, down)
        x = jnp.concatenate([before, x, after], axis=dim)
    return x


def slot_of(step_u, step_v):
    if abs(step_u) > 1 or abs(step_v) > 1:
        return -1
    return (step_u + 1) * 3 + step_v + 1


def add_source(sums, left, shifted, source):
    step_u, step_v = STENCIL[source]
    result = list(sums)
    for target, (goal_u, goal_v) in enumerate(STENCIL):
        other = slot_of(goal_u - step_u, goal_v - step_v)
        if other >= 0:
            result[target] = result[target] + jnp.einsum(
                "uvpm,uvmq->uvpq", left, shifted[:, :, other], precision=lax.Precision.HIGHEST
            )
    return result


def body(x_blocks, pattern, alpha, beta):
    weights = pattern.astype(jnp.float32)[:, :, :, None, None]
    masked = x_blocks * weights
    rows_u = masked.shape[0]
    rows_v = masked.shape[1]
    block_shape = masked.shape[:2] + masked.shape[3:]
    sums = [jnp.zeros(block_shape, jnp.float32) for target in range(9)]
    extended = padded(masked, (("row", 0), ("col", 1)), 1)
    for source, (step_u, step_v) in enumerate(STENCIL):
        shifted = extended[1 + step_u : 1 + step_u + rows_u, 1 + step_v : 1 + step_v + rows_v]
        sums = add_source(sums, masked[:, :, source], shifted, source)
    product = jnp.stack(sums, axis=2)
    updated = weights * (alpha * masked + beta * product)
    local_trace = jnp.sum(jnp.diagonal(updated[:, :, 4], axis1=2, axis2=3))
    total_rows = rows_u * rows_v * lax.axis_size("row") * lax.axis_size("col")
    trace = lax.psum(local_trace, ("row", "col")) / total_rows
    return (updated, trace)


def solution(mesh):
    placed = (P("row", "col", None, None, None), P("row", "col", None), P(), P())
    return jax.shard_map(
        body,
        mesh=mesh,
        in_specs=placed,
        out_specs=(P("row", "col", None, None, None), P()),
        check_vma=False,
    )
```

profile of v0, /device:TPU:1, one launch (start us, length us, event | category | flops | bytes accessed | tf_op | source)
XLA Modules:
  0.0 203.6 jit_solution(12934327311969011518)
XLA Ops:
  0.6 0.7 convert_bitcast_fusion
  1.4 3.3 %copy_multiply_fusion = f32[1,4,9,128,128]{4,3,1,2,0:T(8,128)} fusion(f32[1,4,9,128,128]{4,3,2,1,0:T(8,128)} %param.4, f32[4,9]{0,1:T(8,128)S(1)} %copy.6), kind=kLoop, calls=%fused_computation.1 | loop fusion | flops 589824 | bytes 4718736 | tf_op jit(solution)/shard_map/mul | solution.py:42
  4.7 2.7 %collective-permute-start = (f32[1,4,9,128,128]{4,3,1,2,0:T(8,128)}, f32[1,4,9,128,128]{4,3,1,2,0:T(8,128)}, u32[]{:S(2)}, u32[]{:S(2)}) collective-permute-start(f32[1,4,9,128,128]{4,3,1,2,0:T(8,128)} %copy_multiply_fusion), channel_id=1, source_target_pairs={{0,16},{16,32},{32,48},{48,64},{64,80},{80,96},{96,112},{112,0},{1... | collective-permute-start | bytes 7077896 | tf_op jit(solution)/shard_map/ppermute | solution.py:16
  8.7 1.4 fusion.238
  10.1 1.4 fusion.236
  11.6 1.4 fusion.235
  13.0 1.4 fusion.231
  14.4 1.4 fusion.234
  15.8 1.4 fusion.230
  17.3 1.4 fusion.232
  18.7 1.4 fusion.237
  20.1 1.4 fusion.233
  21.5 12.0 %collective-permute-done = f32[1,4,9,128,128]{4,3,1,2,0:T(8,128)} collective-permute-done((f32[1,4,9,128,128]{4,3,1,2,0:T(8,128)}, f32[1,4,9,128,128]{4,3,1,2,0:T(8,128)}, u32[]{:S(2)}, u32[]{:S(2)}) %collective-permute-start) | collective-permute-done | bytes 2359328 | tf_op jit(solution)/shard_map/ppermute | solution.py:16
  33.5 2.4 %collective-permute-done.1 = f32[1,4,9,128,128]{4,3,1,2,0:T(8,128)S(1)} collective-permute-done((f32[1,4,9,128,128]{4,3,1,2,0:T(8,128)}, f32[1,4,9,128,128]{4,3,1,2,0:T(8,128)S(1)}, u32[]{:S(2)}, u32[]{:S(2)}) %collective-permute-start.1) | collective-permute-done | bytes 2359328 | tf_op jit(solution)/shard_map/ppermute | solution.py:17
  35.9 1.9 pad_maximum_fusion
  37.7 6.0 %collective-permute-start.3 = (f32[3,1,9,128,128]{4,3,1,2,0:T(8,128)S(1)}, f32[3,1,9,128,128]{4,3,1,2,0:T(8,128)S(1)}, u32[]{:S(2)}, u32[]{:S(2)}) collective-permute-start(f32[3,1,9,128,128]{4,3,1,2,0:T(8,128)S(1)} %get-tuple-element.4), channel_id=1, source_target_pairs={{1,0},{2,1},{3,2},{4,3},{5,4},{6,5},{7,6},{8,7},{9,8},{10,9},{11,1... | collective-permute-start | bytes 5308424 | tf_op jit(solution)/shard_map/ppermute | solution.py:17
  43.8 1.4 fusion.148
  45.2 1.4 fusion.169
  46.6 1.4 fusion.209
  48.0 1.4 fusion.223
  49.5 1.3 fusion.155
  50.8 1.3 fusion.120
  52.2 1.3 fusion.99
  53.5 1.3 fusion.78
  54.9 1.3 fusion.60
  56.2 25.4 %collective-permute-done.3 = f32[3,1,9,128,128]{4,3,1,2,0:T(8,128)S(1)} collective-permute-done((f32[3,1,9,128,128]{4,3,1,2,0:T(8,128)S(1)}, f32[3,1,9,128,128]{4,3,1,2,0:T(8,128)S(1)}, u32[]{:S(2)}, u32[]{:S(2)}) %collective-permute-start.3) | collective-permute-done | bytes 1769504 | tf_op jit(solution)/shard_map/ppermute | solution.py:17
  81.6 1.4 fusion.106
  83.0 1.4 fusion.141
  84.4 2.4 %collective-permute-done.2 = f32[3,1,9,128,128]{4,3,1,2,0:T(8,128)S(1)} collective-permute-done((f32[3,1,9,128,128]{4,3,1,2,0:T(8,128)S(1)}, f32[3,1,9,128,128]{4,3,1,2,0:T(8,128)S(1)}, u32[]{:S(2)}, u32[]{:S(2)}) %collective-permute-start.2) | collective-permute-done | bytes 1769504 | tf_op jit(solution)/shard_map/ppermute | solution.py:16
  86.8 1.4 fusion.134
  88.2 1.4 fusion.162
  89.6 1.4 fusion.182
  91.0 1.4 fusion.202
  92.4 1.4 fusion.195
  93.9 1.4 fusion.216
  95.3 1.3 fusion.113
  96.6 1.3 fusion.121
  98.0 1.3 fusion.92
  99.3 1.3 fusion.79
  100.7 1.3 fusion.53
  102.0 1.3 fusion.62
  103.4 1.4 fusion.65
  104.8 1.3 fusion.44
  106.1 1.4 convolution_add_fusion.1
  107.5 1.4 fusion.6
  109.0 1.4 fusion.15
  110.4 1.4 fusion.22
  111.8 1.4 fusion.24
  113.3 1.4 fusion.17
  114.7 1.4 fusion.14
  116.1 1.6 fusion.25
  117.7 1.3 fusion.11
  119.1 1.4 fusion.27
  120.5 1.4 fusion.31
  121.9 1.4 fusion.34
  123.4 1.4 fusion.37
  124.8 1.6 fusion.42
  126.4 1.3 fusion.2
  127.8 0.6 add_multiply_fusion
  128.4 4.7 %copy.8 = f32[4,128,128]{0,2,1:T(8,128)} copy(f32[4,128,128]{2,1,0:T(8,128)S(1)} %slice_bitcast_fusion) | data formatting | bytes 524288 | tf_op jit(solution)/shard_map/squeeze | solution.py:53
  133.0 1.8 gather_fusion
  134.8 0.6 reduce
  135.4 1.6 copy.9
  137.0 64.9 %psum.7 = f32[]{:T(128)} all-reduce(f32[]{:T(128)} %reduce), channel_id=1, replica_groups=mesh['row'=8,'col'=16] {'row','col'}, use_global_device_ids=true, to_apply=%region_1.2 | all-reduce | flops 1 | bytes 8 | tf_op jit(solution)/shard_map/psum | solution.py:55
  (7 shorter events, 0.1 us)
Async XLA Ops:
  4.7 28.8 %collective-permute-start = (f32[1,4,9,128,128]{4,3,1,2,0:T(8,128)}, f32[1,4,9,128,128]{4,3,1,2,0:T(8,128)}, u32[]{:S(2)}, u32[]{:S(2)}) collective-permute-start(f32[1,4,9,128,128]{4,3,1,2,0:T(8,128)} %copy_multiply_fusion), channel_id=1, source_target_pairs={{0,16},{16,32},{32,48},{48,64},{64,80},{80,96},{96,112},{112,0},{1... | collective-permute-start | bytes 7077896 | tf_op jit(solution)/shard_map/ppermute | solution.py:16
  7.4 28.5 %collective-permute-start.1 = (f32[1,4,9,128,128]{4,3,1,2,0:T(8,128)}, f32[1,4,9,128,128]{4,3,1,2,0:T(8,128)S(1)}, u32[]{:S(2)}, u32[]{:S(2)}) collective-permute-start(f32[1,4,9,128,128]{4,3,1,2,0:T(8,128)} %copy_multiply_fusion), channel_id=1, source_target_pairs={{16,0},{32,16},{48,32},{64,48},{80,64},{96,80},{112,96},{0,112},{1... | collective-permute-start | bytes 7077896 | tf_op jit(solution)/shard_map/ppermute | solution.py:17
  37.7 43.9 %collective-permute-start.3 = (f32[3,1,9,128,128]{4,3,1,2,0:T(8,128)S(1)}, f32[3,1,9,128,128]{4,3,1,2,0:T(8,128)S(1)}, u32[]{:S(2)}, u32[]{:S(2)}) collective-permute-start(f32[3,1,9,128,128]{4,3,1,2,0:T(8,128)S(1)} %get-tuple-element.4), channel_id=1, source_target_pairs={{1,0},{2,1},{3,2},{4,3},{5,4},{6,5},{7,6},{8,7},{9,8},{10,9},{11,1... | collective-permute-start | bytes 5308424 | tf_op jit(solution)/shard_map/ppermute | solution.py:17
  43.8 43.1 %collective-permute-start.2 = (f32[3,1,9,128,128]{4,3,1,2,0:T(8,128)S(1)}, f32[3,1,9,128,128]{4,3,1,2,0:T(8,128)S(1)}, u32[]{:S(2)}, u32[]{:S(2)}) collective-permute-start(f32[3,1,9,128,128]{4,3,1,2,0:T(8,128)S(1)} %get-tuple-element.5), channel_id=1, source_target_pairs={{0,1},{1,2},{2,3},{3,4},{4,5},{5,6},{6,7},{7,8},{8,9},{9,10},{10,1... | collective-permute-start | bytes 5308424 | tf_op jit(solution)/shard_map/ppermute | solution.py:16
  124.8 3.0 %copy-start = (f32[1,4,9,128,128]{4,3,2,1,0:T(8,128)S(1)}, f32[1,4,9,128,128]{4,3,2,1,0:T(8,128)}, u32[]{:S(2)}) copy-start(f32[1,4,9,128,128]{4,3,2,1,0:T(8,128)} %param.4) | copy-start | bytes 7077892
where the time goes:
time: 205 us; the launch traced here: 204 us
  matrix products  68.6 us (33%)
  blocking collectives  64.9 us (32%)
  waiting for transfers between devices  42.2 us (21%)
  starting transfers between devices  8.71 us (4%)
  local copies, waits for them, and re-layouts  8.09 us (4%)
  other arithmetic  7.04 us (3%)
  between operations  4.13 us (2%)
    dot_general x49, matrix products, add_source(): jnp.einsum('uvpm,uvmq->uvpq', left, shifted[:, :, other], precision=lax.P...  68.6 us
    psum x1, blocking collectives, body(): trace = lax.psum(local_trace, ('row', 'col')) / total_rows  64.9 us
    ppermute x2, waiting for transfers between devices, padded(): after = lax.ppermute(initial, axis, down)  27.8 us
    ppermute x2, waiting for transfers between devices, padded(): before = lax.ppermute(last, axis, up)  14.4 us
    ppermute x2, starting transfers between devices, padded(): after = lax.ppermute(initial, axis, down)  6.02 us
    squeeze x2, local copies, waits for them, and re-layouts, body(): local_trace = jnp.sum(jnp.diagonal(updated[:, :, 4], axis1=2, axis2=3))  4.68 us
  transfers between devices with their start and end apart: 4, of which 4 were waited for; matrix products, arithmetic and copies ran while one was open for 14% of the time, Pallas kernels for 0%

commit v1 on v0

v1 whole, which is shorter than its diff:
```python
import functools

import jax
import jax.numpy as jnp
from jax import lax
from jax.experimental import pallas as pl
from jax.experimental.pallas import tpu as pltpu
from jax.sharding import PartitionSpec as P

CR, MID, TW = 0, 1, 2
AXES = ("row", "col")
B = 128
F32 = jnp.float32
BF16 = jnp.bfloat16
VMEM_LIMIT = 24 * 1024 * 1024
PARAMS = pltpu.CompilerParams(vmem_limit_bytes=VMEM_LIMIT)

CROSS1 = [(CR, 0, -1), (CR, 0, 0), (CR, 3, 0), (CR, 3, 1), (CR, 0, 1), (CR, 1, 1), (CR, 2, 1), (CR, "m", 0)]
CROSS2 = [(MID, 0, -1), (MID, 0, 0), (MID, 3, 0), (MID, 3, 1), (CR, 1, -1), (CR, 2, -1), (CR, 3, -1), (CR, "n", 0)]
CROSS3 = [(MID, 0, 1), (MID, 1, -1), (MID, 1, 0), (MID, 1, 1), (MID, 2, -1), (MID, 2, 0), (MID, 2, 1), (MID, 3, -1)]
TWIN = [(TW, v, j) for v in range(4) for j in (-1, 0, 1)] + [(MID, v, j) for v in range(4) for j in (-1, 0, 1)]
EAST1 = [(k, 3, 1) for k in (CR, MID, TW)]
EAST2 = [(k, 3, 0) for k in (CR, MID, TW)]
WEST = [(k, 0, j) for k in (CR, MID, TW) for j in (-1, 0)]


def parity():
    return lax.rem(lax.axis_index("row"), 2)


def slot(kind, dv, odd):
    base = {CR: 6 * odd, MID: 3, TW: 6 - 6 * odd}[kind]
    return base + dv + 1


def cell(v, odd):
    if isinstance(v, str):
        return 1 + odd if v == "m" else 2 - odd
    return v


def weight(pat, v, s):
    return pat[0, v, s].astype(F32)


def own(x, pat, kind, v, dv, odd):
    s = slot(kind, dv, odd)
    v = cell(v, odd)
    return x[0, v, s] * weight(pat, v, s)


def split(block):
    high = block.astype(BF16)
    return high, (block - high.astype(F32)).astype(BF16)


def dot3(left, right):
    def side(blocks, part):
        return jnp.concatenate([jnp.concatenate([b[part] for b in line], axis=1) for line in blocks], axis=0)

    lh, ll, rh, rl = side(left, 0), side(left, 1), side(right, 0), side(right, 1)
    return jnp.dot(
        jnp.concatenate([lh, lh, ll], axis=1), jnp.concatenate([rh, rl, rh], axis=0), preferred_element_type=F32
    )


def put(ref, index, block):
    ref[pl.ds(index * B, B), :] = block


def get(ref, index):
    return ref[pl.ds(index * B, B), :]


def put_present(ref, count, pat):
    row = lax.broadcasted_iota(jnp.int32, (8, B), 0)
    value = jnp.zeros((8, B), F32)
    for v in range(4):
        value = jnp.where(row == v, weight(pat, v, 4), value)
    ref[pl.ds(count * B, 8), :] = value


def get_present(ref, count, v):
    return ref[pl.ds(count * B + v, 1), :]


def pack_kernel(messages, present, x, pat, *outs):
    odd = parity()
    for out, message, extra in zip(outs, messages, present):
        for i, (kind, v, dv) in enumerate(message):
            put(out, i, own(x, pat, kind, v, dv, odd))
        if extra:
            put_present(out, len(message), pat)


def pack(x, pat, messages, present):
    shapes = [jax.ShapeDtypeStruct((len(m) * B + 8 * e, B), F32) for m, e in zip(messages, present)]
    return pl.pallas_call(
        functools.partial(pack_kernel, messages, present),
        out_shape=shapes,
        in_specs=[pl.BlockSpec(memory_space=pltpu.VMEM), pl.BlockSpec(memory_space=pltpu.SMEM)],
        out_specs=[pl.BlockSpec(memory_space=pltpu.VMEM)] * len(shapes),
        compiler_params=PARAMS,
        cost_estimate=pl.CostEstimate(flops=0, bytes_accessed=4000000, transcendentals=0),
    )(x, pat)


def trace_kernel(x, pat, alpha, beta, c1, tw, e1, out):
    odd = parity()
    mine = functools.partial(own, x, pat, odd=odd)
    present = lambda v: weight(pat, v, 4)
    pairs = []
    for v in range(4):
        pairs.append((1.0, mine(MID, v, 0), mine(MID, v, 0)))
    for v in range(3):
        pairs.append((present(v) + present(v + 1), mine(MID, v, 1), mine(MID, v + 1, -1)))
    west = get_present(e1, 3, 3)
    pairs.append((west + present(0), mine(MID, 0, -1), get(e1, 1)))
    middle = 2 - odd
    for kind, ref, blocks, count in ((CR, c1, CROSS1, 8), (TW, tw, TWIN, 24)):
        far = functools.partial(get_present, ref, count)
        take = lambda v, dv: get(ref, blocks.index((kind, v, dv)))
        pairs.append((present(0), mine(kind, 0, 0), take(0, 0)))
        pairs.append((present(3), mine(kind, 3, 0), take(3, 0)))
        for w in range(3):
            pairs.append((present(w + 1) + far(w), mine(kind, w + 1, -1), take(w, 1)))
        if kind == CR:
            center = get(c1, blocks.index((CR, "m", 0)))
        else:
            center = tw[pl.ds(pl.multiple_of((middle * 3 + 1) * B, B), B), :]
        far_middle = jnp.where(odd == 1, far(1), far(2))
        pairs.append((present(middle) + far_middle, mine(kind, middle, 0), center))
        pairs.append((west + far(0), get(e1, kind), take(0, -1)))
    total = jnp.zeros((B, B), F32)
    for start in range(0, len(pairs), 11):
        part = pairs[start : start + 11]
        total += dot3([[split(a * w) for w, a, _ in part]], [[split(b)] for _, _, b in part])
    linear = mine(MID, 0, 0) + mine(MID, 1, 0) + mine(MID, 2, 0) + mine(MID, 3, 0)
    value = alpha[0] * linear + beta[0] * total
    rows = lax.broadcasted_iota(jnp.int32, (B, B), 0)
    columns = lax.broadcasted_iota(jnp.int32, (B, B), 1)
    line = jnp.sum(jnp.where(rows == columns, value, 0.0), axis=0, keepdims=True)
    out[...] = jnp.broadcast_to(line, (B, B))


def near_kernel(x, pat, tw, acc, oh, ol, th, tl):
    odd = parity()
    for v in range(4):
        for kind in (CR, MID, TW):
            for j in (-1, 0, 1):
                i = kind * 12 + v * 3 + j + 1
                oh[i], ol[i] = split(own(x, pat, kind, v, j, odd))
    for i in range(24):
        th[i], tl[i] = split(get(tw, i))
    mine = lambda kind, v, j: (oh[kind * 12 + v * 3 + j + 1], ol[kind * 12 + v * 3 + j + 1])
    far = lambda kind, v, j: (th[(kind == MID) * 12 + v * 3 + j + 1], tl[(kind == MID) * 12 + v * 3 + j + 1])
    seen = set()

    def add(kind, v, sv, block):
        i = kind * 12 + v * 3 + sv + 1
        if i in seen:
            acc[i] += block
        else:
            seen.add(i)
            acc[i] = block

    for w in range(4):
        for t in (0, -1, 1):
            targets = [(w - a, a) for a in (-1, 0, 1) if 0 <= w - a < 4 and -1 <= a + t <= 1]
            left = [[mine(MID, v, a), mine(TW, v, a)] for v, a in targets]
            right = [[mine(MID, w, t), mine(TW, w, t)], [far(TW, w, t), far(MID, w, t)]]
            both = dot3(left, right)
            only = dot3([line[:1] for line in left], [[mine(CR, w, t)]])
            for n, (v, a) in enumerate(targets):
                rows = slice(n * B, (n + 1) * B)
                add(MID, v, a + t, both[rows, :B])
                add(TW, v, a + t, both[rows, B:])
                add(CR, v, a + t, only[rows])


def final_kernel(x, pat, alpha, beta, acc, c1, c2, c3, e1, e2, we, fe, fw, tc, out):
    odd = parity()
    mine = lambda kind, v, j: split(own(x, pat, kind, v, j, odd))
    part = lambda ref, i: split(get(ref, i))
    index = lambda kind, v, sv: kind * 12 + v * 3 + sv + 1

    def spread(left, rights, places):
        result = dot3([[left]], [rights])
        for n, (kind, v, sv) in enumerate(places):
            acc[index(kind, v, sv)] += result[:, n * B : (n + 1) * B]

    kinds = (CR, MID, TW)
    spread(mine(MID, 0, -1), [part(ref, k) for ref in (e2, e1) for k in kinds], [(k, 0, s) for s in (-1, 0) for k in kinds])
    spread(mine(MID, 3, 1), [part(we, i) for i in range(6)], [(k, 3, s) for k in kinds for s in (0, 1)])
    spread(mine(TW, 0, -1), [part(tc, i) for i in range(4)], [(MID, 0, -1), (MID, 0, 0), (TW, 0, -1), (TW, 0, 0)])
    spread(mine(TW, 3, 1), [part(tc, i) for i in range(4, 8)], [(MID, 3, 0), (MID, 3, 1), (TW, 3, 0), (TW, 3, 1)])
    spread(mine(CR, 0, -1), [part(fe, i) for i in range(4)], [(MID, 0, -1), (MID, 0, 0), (CR, 0, -1), (CR, 0, 0)])
    spread(mine(CR, 3, 1), [part(fw, i) for i in range(4)], [(MID, 3, 0), (MID, 3, 1), (CR, 3, 0), (CR, 3, 1)])

    def center(w):
        m, n = get(c1, 7), get(c2, 7)
        return split(jnp.where(odd == 1, m, n) if w == 1 else jnp.where(odd == 1, n, m))

    def far(kind, w, t):
        key = (kind, w, t)
        for ref, blocks in ((c1, CROSS1), (c2, CROSS2), (c3, CROSS3)):
            if key in blocks:
                return part(ref, blocks.index(key))
        return center(w)

    lefts = {(v, a): mine(CR, v, a) for v in range(4) for a in (-1, 0, 1)}
    for w in range(4):
        for t in (0, -1, 1):
            targets = [(w - a, a) for a in (-1, 0, 1) if 0 <= w - a < 4 and -1 <= a + t <= 1]
            result = dot3([[lefts[key]] for key in targets], [[far(CR, w, t), far(MID, w, t)]])
            for n, (v, a) in enumerate(targets):
                rows = slice(n * B, (n + 1) * B)
                acc[index(MID, v, a + t)] += result[rows, :B]
                acc[index(CR, v, a + t)] += result[rows, B:]
    for v in range(4):
        for kind in kinds:
            for sv in (-1, 0, 1):
                s = slot(kind, sv, odd)
                p = weight(pat, v, s)
                out[0, v, s] = p * (alpha[0] * (p * x[0, v, s]) + beta[0] * acc[index(kind, v, sv)])


def body(x, pat, alpha, beta):
    rows, columns = lax.axis_size("row"), lax.axis_size("col")

    def moved(message, step):
        pairs = []
        for r in range(rows):
            for c in range(columns):
                r2, c2 = step(r, c)
                pairs.append((r * columns + c, (r2 % rows) * columns + c2 % columns))
        return lax.ppermute(message, AXES, pairs)

    cross = lambda r, c: (r - 1 if r % 2 == 0 else r + 1, c)
    twin = lambda r, c: (r ^ 1, c)
    east = lambda r, c: (r, c + 1)
    west = lambda r, c: (r, c - 1)
    alpha, beta = alpha.reshape(1), beta.reshape(1)
    vmem = pl.BlockSpec(memory_space=pltpu.VMEM)
    smem = pl.BlockSpec(memory_space=pltpu.SMEM)

    first = pack(x, pat, [CROSS1, EAST1], [1, 1])
    c1 = moved(first[0], cross)
    e1 = moved(first[1], east)
    second = pack(x, pat, [TWIN, CROSS2, WEST, EAST2, CROSS3], [1, 0, 0, 0, 0])
    tw = moved(second[0], twin)
    c2 = moved(second[1], cross)
    we = moved(second[2], west)
    e2 = moved(second[3], east)
    c3 = moved(second[4], cross)

    shares = pl.pallas_call(
        trace_kernel,
        out_shape=jax.ShapeDtypeStruct((B, B), F32),
        in_specs=[vmem, smem, smem, smem, vmem, vmem, vmem],
        out_specs=vmem,
        compiler_params=PARAMS,
        cost_estimate=pl.CostEstimate(flops=300000000, bytes_accessed=4000000, transcendentals=0),
    )(x, pat, alpha, beta, c1, tw, e1)
    total = jnp.sum(lax.all_to_all(shares, AXES, 0, 0))
    trace = total / (rows * columns * x.shape[1])

    fe = moved(jnp.concatenate([c1[2 * B : 4 * B], c2[2 * B : 4 * B]]), east)
    fw = moved(jnp.concatenate([c1[: 2 * B], c2[: 2 * B]]), west)
    corner = [e2[2 * B : 3 * B], e1[2 * B : 3 * B], e2[B : 2 * B], e1[B : 2 * B], we[4 * B : 6 * B], we[2 * B : 4 * B]]
    tc = moved(jnp.concatenate(corner), twin)

    acc = pl.pallas_call(
        near_kernel,
        out_shape=jax.ShapeDtypeStruct((36, B, B), F32),
        in_specs=[vmem, smem, vmem],
        out_specs=vmem,
        scratch_shapes=[pltpu.VMEM((36, B, B), BF16)] * 2 + [pltpu.VMEM((24, B, B), BF16)] * 2,
        compiler_params=PARAMS,
        cost_estimate=pl.CostEstimate(flops=1500000000, bytes_accessed=8000000, transcendentals=0),
    )(x, pat, tw)

    updated = pl.pallas_call(
        final_entry,
        out_shape=jax.ShapeDtypeStruct(x.shape, F32),
        in_specs=[vmem, smem, smem, smem] + [vmem] * 10,
        out_specs=vmem,
        scratch_shapes=[pltpu.VMEM((36, B, B), F32)],
        compiler_params=PARAMS,
        cost_estimate=pl.CostEstimate(flops=1000000000, bytes_accessed=12000000, transcendentals=0),
    )(x, pat, alpha, beta, acc, c1, c2, c3, e1, e2, we, fe, fw, tc)
    return (updated, trace)


def final_entry(x, pat, alpha, beta, start, *rest):
    *messages, out, acc = rest
    acc[...] = start[...]
    final_kernel(x, pat, alpha, beta, acc, *messages, out)


def solution(mesh):
    placed = (P("row", "col", None, None, None), P("row", "col", None), P(), P())
    return jax.shard_map(
        body,
        mesh=mesh,
        in_specs=placed,
        out_specs=(P("row", "col", None, None, None), P()),
        check_vma=False,
    )
```

time: 205 us -> 56.2 us (0.27)
  matrix products: 68.6 us -> 0 us
  blocking collectives: 64.9 us -> 0 us
  waiting for transfers between devices: 42.2 us -> 3.34 us
  starting transfers between devices: 8.71 us -> 26 us
  Pallas kernels: 0 us -> 13.5 us
  other arithmetic: 7.04 us -> 2.2 us
    dot_general x49 -> x0, matrix products: 68.6 us -> none  [add_source(): jnp.einsum('uvpm,uvmq->uvpq', left, shifted[:, :, other], precision=lax.P...]
    psum x1 -> x0, blocking collectives: 64.9 us -> none  [body(): trace = lax.psum(local_trace, ('row', 'col')) / total_rows]
    ppermute x4 -> x10, waiting for transfers between devices: 42.2 us -> 1.62 us  [moved(): return lax.ppermute(message, AXES, pairs)]
    pallas_call x0 -> x5, Pallas kernels: none -> 13.5 us  [the longest x1 4.41 us: body(): pl.pallas_call(final_entry, out_shape=jax.ShapeDtypeStruct(x.shape, F32),...]
    ppermute x4 -> x10, starting transfers between devices: 8.71 us -> 20 us  [moved(): return lax.ppermute(message, AXES, pairs)]
    all_to_all x0 -> x1, starting transfers between devices: none -> 5.95 us  [body(): total = jnp.sum(lax.all_to_all(shares, AXES, 0, 0))]
    unnamed x3 -> x21, local copies, waits for them, and re-layouts: 1.56 us -> 6.31 us
    squeeze x2 -> x0, local copies, waits for them, and re-layouts: 4.68 us -> none  [body(): local_trace = jnp.sum(jnp.diagonal(updated[:, :, 4], axis1=2, axis2=3))]
  transfers between devices with their start and end apart: 4 -> 11, of which waited for: 4 -> 3; matrix products, arithmetic and copies ran while one was open for 14% -> 10% of each run, Pallas kernels for 0% -> 20%
where the time goes in v1:
time: 56.2 us; the launch traced here: 55.9 us
  starting transfers between devices  26 us (46%)
  Pallas kernels  13.5 us (24%)
  local copies, waits for them, and re-layouts  7.01 us (12%)
  between operations  3.86 us (7%)
  waiting for transfers between devices  3.34 us (6%)
  other arithmetic  2.2 us (4%)
    ppermute x10, starting transfers between devices, moved(): return lax.ppermute(message, AXES, pairs)  20 us
    unnamed x21, local copies, waits for them, and re-layouts  6.31 us
    all_to_all x1, starting transfers between devices, body(): total = jnp.sum(lax.all_to_all(shares, AXES, 0, 0))  5.95 us
    pallas_call x1, Pallas kernels, body(): pl.pallas_call(final_entry, out_shape=jax.ShapeDtypeStruct(x.shape, F32),...  4.41 us
    pallas_call x1, Pallas kernels, body(): pl.pallas_call(near_kernel, out_shape=jax.ShapeDtypeStruct((36, B, B), F3...  3.54 us
    pallas_call x1, Pallas kernels, body(): pl.pallas_call(trace_kernel, out_shape=jax.ShapeDtypeStruct((B, B), F32),...  2.85 us
    pallas_call x2, Pallas kernels, pack(): pl.pallas_call(functools.partial(pack_kernel, messages, present), out_sha...  2.71 us
    all_to_all x1, waiting for transfers between devices, body(): total = jnp.sum(lax.all_to_all(shares, AXES, 0, 0))  1.73 us
  transfers between devices with their start and end apart: 11, of which 3 were waited for; matrix products, arithmetic and copies ran while one was open for 10% of the time, Pallas kernels for 20%

profile of v1, /device:TPU:1, one launch (start us, length us, event | category | flops | bytes accessed | tf_op | source)
XLA Modules:
  0.0 55.9 jit_solution(8579369712455810398)
XLA Ops:
  0.6 0.0 copy-start
  0.6 1.7 %copy-done = f32[1,4,9,128,128]{4,3,2,1,0:T(8,128)S(1)} copy-done((f32[1,4,9,128,128]{4,3,2,1,0:T(8,128)S(1)}, f32[1,4,9,128,128]{4,3,2,1,0:T(8,128)}, u32[]{:S(2)}) %copy-start) | copy-done | bytes 2359320
  2.3 0.0 copy-start.6
  2.3 0.7 %copy-done.6 = s32[1,4,9]{2,1,0:T(4,128)S(1)} copy-done((s32[1,4,9]{2,1,0:T(4,128)S(1)}, s32[1,4,9]{2,1,0:T(4,128)}, u32[]{:S(2)}) %copy-start.6) | copy-done | bytes 168
  3.0 2.1 %shard_map.59 = (f32[3080,128]{1,0:T(8,128)}, f32[1024,128]{1,0:T(8,128)S(1)}, f32[768,128]{1,0:T(8,128)S(1)}, f32[384,128]{1,0:T(8,128)S(1)}, f32[1024,128]{1,0:T(8,128)}) custom-call(f32[1,4,9,128,128]{4,3,2,1,0:T(8,128)S(1)} %copy-done, s32[1,4,9]{2,1,0:T(4,128)S(1)} %copy-done.6), custom_call_target="tpu_custom_call" | custom-call | bytes 4000000 | tf_op jit(solution)/shard_map/pallas_call | solution.py:98
  5.1 0.0 copy-start.1
  5.1 0.0 copy-start.7
  5.1 2.0 %collective-permute-start.5 = (f32[384,128]{1,0:T(8,128)S(1)}, f32[384,128]{1,0:T(8,128)S(1)}, u32[]{:S(2)}, u32[]{:S(2)}) collective-permute-start(f32[384,128]{1,0:T(8,128)S(1)} %get-tuple-element.14), channel_id=1, source_target_pairs={{0,1},{1,2},{2,3},{3,4},{4,5},{5,6},{6,7},{7,8},{8,9},{9,10},{10,1... | collective-permute-start | bytes 589832 | tf_op jit(solution)/shard_map/ppermute | solution.py:237
  7.1 0.6 %shard_map.61 = (f32[1032,128]{1,0:T(8,128)S(1)}, f32[392,128]{1,0:T(8,128)S(1)}) custom-call(f32[1,4,9,128,128]{4,3,2,1,0:T(8,128)S(1)} %copy-done, s32[1,4,9]{2,1,0:T(4,128)S(1)} %copy-done.6), custom_call_target="tpu_custom_call" | custom-call | bytes 4000000 | tf_op jit(solution)/shard_map/pallas_call | solution.py:98
  7.7 1.3 %collective-permute-start.4 = (f32[392,128]{1,0:T(8,128)S(1)}, f32[392,128]{1,0:T(8,128)S(1)}, u32[]{:S(2)}, u32[]{:S(2)}) collective-permute-start(f32[392,128]{1,0:T(8,128)S(1)} %get-tuple-element.13), channel_id=1, source_target_pairs={{0,1},{1,2},{2,3},{3,4},{4,5},{5,6},{6,7},{7,8},{8,9},{9,10},{10,1... | collective-permute-start | bytes 602120 | tf_op jit(solution)/shard_map/ppermute | solution.py:237
  9.0 2.4 %collective-permute-start.1 = (f32[1032,128]{1,0:T(8,128)S(1)}, f32[1032,128]{1,0:T(8,128)S(1)}, u32[]{:S(2)}, u32[]{:S(2)}) collective-permute-start(f32[1032,128]{1,0:T(8,128)S(1)} %get-tuple-element.10), channel_id=1, source_target_pairs={{0,112},{1,113},{2,114},{3,115},{4,116},{5,117},{6,118},{7,119},{8... | collective-permute-start | bytes 1585160 | tf_op jit(solution)/shard_map/ppermute | solution.py:237
  11.4 3.6 %collective-permute-start.6 = (f32[768,128]{1,0:T(8,128)S(1)}, f32[768,128]{1,0:T(8,128)S(1)}, u32[]{:S(2)}, u32[]{:S(2)}) collective-permute-start(f32[768,128]{1,0:T(8,128)S(1)} %get-tuple-element.15), channel_id=1, source_target_pairs={{0,15},{1,0},{2,1},{3,2},{4,3},{5,4},{6,5},{7,6},{8,7},{9,8},{10,9... | collective-permute-start | bytes 1179656 | tf_op jit(solution)/shard_map/ppermute | solution.py:237
  15.0 0.3 collective-permute-start.2
  15.3 1.2 %collective-permute-done.5.rest_4_ = f32[384,128]{1,0:T(8,128)S(1)} collective-permute-done((f32[384,128]{1,0:T(8,128)S(1)}, f32[384,128]{1,0:T(8,128)S(1)}, u32[]{:S(2)}, u32[]{:S(2)}) %collective-permute-start.5) | collective-permute-done | bytes 196640 | tf_op jit(solution)/shard_map/ppermute | solution.py:237
  16.5 0.0 copy-start.4
  16.5 3.2 %collective-permute-start.3 = (f32[1024,128]{1,0:T(8,128)}, f32[1024,128]{1,0:T(8,128)}, u32[]{:S(2)}, u32[]{:S(2)}) collective-permute-start(f32[1024,128]{1,0:T(8,128)} %get-tuple-element.12), channel_id=1, source_target_pairs={{0,112},{1,113},{2,114},{3,115},{4,116},{5,117},{6,118},{7,119},{8... | collective-permute-start | bytes 1572872 | tf_op jit(solution)/shard_map/ppermute | solution.py:237
  19.7 0.6 %slice_dynamic-update-slice_fusion.5 = f32[1024,128]{1,0:T(8,128)} fusion(f32[384,128]{1,0:T(8,128)S(1)} %collective-permute-done.5.rest_4_), kind=kLoop, calls=%fused_computation.7 | loop fusion | bytes 131072
  20.4 0.4 collective-permute-done.4.rest_3_.e1
  20.8 1.2 %collective-permute-start = (f32[3080,128]{1,0:T(8,128)}, f32[3080,128]{1,0:T(8,128)}, u32[]{:S(2)}, u32[]{:S(2)}) collective-permute-start(f32[3080,128]{1,0:T(8,128)} %get-tuple-element.9), channel_id=1, source_target_pairs={{0,16},{1,17},{2,18},{3,19},{4,20},{5,21},{6,22},{7,23},{8,24},{9,... | collective-permute-start | bytes 4730888 | tf_op jit(solution)/shard_map/ppermute | solution.py:237
  22.0 0.6 %slice_dynamic-update-slice_fusion.4 = f32[1024,128]{1,0:T(8,128)} fusion(f32[1024,128]{1,0:T(8,128)} %slice_dynamic-update-slice_fusion.5, f32[392,128]{1,0:T(8,128)S(1)} %collective-permute-done.4.rest_3_.e1), kind=kLoop, calls=%fused_computation.6 | loop fusion | bytes 131072
  22.6 0.6 %slice_dynamic-update-slice_fusion.3 = f32[1024,128]{1,0:T(8,128)} fusion(f32[1024,128]{1,0:T(8,128)} %slice_dynamic-update-slice_fusion.4, f32[384,128]{1,0:T(8,128)S(1)} %collective-permute-done.5.rest_4_), kind=kLoop, calls=%fused_computation.5 | loop fusion | bytes 131072
  23.3 0.6 %slice_dynamic-update-slice_fusion.2 = f32[1024,128]{1,0:T(8,128)} fusion(f32[1024,128]{1,0:T(8,128)} %slice_dynamic-update-slice_fusion.3, f32[392,128]{1,0:T(8,128)S(1)} %collective-permute-done.4.rest_3_.e1), kind=kLoop, calls=%fused_computation.4 | loop fusion | bytes 131072
  23.9 0.0 collective-permute-done.6.rest_5_
  23.9 0.7 %slice_dynamic-update-slice_fusion.1 = f32[1024,128]{1,0:T(8,128)} fusion(f32[1024,128]{1,0:T(8,128)} %slice_dynamic-update-slice_fusion.2, f32[768,128]{1,0:T(8,128)S(1)} %collective-permute-done.6.rest_5_), kind=kLoop, calls=%fused_computation.3 | loop fusion | bytes 262144
  24.6 0.7 %slice_dynamic-update-slice_fusion = f32[1024,128]{1,0:T(8,128)} fusion(f32[1024,128]{1,0:T(8,128)} %slice_dynamic-update-slice_fusion.1, f32[768,128]{1,0:T(8,128)S(1)} %collective-permute-done.6.rest_5_), kind=kLoop, calls=%fused_computation.2 | loop fusion | bytes 262144 | tf_op jit(solution)/shard_map/concatenate | solution.py:271
  25.2 0.4 collective-permute-start.9
  25.7 0.0 collective-permute-done.2.rest_1_
  25.7 0.0 copy-start.2
  25.7 0.0 collective-permute-done.1.rest_0_.c1
  25.7 0.8 %copy-done.2 = f32[1024,128]{1,0:T(8,128)} copy-done((f32[1024,128]{1,0:T(8,128)}, f32[1024,128]{1,0:T(8,128)S(1)}, u32[]{:S(2)}) %copy-start.2) | copy-done | bytes 524312
  26.5 0.0 copy-done.4
  26.5 0.7 %pad_maximum_fusion = f32[512,128]{1,0:T(8,128)} fusion(f32[256,128]{1,0:T(8,128)S(1)} %get-tuple-element.19, f32[256,128]{1,0:T(8,128)S(1)} %get-tuple-element.17), kind=kLoop, calls=%fused_computation | loop fusion | flops 65536 | bytes 524288 | tf_op jit(solution)/shard_map/concatenate | solution.py:268
  27.2 0.0 collective-permute-start.7
  27.2 0.7 %pad_maximum_fusion.1 = f32[512,128]{1,0:T(8,128)} fusion(f32[256,128]{1,0:T(8,128)S(1)} %get-tuple-element.18, f32[256,128]{1,0:T(8,128)S(1)} %get-tuple-element.16), kind=kLoop, calls=%fused_computation.1 | loop fusion | flops 65536 | bytes 524288 | tf_op jit(solution)/shard_map/concatenate | solution.py:269
  28.0 5.5 %collective-permute-start.8 = (f32[512,128]{1,0:T(8,128)}, f32[512,128]{1,0:T(8,128)}, u32[]{:S(2)}, u32[]{:S(2)}) collective-permute-start(f32[512,128]{1,0:T(8,128)} %pad_maximum_fusion.1), channel_id=1, source_target_pairs={{0,15},{1,0},{2,1},{3,2},{4,3},{5,4},{6,5},{7,6},{8,7},{9,8},{10,9... | collective-permute-start | bytes 786440 | tf_op jit(solution)/shard_map/ppermute | solution.py:237
  34.8 0.0 collective-permute-done.tw
  34.8 0.0 copy-done.1
  34.8 0.0 copy-done.7
  34.8 2.9 %shard_map.63 = f32[128,128]{1,0:T(8,128)} custom-call(f32[1,4,9,128,128]{4,3,2,1,0:T(8,128)S(1)} %copy-done.1, s32[1,4,9]{2,1,0:T(4,128)S(1)} %copy-done.7, f32[1]{0:T(128)} %bitcast.6.alpha, f32[1]{0:T(128)} %bitcast.8.beta, f32[1032,128]{1,0:T(8,128)S(1)} %collective-permute-done.1.rest_0_.c1, f32[3080,128]{1,0:T(8,128)} %collective-permute-done.tw, ...), custom_call_target="tpu_custom_call" | custom-call | flops 300000000 | bytes 4000000 | tf_op jit(solution)/shard_map/pallas_call | solution.py:257
  37.7 5.9 %all-to-all-start = ((f32[128,1,128]{2,1,0:T(1,128)}), f32[128,1,128]{2,1,0:T(1,128)S(1)}, u32[]{:S(2)}, u32[]{:S(2)}) async-start(f32[128,1,128]{2,1,0:T(1,128)} %bitcast.3), calls=%async_computation | async-start | bytes 131072 | tf_op jit(solution)/shard_map/all_to_all | solution.py:265
  43.6 0.0 copy-start.3
  43.6 0.0 copy-start.5
  43.6 3.5 %shard_map.60.start = f32[36,128,128]{2,1,0:T(8,128)S(1)} custom-call(f32[1,4,9,128,128]{4,3,2,1,0:T(8,128)S(1)} %copy-done.1, s32[1,4,9]{2,1,0:T(4,128)S(1)} %copy-done.7, f32[3080,128]{1,0:T(8,128)} %collective-permute-done.tw), custom_call_target="tpu_custom_call" | custom-call | flops 1500000000 | bytes 8000000 | tf_op jit(solution)/shard_map/pallas_call | solution.py:273
  47.2 0.0 collective-permute-done.3.rest_2_
  47.2 0.0 collective-permute-done.7.rest_6_
  47.2 0.0 collective-permute-done.8.rest_7_
  47.2 0.0 collective-permute-done.9.rest_8_
  47.2 0.0 copy-done.3
  47.2 0.0 copy-done.5
  47.2 4.4 %shard_map.62 = f32[1,4,9,128,128]{4,3,2,1,0:T(8,128)} custom-call(f32[1,4,9,128,128]{4,3,2,1,0:T(8,128)S(1)} %copy-done.1, s32[1,4,9]{2,1,0:T(4,128)S(1)} %copy-done.7, f32[1]{0:T(128)} %bitcast.5.alpha, f32[1]{0:T(128)} %bitcast.7.beta, f32[36,128,128]{2,1,0:T(8,128)S(1)} %shard_map.60.start, f32[1032,128]{1,0:T(8,128)S(1)} %collective-permute-done.1.rest_0_.c1, ...), custom_call_target="tpu_custom_call" | custom-call | flops 1000000000 | bytes 12000000 | tf_op jit(solution)/shard_map/pallas_call | solution.py:283
  51.7 1.7 %all-to-all-done = f32[128,1,128]{2,1,0:T(1,128)S(1)} async-done(((f32[128,1,128]{2,1,0:T(1,128)}), f32[128,1,128]{2,1,0:T(1,128)S(1)}, u32[]{:S(2)}, u32[]{:S(2)}) %all-to-all-start) | async-done | bytes 65568 | tf_op jit(solution)/shard_map/all_to_all | solution.py:265
  53.4 0.7 %reduce_sum.9 = f32[]{:T(128)} reduce(f32[128,1,128]{2,1,0:T(1,128)S(1)} %all-to-all-done, f32[]{:T(128)} %constant.1.clone.1), dimensions={0,1,2}, to_apply=%region_0.0 | reduce | flops 16383 | bytes 65544 | tf_op jit(solution)/shard_map/reduce_sum | solution.py:265
  (2 shorter events, 0.0 us)
Async XLA Ops:
  0.6 1.7 %copy-start = (f32[1,4,9,128,128]{4,3,2,1,0:T(8,128)S(1)}, f32[1,4,9,128,128]{4,3,2,1,0:T(8,128)}, u32[]{:S(2)}) copy-start(f32[1,4,9,128,128]{4,3,2,1,0:T(8,128)} %x.9) | copy-start | bytes 7077892
  2.3 0.7 %copy-start.6 = (s32[1,4,9]{2,1,0:T(4,128)S(1)}, s32[1,4,9]{2,1,0:T(4,128)}, u32[]{:S(2)}) copy-start(s32[1,4,9]{2,1,0:T(4,128)} %pat.9) | copy-start | bytes 436
  5.1 29.7 %copy-start.1 = (f32[1,4,9,128,128]{4,3,2,1,0:T(8,128)S(1)}, f32[1,4,9,128,128]{4,3,2,1,0:T(8,128)}, u32[]{:S(2)}) copy-start(f32[1,4,9,128,128]{4,3,2,1,0:T(8,128)} %x.9) | copy-start | bytes 7077892
  5.1 29.7 %copy-start.7 = (s32[1,4,9]{2,1,0:T(4,128)S(1)}, s32[1,4,9]{2,1,0:T(4,128)}, u32[]{:S(2)}) copy-start(s32[1,4,9]{2,1,0:T(4,128)} %pat.9) | copy-start | bytes 436
  5.1 11.4 %collective-permute-start.5 = (f32[384,128]{1,0:T(8,128)S(1)}, f32[384,128]{1,0:T(8,128)S(1)}, u32[]{:S(2)}, u32[]{:S(2)}) collective-permute-start(f32[384,128]{1,0:T(8,128)S(1)} %get-tuple-element.14), channel_id=1, source_target_pairs={{0,1},{1,2},{2,3},{3,4},{4,5},{5,6},{6,7},{7,8},{8,9},{9,10},{10,1... | collective-permute-start | bytes 589832 | tf_op jit(solution)/shard_map/ppermute | solution.py:237
  7.7 13.0 %collective-permute-start.4 = (f32[392,128]{1,0:T(8,128)S(1)}, f32[392,128]{1,0:T(8,128)S(1)}, u32[]{:S(2)}, u32[]{:S(2)}) collective-permute-start(f32[392,128]{1,0:T(8,128)S(1)} %get-tuple-element.13), channel_id=1, source_target_pairs={{0,1},{1,2},{2,3},{3,4},{4,5},{5,6},{6,7},{7,8},{8,9},{9,10},{10,1... | collective-permute-start | bytes 602120 | tf_op jit(solution)/shard_map/ppermute | solution.py:237
  9.0 16.7 %collective-permute-start.1 = (f32[1032,128]{1,0:T(8,128)S(1)}, f32[1032,128]{1,0:T(8,128)S(1)}, u32[]{:S(2)}, u32[]{:S(2)}) collective-permute-start(f32[1032,128]{1,0:T(8,128)S(1)} %get-tuple-element.10), channel_id=1, source_target_pairs={{0,112},{1,113},{2,114},{3,115},{4,116},{5,117},{6,118},{7,119},{8... | collective-permute-start | bytes 1585160 | tf_op jit(solution)/shard_map/ppermute | solution.py:237
  11.4 12.5 %collective-permute-start.6 = (f32[768,128]{1,0:T(8,128)S(1)}, f32[768,128]{1,0:T(8,128)S(1)}, u32[]{:S(2)}, u32[]{:S(2)}) collective-permute-start(f32[768,128]{1,0:T(8,128)S(1)} %get-tuple-element.15), channel_id=1, source_target_pairs={{0,15},{1,0},{2,1},{3,2},{4,3},{5,4},{6,5},{7,6},{8,7},{9,8},{10,9... | collective-permute-start | bytes 1179656 | tf_op jit(solution)/shard_map/ppermute | solution.py:237
  15.0 10.7 %collective-permute-start.2 = (f32[1024,128]{1,0:T(8,128)S(1)}, f32[1024,128]{1,0:T(8,128)S(1)}, u32[]{:S(2)}, u32[]{:S(2)}) collective-permute-start(f32[1024,128]{1,0:T(8,128)S(1)} %get-tuple-element.11), channel_id=1, source_target_pairs={{0,112},{1,113},{2,114},{3,115},{4,116},{5,117},{6,118},{7,119},{8... | collective-permute-start | bytes 1572872 | tf_op jit(solution)/shard_map/ppermute | solution.py:237
  16.5 10.0 %copy-start.4 = (f32[384,128]{1,0:T(8,128)}, f32[384,128]{1,0:T(8,128)S(1)}, u32[]{:S(2)}) copy-start(f32[384,128]{1,0:T(8,128)S(1)} %collective-permute-done.5.rest_4_) | copy-start | bytes 589828
  16.5 30.7 %collective-permute-start.3 = (f32[1024,128]{1,0:T(8,128)}, f32[1024,128]{1,0:T(8,128)}, u32[]{:S(2)}, u32[]{:S(2)}) collective-permute-start(f32[1024,128]{1,0:T(8,128)} %get-tuple-element.12), channel_id=1, source_target_pairs={{0,112},{1,113},{2,114},{3,115},{4,116},{5,117},{6,118},{7,119},{8... | collective-permute-start | bytes 1572872 | tf_op jit(solution)/shard_map/ppermute | solution.py:237
  20.8 14.0 %collective-permute-start = (f32[3080,128]{1,0:T(8,128)}, f32[3080,128]{1,0:T(8,128)}, u32[]{:S(2)}, u32[]{:S(2)}) collective-permute-start(f32[3080,128]{1,0:T(8,128)} %get-tuple-element.9), channel_id=1, source_target_pairs={{0,16},{1,17},{2,18},{3,19},{4,20},{5,21},{6,22},{7,23},{8,24},{9,... | collective-permute-start | bytes 4730888 | tf_op jit(solution)/shard_map/ppermute | solution.py:237
  25.2 22.0 %collective-permute-start.9 = (f32[1024,128]{1,0:T(8,128)}, f32[1024,128]{1,0:T(8,128)}, u32[]{:S(2)}, u32[]{:S(2)}) collective-permute-start(f32[1024,128]{1,0:T(8,128)} %slice_dynamic-update-slice_fusion), channel_id=1, source_target_pairs={{0,16},{1,17},{2,18},{3,19},{4,20},{5,21},{6,22},{7,23},{8,24},{9,... | collective-permute-start | bytes 1572872 | tf_op jit(solution)/shard_map/ppermute | solution.py:237
  25.7 0.8 %copy-start.2 = (f32[1024,128]{1,0:T(8,128)}, f32[1024,128]{1,0:T(8,128)S(1)}, u32[]{:S(2)}) copy-start(f32[1024,128]{1,0:T(8,128)S(1)} %collective-permute-done.2.rest_1_) | copy-start | bytes 1572868
  27.2 20.0 %collective-permute-start.7 = (f32[512,128]{1,0:T(8,128)}, f32[512,128]{1,0:T(8,128)}, u32[]{:S(2)}, u32[]{:S(2)}) collective-permute-start(f32[512,128]{1,0:T(8,128)} %pad_maximum_fusion), channel_id=1, source_target_pairs={{0,1},{1,2},{2,3},{3,4},{4,5},{5,6},{6,7},{7,8},{8,9},{9,10},{10,1... | collective-permute-start | bytes 786440 | tf_op jit(solution)/shard_map/ppermute | solution.py:237
  28.0 19.3 %collective-permute-start.8 = (f32[512,128]{1,0:T(8,128)}, f32[512,128]{1,0:T(8,128)}, u32[]{:S(2)}, u32[]{:S(2)}) collective-permute-start(f32[512,128]{1,0:T(8,128)} %pad_maximum_fusion.1), channel_id=1, source_target_pairs={{0,15},{1,0},{2,1},{3,2},{4,3},{5,4},{6,5},{7,6},{8,7},{9,8},{10,9... | collective-permute-start | bytes 786440 | tf_op jit(solution)/shard_map/ppermute | solution.py:237
  37.7 15.7 %all-to-all-start = ((f32[128,1,128]{2,1,0:T(1,128)}), f32[128,1,128]{2,1,0:T(1,128)S(1)}, u32[]{:S(2)}, u32[]{:S(2)}) async-start(f32[128,1,128]{2,1,0:T(1,128)} %bitcast.3), calls=%async_computation | async-start | bytes 131072 | tf_op jit(solution)/shard_map/all_to_all | solution.py:265
  43.6 3.6 %copy-start.3 = (f32[1024,128]{1,0:T(8,128)S(1)}, f32[1024,128]{1,0:T(8,128)}, u32[]{:S(2)}) copy-start(f32[1024,128]{1,0:T(8,128)} %copy-done.2) | copy-start | bytes 1572868
  43.6 3.6 %copy-start.5 = (f32[384,128]{1,0:T(8,128)S(1)}, f32[384,128]{1,0:T(8,128)}, u32[]{:S(2)}) copy-start(f32[384,128]{1,0:T(8,128)} %copy-done.4) | copy-start | bytes 589828

commit v2 on v0

v2 whole, which is shorter than its diff:
```python
import functools

import jax
import jax.numpy as jnp
from jax import lax
from jax.experimental import pallas as pl
from jax.experimental.pallas import tpu as pltpu
from jax.sharding import PartitionSpec as P

CR, TW, MID = KINDS = (0, 1, 2)
AXES = ("row", "col")
B = 128
F32 = jnp.float32
BF16 = jnp.bfloat16
ANY = pl.BlockSpec(memory_space=pl.ANY)
VMEM = pl.BlockSpec(memory_space=pltpu.VMEM)
FAR = None
SMEM = pl.BlockSpec(memory_space=pltpu.SMEM)


def at(kind, v, j):
    return kind * 12 + v * 3 + j + 1


FIRST = [0, 1, 2, 4, 5, 7, 8, 10, 11]
SECOND = [3, 6, 9]
HEAD = 8


def slot(kind, dv, odd):
    base = {CR: 6 * odd, MID: 3, TW: 6 - 6 * odd}[kind]
    return base + dv + 1


def weight(pat, v, s):
    return pat[0, v, s].astype(F32)


def split(block):
    high = block.astype(BF16)
    return high, (block - high.astype(F32)).astype(BF16)


def dot3(left, right):
    def side(blocks, part):
        return jnp.concatenate([jnp.concatenate([b[part] for b in line], axis=1) for line in blocks], axis=0)

    lh, ll, rh, rl = side(left, 0), side(left, 1), side(right, 0), side(right, 1)
    return jnp.dot(
        jnp.concatenate([lh, lh, ll], axis=1), jnp.concatenate([rh, rl, rh], axis=0), preferred_element_type=F32
    )


def get(ref, i, head=0):
    return ref[pl.ds(head + i * B, B), :]


def put(ref, i, block, head=0):
    ref[pl.ds(head + i * B, B), :] = block


class Copies:
    def __init__(self, sems):
        self.sems, self.count = sems, 0

    def start(self, source, target):
        copy = pltpu.make_async_copy(source, target, self.sems.at[self.count])
        self.count += 1
        copy.start()
        return copy


def pack_kernel(x, pat, c1, ea, tw, c2, we, rest, stage, table, sems):
    odd = lax.rem(lax.axis_index("row"), 2)
    dma = Copies(sems)
    order = (0, 3, 1, 2)
    table_load = dma.start(pat, table)
    loads = {v: dma.start(x.at[0, v], stage.at[v]) for v in order}
    table_load.wait()
    rows = lax.broadcasted_iota(jnp.int32, (HEAD, B), 0)
    present = jnp.zeros((HEAD, B), F32)
    for v in range(4):
        present = jnp.where(rows == v, weight(table, v, 4), present)
    for ref in (c1, ea, tw):
        ref[pl.ds(0, HEAD), :] = present

    for v in order:
        loads[v].wait()
        for kind in KINDS:
            for j in (-1, 0, 1):
                s = slot(kind, j, odd)
                block = stage[v, s] * weight(table, v, s)
                i = at(kind, v, j)
                if kind != CR:
                    put(tw, i - 12, block, HEAD)
                elif i in FIRST:
                    put(c1, FIRST.index(i), block, HEAD)
                else:
                    put(c2, SECOND.index(i), block)
                    put(rest, SECOND.index(i), block)
                if kind == MID:
                    put(c2, 3 + i - 24, block)
                if v == 3 and j >= 0:
                    put(ea, 2 * kind + j, block, HEAD)
                if v == 0 and j < 1:
                    put(we, 2 * kind + j + 1, block)


def near_kernel(alpha, beta, c1m, rest, twm, tw, acc, lefts, pairs, few, lh, ll, sh, sl, rh, rl):
    def own(kind, v, j):
        i = at(kind, v, j)
        if kind != CR:
            return get(twm, i - 12, HEAD)
        return get(c1m, FIRST.index(i), HEAD) if i in FIRST else get(rest, SECOND.index(i))

    sources = {at(CR, v, a): at(CR, v, a) for v in range(4) for a in (-1, 0, 1)}
    sources.update({at(TW, 0, -1): 12, at(TW, 3, 1): 13, at(MID, 0, -1): 14, at(MID, 3, 1): 15})

    def prepare(v):
        for kind in KINDS:
            for j in (-1, 0, 1):
                i = at(kind, v, j)
                block = own(kind, v, j)
                acc[v * 9 + kind * 3 + j + 1] = alpha[...] * block
                rh[i], rl[i] = split(block)
                high, low = split(beta[...] * block)
                if kind != CR:
                    lh[i - 12], ll[i - 12] = high, low
                if i in sources:
                    lefts[sources[i]], lefts[16 + sources[i]] = high, low
        for j in (-1, 0, 1):
            for kind in (TW, MID):
                i = at(kind, v, j) - 12
                sh[i], sl[i] = split(get(tw, i, HEAD))

    left = lambda kind, v, j: (lh[at(kind, v, j) - 12], ll[at(kind, v, j) - 12])
    mine = lambda kind, v, j: (rh[at(kind, v, j)], rl[at(kind, v, j)])
    theirs = lambda kind, v, j: (sh[at(kind, v, j) - 12], sl[at(kind, v, j) - 12])

    def add(kind, v, sv, block):
        acc[v * 9 + kind * 3 + sv + 1] += block

    for w in range(4):
        prepare(w)
    for w in range(4):
        for t in (0, -1, 1):
            targets = [(w - a, a) for a in (-1, 0, 1) if 0 <= w - a < 4 and -1 <= a + t <= 1]
            lines = [[left(MID, v, a), left(TW, v, a)] for v, a in targets]
            right = [[mine(MID, w, t), mine(TW, w, t)], [theirs(TW, w, t), theirs(MID, w, t)]]
            both = dot3(lines, right)
            only = dot3([line[:1] for line in lines], [[mine(CR, w, t)]])
            for n, (v, a) in enumerate(targets):
                rows = slice(n * B, (n + 1) * B)
                add(MID, v, a + t, both[rows, :B])
                add(TW, v, a + t, both[rows, B:])
                add(CR, v, a + t, only[rows])
    present = lambda v: twm[pl.ds(v, 1), :]
    other = lambda v: tw[pl.ds(v, 1), :]
    listed = []
    for v in range(4):
        listed.append((own(MID, v, 0), mine(MID, v, 0)))
        listed.append((own(TW, v, 0) * present(v), theirs(TW, v, 0)))
    for v in range(3):
        listed.append((own(MID, v, 1) * (present(v) + present(v + 1)), mine(MID, v + 1, -1)))
        listed.append((own(TW, v + 1, -1) * (present(v + 1) + other(v)), theirs(TW, v, 1)))
    value = beta[...] * dot3([[split(a) for a, _ in listed]], [[b] for _, b in listed])
    for v in range(4):
        value += alpha[...] * own(MID, v, 0)
    pairs[...] = value
    few[pl.ds(0, HEAD), :] = twm[pl.ds(0, HEAD), :]
    few[pl.ds(HEAD, HEAD), :] = tw[pl.ds(0, HEAD), :]
    kept = [own(CR, v, 0) for v in range(4)] + [own(CR, v, -1) for v in (1, 2, 3)] + [own(MID, 0, -1), get(tw, 0, HEAD)]
    for i, block in enumerate(kept):
        put(few, i, block, 2 * HEAD)


def trace_kernel(beta, pairs, few, c1, ea, out):
    own = lambda v: few[pl.ds(v, 1), :]
    far = lambda v: c1[pl.ds(v, 1), :]
    west = ea[pl.ds(3, 1), :]
    kept = lambda i: get(few, i, 2 * HEAD)
    listed = []
    for v in range(4):
        listed.append((own(v), kept(v), get(c1, 2 * v + 1, HEAD)))
    for v in range(3):
        listed.append((own(v + 1) + far(v), kept(4 + v), get(c1, 2 * v + 2, HEAD)))
    listed.append((west + own(0), get(ea, 2 * MID + 1, HEAD), kept(7)))
    listed.append((west + far(0), get(ea, 2 * CR + 1, HEAD), get(c1, 0, HEAD)))
    listed.append((west + few[pl.ds(HEAD, 1), :], get(ea, 2 * TW + 1, HEAD), kept(8)))
    value = pairs[...] + beta[...] * dot3([[split(a * w) for w, a, _ in listed]], [[split(b)] for _, _, b in listed])
    rows = lax.broadcasted_iota(jnp.int32, (B, B), 0)
    columns = lax.broadcasted_iota(jnp.int32, (B, B), 1)
    line = jnp.sum(jnp.where(rows == columns, value, 0.0), axis=0, keepdims=True)
    out[...] = jnp.broadcast_to(line, (B, B))


def sum_kernel(scale, shares, after, out):
    out[0, 0] = jnp.sum(shares[...]) * scale


def corner_kernel(ea, we, after, cc, tc):
    for out, toward in ((cc, CR), (tc, TW)):
        for i, k in enumerate((toward, MID)):
            for n in (0, 1):
                put(out, 2 * i + n, get(ea, 2 * k + n, HEAD))
                put(out, 4 + 2 * i + n, get(we, 2 * k + n))


def final_kernel(pat, lefts, acc, c1, c2, ea, we, cc, tc, out, total, stage, sems):
    odd = lax.rem(lax.axis_index("row"), 2)
    dma = Copies(sems)
    left = lambda i: (lefts[i], lefts[16 + i])
    seen = set()

    def add(kind, v, sv, block):
        i = v * 9 + kind * 3 + sv + 1
        total[i] = (total[i] if i in seen else acc[i]) + block
        seen.add(i)

    def spread(source, rights, places):
        result = dot3([[left(source)]], [[split(block) for block in rights]])
        for n, (kind, v, sv) in enumerate(places):
            add(kind, v, sv, result[:, n * B : (n + 1) * B])

    spread(14, [get(ea, i, HEAD) for i in range(6)], [(k, 0, s) for k in KINDS for s in (-1, 0)])
    spread(15, [get(we, i) for i in range(6)], [(k, 3, s) for k in KINDS for s in (0, 1)])
    spread(12, [get(tc, i) for i in range(4)], [(MID, 0, -1), (MID, 0, 0), (TW, 0, -1), (TW, 0, 0)])
    spread(13, [get(tc, 4 + i) for i in range(4)], [(MID, 3, 0), (MID, 3, 1), (TW, 3, 0), (TW, 3, 1)])
    spread(at(CR, 0, -1), [get(cc, i) for i in range(4)], [(MID, 0, -1), (MID, 0, 0), (CR, 0, -1), (CR, 0, 0)])
    spread(at(CR, 3, 1), [get(cc, 4 + i) for i in range(4)], [(MID, 3, 0), (MID, 3, 1), (CR, 3, 0), (CR, 3, 1)])

    def far(w, t):
        i = at(CR, w, t)
        return get(c1, FIRST.index(i), HEAD) if i in FIRST else get(c2, SECOND.index(i))

    stores = []

    def finish(v):
        for kind in KINDS:
            for sv in (-1, 0, 1):
                i, s = v * 9 + kind * 3 + sv + 1, slot(kind, sv, odd)
                stage[v, s] = weight(pat, v, s) * (total[i] if i in seen else acc[i])
        stores.append(dma.start(stage.at[v], out.at[0, v]))

    for w in range(4):
        for t in (0, -1, 1):
            targets = [(w - a, a) for a in (-1, 0, 1) if 0 <= w - a < 4 and -1 <= a + t <= 1]
            lines = [[left(at(CR, v, a))] for v, a in targets]
            result = dot3(lines, [[split(far(w, t)), split(get(c2, 3 + w * 3 + t + 1))]])
            for n, (v, a) in enumerate(targets):
                rows = slice(n * B, (n + 1) * B)
                add(MID, v, a + t, result[rows, :B])
                add(CR, v, a + t, result[rows, B:])
        if w >= 1:
            finish(w - 1)
    finish(3)
    for copy in stores:
        copy.wait()


def body(x, pat, alpha, beta):
    rows, columns = lax.axis_size("row"), lax.axis_size("col")

    def moved(message, step):
        pairs = []
        for r in range(rows):
            for c in range(columns):
                r2, c2 = step(r, c)
                pairs.append((r * columns + c, (r2 % rows) * columns + c2 % columns))
        return lax.ppermute(message, AXES, pairs)

    def call(kernel, outs, args, specs, size, scratch=()):
        spaces = [pltpu.HBM if s is ANY or a is pat else None for a, s in zip(args, specs)]
        return pl.pallas_call(
            kernel,
            out_shape=[pltpu.HBM(o.shape, o.dtype) if s is ANY or s is FAR else o for o, s in outs],
            in_specs=specs,
            out_specs=[VMEM if s is FAR else s for _, s in outs],
            scratch_shapes=scratch,
            compiler_params=pltpu.CompilerParams(vmem_limit_bytes=size * 1024 * 1024),
            cost_estimate=pl.CostEstimate(flops=1000, bytes_accessed=1000, transcendentals=0),
        )(*[pltpu.with_memory_space_constraint(a, m) if m else a for a, m in zip(args, spaces)])

    shape = lambda *dims, dtype=F32: jax.ShapeDtypeStruct(dims, dtype)
    lines = lambda count, head=0: shape(count * B + head, B)
    sems = lambda count: pltpu.SemaphoreType.DMA((count,))
    far = lambda a: pltpu.with_memory_space_constraint(a, pltpu.HBM)
    vmem = lambda *dims, dtype=F32: pltpu.VMEM(dims, dtype)
    crossing = lambda r: r - 1 if r % 2 == 0 else r + 1
    cross = lambda r, c: (crossing(r), c)
    twin = lambda r, c: (r ^ 1, c)
    east = lambda r, c: (r, c + 1)
    west = lambda r, c: (r, c - 1)
    alpha, beta = alpha.reshape(1, 1), beta.reshape(1, 1)

    *messages, rest = call(
        pack_kernel,
        [(lines(9, HEAD), VMEM), (lines(6, HEAD), VMEM), (lines(24, HEAD), VMEM), (lines(15), VMEM), (lines(6), VMEM), (lines(3), VMEM)],
        (x, pat),
        [ANY, ANY],
        10,
        [vmem(4, 9, B, B), pltpu.SMEM(pat.shape, jnp.int32), sems(5)],
    )
    c1, ea, tw, c2, we = [moved(m, s) for m, s in zip(messages, [cross, east, twin, cross, west])]
    c1m, _, twm = messages[:3]
    acc, lefts, pairs, few = call(
        near_kernel,
        [(shape(36, B, B), FAR), (shape(32, B, B, dtype=BF16), FAR), (shape(B, B), VMEM), (lines(9, 2 * HEAD), VMEM)],
        (alpha, beta, c1m, rest, twm, tw),
        [VMEM] * 6,
        14,
        [vmem(n, B, B, dtype=BF16) for n in (24, 24, 24, 24, 36, 36)],
    )
    (shares,) = call(
        trace_kernel,
        [(shape(B, B), VMEM)],
        (beta, pairs, few, c1, ea),
        [VMEM] * 5,
        4,
    )
    gathered = lax.all_to_all(shares, AXES, 0, 0)
    corners = call(corner_kernel, [(lines(8), VMEM)] * 2, (ea, we, pairs), [VMEM] * 3, 4)
    cc, tc = moved(corners[0], cross), moved(corners[1], twin)
    (updated,) = call(
        final_kernel,
        [(shape(*x.shape), ANY)],
        (pat, far(lefts), far(acc), c1, c2, ea, we, cc, tc),
        [SMEM] + [VMEM] * 8,
        14,
        [vmem(36, B, B), vmem(4, 9, B, B), sems(4)],
    )
    scale = 1.0 / (rows * columns * x.shape[1])
    (trace,) = call(functools.partial(sum_kernel, scale), [(shape(1, 1), SMEM)], (gathered, updated), [VMEM, ANY], 2)
    return (updated, trace.reshape(()))


def solution(mesh):
    placed = (P("row", "col", None, None, None), P("row", "col", None), P(), P())
    return jax.shard_map(
        body,
        mesh=mesh,
        in_specs=placed,
        out_specs=(P("row", "col", None, None, None), P()),
        check_vma=False,
    )
```

time: 205 us -> 48.7 us (0.24)
  matrix products: 68.6 us -> 0 us
  blocking collectives: 64.9 us -> 0 us
  waiting for transfers between devices: 42.2 us -> 4.94 us
  Pallas kernels: 0 us -> 15.8 us
  starting transfers between devices: 8.71 us -> 24.1 us
  other arithmetic: 7.04 us -> 0 us
  local copies, waits for them, and re-layouts: 8.09 us -> 1.59 us
  between operations: 4.13 us -> 2.01 us
    dot_general x49 -> x0, matrix products: 68.6 us -> none  [add_source(): jnp.einsum('uvpm,uvmq->uvpq', left, shifted[:, :, other], precision=lax.P...]
    psum x1 -> x0, blocking collectives: 64.9 us -> none  [body(): trace = lax.psum(local_trace, ('row', 'col')) / total_rows]
    ppermute x4 -> x7, waiting for transfers between devices: 42.2 us -> 0.02 us  [moved(): return lax.ppermute(message, AXES, pairs)]
    pallas_call x0 -> x6, Pallas kernels: none -> 15.8 us  [call(): pl.pallas_call(kernel, out_shape=[pltpu.HBM(o.shape, o.dtype) if s is ANY...]
    all_to_all x0 -> x1, starting transfers between devices: none -> 10.3 us  [body(): gathered = lax.all_to_all(shares, AXES, 0, 0)]
    ppermute x4 -> x7, starting transfers between devices: 8.71 us -> 13.8 us  [moved(): return lax.ppermute(message, AXES, pairs)]
    all_to_all x0 -> x1, waiting for transfers between devices: none -> 4.92 us  [body(): gathered = lax.all_to_all(shares, AXES, 0, 0)]
    squeeze x2 -> x0, local copies, waits for them, and re-layouts: 4.68 us -> none  [body(): local_trace = jnp.sum(jnp.diagonal(updated[:, :, 4], axis1=2, axis2=3))]
  transfers between devices with their start and end apart: 4 -> 8, of which waited for: 4 -> 1; matrix products, arithmetic and copies ran while one was open for 14% -> 0% of each run, Pallas kernels for 0% -> 25%
where the time goes in v2:
time: 48.7 us; the launch traced here: 48.4 us
  starting transfers between devices  24.1 us (49%)
  Pallas kernels  15.8 us (32%)
  waiting for transfers between devices  4.94 us (10%)
  between operations  2.01 us (4%)
  local copies, waits for them, and re-layouts  1.59 us (3%)
    pallas_call x6, Pallas kernels, call(): pl.pallas_call(kernel, out_shape=[pltpu.HBM(o.shape, o.dtype) if s is ANY...  15.8 us
    ppermute x7, starting transfers between devices, moved(): return lax.ppermute(message, AXES, pairs)  13.8 us
    all_to_all x1, starting transfers between devices, body(): gathered = lax.all_to_all(shares, AXES, 0, 0)  10.3 us
    all_to_all x1, waiting for transfers between devices, body(): gathered = lax.all_to_all(shares, AXES, 0, 0)  4.92 us
    unnamed x4, local copies, waits for them, and re-layouts  1.59 us
  transfers between devices with their start and end apart: 8, of which 1 were waited for; matrix products, arithmetic and copies ran while one was open for 0% of the time, Pallas kernels for 25%

profile of v2, /device:TPU:1, one launch (start us, length us, event | category | flops | bytes accessed | tf_op | source)
XLA Modules:
  0.0 48.4 jit_solution(9176210600787458624)
XLA Ops:
  0.6 2.9 %shard_map.59 = (f32[1160,128]{1,0:T(8,128)S(1)}, f32[776,128]{1,0:T(8,128)}, f32[3080,128]{1,0:T(8,128)S(1)}, f32[1920,128]{1,0:T(8,128)}, f32[768,128]{1,0:T(8,128)}, /*index=5*/f32[384,128]{1,0:T(8,128)S(1)}) custom-call(f32[1,4,9,128,128]{4,3,2,1,0:T(8,128)} %x.1, s32[1,4,9]{2,1,0:T(4,128)} %pat.3), custom_call_target="tpu_custom_call" | custom-call | flops 1000 | bytes 1000 | tf_op jit(solution)/shard_map/pallas_call | solution.py:274
  3.5 0.0 copy-start
  3.5 0.7 %copy-done = f32[384,128]{1,0:T(8,128)} copy-done((f32[384,128]{1,0:T(8,128)}, f32[384,128]{1,0:T(8,128)S(1)}, u32[]{:S(2)}) %copy-start) | copy-done | bytes 196632
  4.2 1.4 %collective-permute-start = (f32[3080,128]{1,0:T(8,128)S(1)}, f32[3080,128]{1,0:T(8,128)}, u32[]{:S(2)}, u32[]{:S(2)}) collective-permute-start(f32[3080,128]{1,0:T(8,128)S(1)} %get-tuple-element.16.twm), channel_id=1, source_target_pairs={{0,16},{1,17},{2,18},{3,19},{4,20},{5,21},{6,22},{7,23},{8,24},{9,... | collective-permute-start | bytes 4730888 | tf_op jit(solution)/shard_map/ppermute | solution.py:270
  5.6 1.3 %collective-permute-start.2 = (f32[1920,128]{1,0:T(8,128)}, f32[1920,128]{1,0:T(8,128)}, u32[]{:S(2)}, u32[]{:S(2)}) collective-permute-start(f32[1920,128]{1,0:T(8,128)} %get-tuple-element.19), channel_id=1, source_target_pairs={{0,112},{1,113},{2,114},{3,115},{4,116},{5,117},{6,118},{7,119},{8... | collective-permute-start | bytes 2949128 | tf_op jit(solution)/shard_map/ppermute | solution.py:270
  6.9 1.2 %collective-permute-start.3 = (f32[776,128]{1,0:T(8,128)}, f32[776,128]{1,0:T(8,128)S(1)}, u32[]{:S(2)}, u32[]{:S(2)}) collective-permute-start(f32[776,128]{1,0:T(8,128)} %get-tuple-element.20), channel_id=1, source_target_pairs={{0,1},{1,2},{2,3},{3,4},{4,5},{5,6},{6,7},{7,8},{8,9},{9,10},{10,1... | collective-permute-start | bytes 1191944 | tf_op jit(solution)/shard_map/ppermute | solution.py:270
  8.1 4.7 %collective-permute-start.4 = (f32[768,128]{1,0:T(8,128)}, f32[768,128]{1,0:T(8,128)S(1)}, u32[]{:S(2)}, u32[]{:S(2)}) collective-permute-start(f32[768,128]{1,0:T(8,128)} %get-tuple-element.21), channel_id=1, source_target_pairs={{0,15},{1,0},{2,1},{3,2},{4,3},{5,4},{6,5},{7,6},{8,7},{9,8},{10,9... | collective-permute-start | bytes 1179656 | tf_op jit(solution)/shard_map/ppermute | solution.py:270
  12.8 0.8 %collective-permute-start.1 = (f32[1160,128]{1,0:T(8,128)S(1)}, f32[1160,128]{1,0:T(8,128)S(1)}, u32[]{:S(2)}, u32[]{:S(2)}) collective-permute-start(f32[1160,128]{1,0:T(8,128)S(1)} %get-tuple-element.14.c1m), channel_id=1, source_target_pairs={{0,112},{1,113},{2,114},{3,115},{4,116},{5,117},{6,118},{7,119},{8... | collective-permute-start | bytes 1781768 | tf_op jit(solution)/shard_map/ppermute | solution.py:270
  15.0 0.0 collective-permute-done.tw
  15.0 0.0 copy-start.1
  15.0 0.9 %copy-done.1 = f32[384,128]{1,0:T(8,128)S(1)} copy-done((f32[384,128]{1,0:T(8,128)S(1)}, f32[384,128]{1,0:T(8,128)}, u32[]{:S(2)}) %copy-start.1) | copy-done | bytes 196632
  15.9 5.3 %shard_map.60 = (f32[36,128,128]{2,1,0:T(8,128)}, bf16[32,128,128]{2,1,0:T(8,128)(2,1)}, f32[128,128]{1,0:T(8,128)S(1)}, f32[1168,128]{1,0:T(8,128)S(1)}) custom-call(f32[1,1]{1,0:T(1,128)} %bitcast.7.alpha, f32[1,1]{1,0:T(1,128)} %bitcast.8.beta, f32[1160,128]{1,0:T(8,128)S(1)} %get-tuple-element.14.c1m, f32[384,128]{1,0:T(8,128)S(1)} %copy-done.1, ...), custom_call_target="tpu_custom_call" | custom-call | flops 1000 | bytes 1000 | tf_op jit(solution)/shard_map/pallas_call | solution.py:274
  21.2 0.0 collective-permute-done.4.we
  21.2 0.0 collective-permute-done.3.ea
  21.2 1.0 %shard_map.61 = (f32[1024,128]{1,0:T(8,128)}, f32[1024,128]{1,0:T(8,128)}) custom-call(f32[776,128]{1,0:T(8,128)S(1)} %collective-permute-done.3.ea, f32[768,128]{1,0:T(8,128)S(1)} %collective-permute-done.4.we, f32[128,128]{1,0:T(8,128)S(1)} %get-tuple-element.22.after.pairs), custom_call_target="tpu_custom_call" | custom-call | flops 1000 | bytes 1000 | tf_op jit(solution)/shard_map/pallas_call | solution.py:274
  22.3 2.4 %collective-permute-start.5 = (f32[1024,128]{1,0:T(8,128)}, f32[1024,128]{1,0:T(8,128)S(1)}, u32[]{:S(2)}, u32[]{:S(2)}) collective-permute-start(f32[1024,128]{1,0:T(8,128)} %get-tuple-element.23), channel_id=1, source_target_pairs={{0,112},{1,113},{2,114},{3,115},{4,116},{5,117},{6,118},{7,119},{8... | collective-permute-start | bytes 1572872 | tf_op jit(solution)/shard_map/ppermute | solution.py:270
  24.6 2.0 %collective-permute-start.6 = (f32[1024,128]{1,0:T(8,128)}, f32[1024,128]{1,0:T(8,128)S(1)}, u32[]{:S(2)}, u32[]{:S(2)}) collective-permute-start(f32[1024,128]{1,0:T(8,128)} %get-tuple-element.24), channel_id=1, source_target_pairs={{0,16},{1,17},{2,18},{3,19},{4,20},{5,21},{6,22},{7,23},{8,24},{9,... | collective-permute-start | bytes 1572872 | tf_op jit(solution)/shard_map/ppermute | solution.py:270
  26.6 0.0 collective-permute-done.1.c1
  26.6 1.1 %shard_map.63 = f32[128,128]{1,0:T(8,128)} custom-call(f32[1,1]{1,0:T(1,128)} %bitcast.9.beta, f32[128,128]{1,0:T(8,128)S(1)} %get-tuple-element.22.after.pairs, f32[1168,128]{1,0:T(8,128)S(1)} %get-tuple-element.25.few, f32[1160,128]{1,0:T(8,128)S(1)} %collective-permute-done.1.c1, f32[776,128]{1,0:T(8,128)S(1)} %collective-permute-done.3.ea), custom_call_target="tpu_custom_call" | custom-call | flops 1000 | bytes 1000 | tf_op jit(solution)/shard_map/pallas_call | solution.py:274
  27.7 10.3 %all-to-all-start = ((f32[128,1,128]{2,1,0:T(1,128)}), f32[128,1,128]{2,1,0:T(1,128)S(1)}, u32[]{:S(2)}, u32[]{:S(2)}) async-start(f32[128,1,128]{2,1,0:T(1,128)} %bitcast.3), calls=%async_computation | async-start | bytes 131072 | tf_op jit(solution)/shard_map/all_to_all | solution.py:321
  38.0 0.0 collective-permute-done.2.c2
  38.0 0.0 collective-permute-done.5.cc
  38.0 0.0 collective-permute-done.6.tc
  38.1 4.8 %shard_map.62.after = f32[1,4,9,128,128]{4,3,2,1,0:T(8,128)} custom-call(s32[1,4,9]{2,1,0:T(4,128)} %pat.3, bf16[32,128,128]{2,1,0:T(8,128)(2,1)} %get-tuple-element.17.lefts, f32[36,128,128]{2,1,0:T(8,128)} %get-tuple-element.18.acc, f32[1160,128]{1,0:T(8,128)S(1)} %collective-permute-done.1.c1, f32[1920,128]{1,0:T(8,128)} %collective-permute-done.2.c2, ...), custom_call_target="tpu_custom_call" | custom-call | flops 1000 | bytes 1000 | tf_op jit(solution)/shard_map/pallas_call | solution.py:274
  42.9 4.9 %all-to-all-done = f32[128,1,128]{2,1,0:T(1,128)S(1)} async-done(((f32[128,1,128]{2,1,0:T(1,128)}), f32[128,1,128]{2,1,0:T(1,128)S(1)}, u32[]{:S(2)}, u32[]{:S(2)}) %all-to-all-start) | async-done | bytes 65568 | tf_op jit(solution)/shard_map/all_to_all | solution.py:321
  47.8 0.6 %shard_map.64 = f32[1,1]{1,0:T(1,128)} custom-call(f32[128,128]{1,0:T(8,128)S(1)} %bitcast.10, f32[1,4,9,128,128]{4,3,2,1,0:T(8,128)} %shard_map.62.after), custom_call_target="tpu_custom_call" | custom-call | flops 1000 | bytes 1000 | tf_op jit(solution)/shard_map/pallas_call | solution.py:274
Async XLA Ops:
  3.5 0.7 %copy-start = (f32[384,128]{1,0:T(8,128)}, f32[384,128]{1,0:T(8,128)S(1)}, u32[]{:S(2)}) copy-start(f32[384,128]{1,0:T(8,128)S(1)} %get-tuple-element.15.rest) | copy-start | bytes 589828
  4.2 10.8 %collective-permute-start = (f32[3080,128]{1,0:T(8,128)S(1)}, f32[3080,128]{1,0:T(8,128)}, u32[]{:S(2)}, u32[]{:S(2)}) collective-permute-start(f32[3080,128]{1,0:T(8,128)S(1)} %get-tuple-element.16.twm), channel_id=1, source_target_pairs={{0,16},{1,17},{2,18},{3,19},{4,20},{5,21},{6,22},{7,23},{8,24},{9,... | collective-permute-start | bytes 4730888 | tf_op jit(solution)/shard_map/ppermute | solution.py:270
  5.6 32.4 %collective-permute-start.2 = (f32[1920,128]{1,0:T(8,128)}, f32[1920,128]{1,0:T(8,128)}, u32[]{:S(2)}, u32[]{:S(2)}) collective-permute-start(f32[1920,128]{1,0:T(8,128)} %get-tuple-element.19), channel_id=1, source_target_pairs={{0,112},{1,113},{2,114},{3,115},{4,116},{5,117},{6,118},{7,119},{8... | collective-permute-start | bytes 2949128 | tf_op jit(solution)/shard_map/ppermute | solution.py:270
  6.9 14.3 %collective-permute-start.3 = (f32[776,128]{1,0:T(8,128)}, f32[776,128]{1,0:T(8,128)S(1)}, u32[]{:S(2)}, u32[]{:S(2)}) collective-permute-start(f32[776,128]{1,0:T(8,128)} %get-tuple-element.20), channel_id=1, source_target_pairs={{0,1},{1,2},{2,3},{3,4},{4,5},{5,6},{6,7},{7,8},{8,9},{9,10},{10,1... | collective-permute-start | bytes 1191944 | tf_op jit(solution)/shard_map/ppermute | solution.py:270
  8.1 13.1 %collective-permute-start.4 = (f32[768,128]{1,0:T(8,128)}, f32[768,128]{1,0:T(8,128)S(1)}, u32[]{:S(2)}, u32[]{:S(2)}) collective-permute-start(f32[768,128]{1,0:T(8,128)} %get-tuple-element.21), channel_id=1, source_target_pairs={{0,15},{1,0},{2,1},{3,2},{4,3},{5,4},{6,5},{7,6},{8,7},{9,8},{10,9... | collective-permute-start | bytes 1179656 | tf_op jit(solution)/shard_map/ppermute | solution.py:270
  12.8 13.8 %collective-permute-start.1 = (f32[1160,128]{1,0:T(8,128)S(1)}, f32[1160,128]{1,0:T(8,128)S(1)}, u32[]{:S(2)}, u32[]{:S(2)}) collective-permute-start(f32[1160,128]{1,0:T(8,128)S(1)} %get-tuple-element.14.c1m), channel_id=1, source_target_pairs={{0,112},{1,113},{2,114},{3,115},{4,116},{5,117},{6,118},{7,119},{8... | collective-permute-start | bytes 1781768 | tf_op jit(solution)/shard_map/ppermute | solution.py:270
  15.0 0.9 %copy-start.1 = (f32[384,128]{1,0:T(8,128)S(1)}, f32[384,128]{1,0:T(8,128)}, u32[]{:S(2)}) copy-start(f32[384,128]{1,0:T(8,128)} %copy-done) | copy-start | bytes 589828
  22.3 15.8 %collective-permute-start.5 = (f32[1024,128]{1,0:T(8,128)}, f32[1024,128]{1,0:T(8,128)S(1)}, u32[]{:S(2)}, u32[]{:S(2)}) collective-permute-start(f32[1024,128]{1,0:T(8,128)} %get-tuple-element.23), channel_id=1, source_target_pairs={{0,112},{1,113},{2,114},{3,115},{4,116},{5,117},{6,118},{7,119},{8... | collective-permute-start | bytes 1572872 | tf_op jit(solution)/shard_map/ppermute | solution.py:270
  24.6 13.4 %collective-permute-start.6 = (f32[1024,128]{1,0:T(8,128)}, f32[1024,128]{1,0:T(8,128)S(1)}, u32[]{:S(2)}, u32[]{:S(2)}) collective-permute-start(f32[1024,128]{1,0:T(8,128)} %get-tuple-element.24), channel_id=1, source_target_pairs={{0,16},{1,17},{2,18},{3,19},{4,20},{5,21},{6,22},{7,23},{8,24},{9,... | collective-permute-start | bytes 1572872 | tf_op jit(solution)/shard_map/ppermute | solution.py:270
  27.7 20.1 %all-to-all-start = ((f32[128,1,128]{2,1,0:T(1,128)}), f32[128,1,128]{2,1,0:T(1,128)S(1)}, u32[]{:S(2)}, u32[]{:S(2)}) async-start(f32[128,1,128]{2,1,0:T(1,128)} %bitcast.3), calls=%async_computation | async-start | bytes 131072 | tf_op jit(solution)/shard_map/all_to_all | solution.py:321

commit v3 on v2

--- a/solution.py
+++ b/solution.py
@@ -22,8 +22,6 @@
     return kind * 12 + v * 3 + j + 1
 
 
-FIRST = [0, 1, 2, 4, 5, 7, 8, 10, 11]
-SECOND = [3, 6, 9]
 HEAD = 8
 
 
@@ -70,7 +68,7 @@
         return copy
 
 
-def pack_kernel(x, pat, c1, ea, tw, c2, we, rest, stage, table, sems):
+def pack_kernel(x, pat, c1, ea, tw, c2, we, stage, table, sems):
     odd = lax.rem(lax.axis_index("row"), 2)
     dma = Copies(sems)
     order = (0, 3, 1, 2)
@@ -91,27 +89,22 @@
                 s = slot(kind, j, odd)
                 block = stage[v, s] * weight(table, v, s)
                 i = at(kind, v, j)
-                if kind != CR:
+                if kind == CR:
+                    put(c1, i, block, HEAD)
+                else:
                     put(tw, i - 12, block, HEAD)
-                elif i in FIRST:
-                    put(c1, FIRST.index(i), block, HEAD)
-                else:
-                    put(c2, SECOND.index(i), block)
-                    put(rest, SECOND.index(i), block)
                 if kind == MID:
-                    put(c2, 3 + i - 24, block)
+                    put(c2, i - 24, block)
                 if v == 3 and j >= 0:
                     put(ea, 2 * kind + j, block, HEAD)
                 if v == 0 and j < 1:
                     put(we, 2 * kind + j + 1, block)
 
 
-def near_kernel(alpha, beta, c1m, rest, twm, tw, acc, lefts, pairs, few, lh, ll, sh, sl, rh, rl):
+def near_kernel(alpha, beta, c1m, twm, tw, acc, lefts, pairs, few, lh, ll, sh, sl, rh, rl):
     def own(kind, v, j):
         i = at(kind, v, j)
-        if kind != CR:
-            return get(twm, i - 12, HEAD)
-        return get(c1m, FIRST.index(i), HEAD) if i in FIRST else get(rest, SECOND.index(i))
+        return get(c1m, i, HEAD) if kind == CR else get(twm, i - 12, HEAD)
 
     sources = {at(CR, v, a): at(CR, v, a) for v in range(4) for a in (-1, 0, 1)}
     sources.update({at(TW, 0, -1): 12, at(TW, 3, 1): 13, at(MID, 0, -1): 14, at(MID, 3, 1): 15})
@@ -174,16 +167,22 @@
         put(few, i, block, 2 * HEAD)
 
 
-def trace_kernel(beta, pairs, few, c1, ea, out):
+def middle_kernel(beta, pairs, few, c1, ea, we, cc, tc, shares):
+    for out, toward in ((cc, CR), (tc, TW)):
+        for i, k in enumerate((toward, MID)):
+            for n in (0, 1):
+                put(out, 2 * i + n, get(ea, 2 * k + n, HEAD))
+                put(out, 4 + 2 * i + n, get(we, 2 * k + n))
+
     own = lambda v: few[pl.ds(v, 1), :]
     far = lambda v: c1[pl.ds(v, 1), :]
     west = ea[pl.ds(3, 1), :]
     kept = lambda i: get(few, i, 2 * HEAD)
     listed = []
     for v in range(4):
-        listed.append((own(v), kept(v), get(c1, 2 * v + 1, HEAD)))
+        listed.append((own(v), kept(v), get(c1, at(CR, v, 0), HEAD)))
     for v in range(3):
-        listed.append((own(v + 1) + far(v), kept(4 + v), get(c1, 2 * v + 2, HEAD)))
+        listed.append((own(v + 1) + far(v), kept(4 + v), get(c1, at(CR, v, 1), HEAD)))
     listed.append((west + own(0), get(ea, 2 * MID + 1, HEAD), kept(7)))
     listed.append((west + far(0), get(ea, 2 * CR + 1, HEAD), get(c1, 0, HEAD)))
     listed.append((west + few[pl.ds(HEAD, 1), :], get(ea, 2 * TW + 1, HEAD), kept(8)))
@@ -191,19 +190,11 @@
     rows = lax.broadcasted_iota(jnp.int32, (B, B), 0)
     columns = lax.broadcasted_iota(jnp.int32, (B, B), 1)
     line = jnp.sum(jnp.where(rows == columns, value, 0.0), axis=0, keepdims=True)
-    out[...] = jnp.broadcast_to(line, (B, B))
+    shares[...] = jnp.broadcast_to(line, (B, B))
 
 
 def sum_kernel(scale, shares, after, out):
     out[0, 0] = jnp.sum(shares[...]) * scale
-
-
-def corner_kernel(ea, we, after, cc, tc):
-    for out, toward in ((cc, CR), (tc, TW)):
-        for i, k in enumerate((toward, MID)):
-            for n in (0, 1):
-                put(out, 2 * i + n, get(ea, 2 * k + n, HEAD))
-                put(out, 4 + 2 * i + n, get(we, 2 * k + n))
 
 
 def final_kernel(pat, lefts, acc, c1, c2, ea, we, cc, tc, out, total, stage, sems):
@@ -229,10 +220,6 @@
     spread(at(CR, 0, -1), [get(cc, i) for i in range(4)], [(MID, 0, -1), (MID, 0, 0), (CR, 0, -1), (CR, 0, 0)])
     spread(at(CR, 3, 1), [get(cc, 4 + i) for i in range(4)], [(MID, 3, 0), (MID, 3, 1), (CR, 3, 0), (CR, 3, 1)])
 
-    def far(w, t):
-        i = at(CR, w, t)
-        return get(c1, FIRST.index(i), HEAD) if i in FIRST else get(c2, SECOND.index(i))
-
     stores = []
 
     def finish(v):
@@ -246,7 +233,7 @@
         for t in (0, -1, 1):
             targets = [(w - a, a) for a in (-1, 0, 1) if 0 <= w - a < 4 and -1 <= a + t <= 1]
             lines = [[left(at(CR, v, a))] for v, a in targets]
-            result = dot3(lines, [[split(far(w, t)), split(get(c2, 3 + w * 3 + t + 1))]])
+            result = dot3(lines, [[split(get(c1, at(CR, w, t), HEAD)), split(get(c2, at(CR, w, t)))]])
             for n, (v, a) in enumerate(targets):
                 rows = slice(n * B, (n + 1) * B)
                 add(MID, v, a + t, result[rows, :B])
@@ -293,9 +280,9 @@
     west = lambda r, c: (r, c - 1)
     alpha, beta = alpha.reshape(1, 1), beta.reshape(1, 1)
 
-    *messages, rest = call(
+    messages = call(
         pack_kernel,
-        [(lines(9, HEAD), VMEM), (lines(6, HEAD), VMEM), (lines(24, HEAD), VMEM), (lines(15), VMEM), (lines(6), VMEM), (lines(3), VMEM)],
+        [(lines(12, HEAD), VMEM), (lines(6, HEAD), VMEM), (lines(24, HEAD), VMEM), (lines(12), VMEM), (lines(6), VMEM)],
         (x, pat),
         [ANY, ANY],
         10,
@@ -306,21 +293,20 @@
     acc, lefts, pairs, few = call(
         near_kernel,
         [(shape(36, B, B), FAR), (shape(32, B, B, dtype=BF16), FAR), (shape(B, B), VMEM), (lines(9, 2 * HEAD), VMEM)],
-        (alpha, beta, c1m, rest, twm, tw),
-        [VMEM] * 6,
+        (alpha, beta, c1m, twm, tw),
+        [VMEM] * 5,
         14,
         [vmem(n, B, B, dtype=BF16) for n in (24, 24, 24, 24, 36, 36)],
     )
-    (shares,) = call(
-        trace_kernel,
-        [(shape(B, B), VMEM)],
-        (beta, pairs, few, c1, ea),
-        [VMEM] * 5,
+    *corners, shares = call(
+        middle_kernel,
+        [(lines(8), VMEM), (lines(8), VMEM), (shape(B, B), VMEM)],
+        (beta, pairs, few, c1, ea, we),
+        [VMEM] * 6,
         4,
     )
+    cc, tc = moved(corners[0], cross), moved(corners[1], twin)
     gathered = lax.all_to_all(shares, AXES, 0, 0)
-    corners = call(corner_kernel, [(lines(8), VMEM)] * 2, (ea, we, pairs), [VMEM] * 3, 4)
-    cc, tc = moved(corners[0], cross), moved(corners[1], twin)
     (updated,) = call(
         final_kernel,
         [(shape(*x.shape), ANY)],

time: 48.7 us -> 43.5 us (0.89)
  starting transfers between devices: 24.1 us -> 20.9 us
  local copies, waits for them, and re-layouts: 1.59 us -> 0 us
  Pallas kernels: 15.8 us -> 15.2 us
    all_to_all x1, starting transfers between devices: 10.3 us -> 7.08 us  [body(): gathered = lax.all_to_all(shares, AXES, 0, 0)]
    unnamed x4 -> x0, local copies, waits for them, and re-layouts: 1.59 us -> none
    pallas_call x6 -> x5, Pallas kernels: 15.8 us -> 15.2 us  [call(): pl.pallas_call(kernel, out_shape=[pltpu.HBM(o.shape, o.dtype) if s is ANY...]
  transfers between devices with their start and end apart: 8 -> 8, of which waited for: 1 -> 2; matrix products, arithmetic and copies ran while one was open for 0% -> 0% of each run, Pallas kernels for 25% -> 27%
where the time goes in v3:
time: 43.5 us; the launch traced here: 43.2 us
  starting transfers between devices  20.9 us (48%)
  Pallas kernels  15.2 us (35%)
  waiting for transfers between devices  5.11 us (12%)
  between operations  1.99 us (5%)
    pallas_call x5, Pallas kernels, call(): pl.pallas_call(kernel, out_shape=[pltpu.HBM(o.shape, o.dtype) if s is ANY...  15.2 us
    ppermute x7, starting transfers between devices, moved(): return lax.ppermute(message, AXES, pairs)  13.8 us
    all_to_all x1, starting transfers between devices, body(): gathered = lax.all_to_all(shares, AXES, 0, 0)  7.08 us
    all_to_all x1, waiting for transfers between devices, body(): gathered = lax.all_to_all(shares, AXES, 0, 0)  5 us
  transfers between devices with their start and end apart: 8, of which 2 were waited for; matrix products, arithmetic and copies ran while one was open for 0% of the time, Pallas kernels for 27%

profile of v3, /device:TPU:1, one launch (start us, length us, event | category | flops | bytes accessed | tf_op | source)
XLA Modules:
  0.0 43.2 jit_solution(13399925992397071400)
XLA Ops:
  0.6 3.0 %shard_map.59 = (f32[1544,128]{1,0:T(8,128)}, f32[776,128]{1,0:T(8,128)S(1)}, f32[3080,128]{1,0:T(8,128)S(1)}, f32[1536,128]{1,0:T(8,128)}, f32[768,128]{1,0:T(8,128)}) custom-call(f32[1,4,9,128,128]{4,3,2,1,0:T(8,128)} %x.1, s32[1,4,9]{2,1,0:T(4,128)} %pat.3), custom_call_target="tpu_custom_call" | custom-call | flops 1000 | bytes 1000 | tf_op jit(solution)/shard_map/pallas_call | solution.py:261
  3.6 1.5 %collective-permute-start = (f32[3080,128]{1,0:T(8,128)S(1)}, f32[3080,128]{1,0:T(8,128)}, u32[]{:S(2)}, u32[]{:S(2)}) collective-permute-start(f32[3080,128]{1,0:T(8,128)S(1)} %get-tuple-element.15.twm), channel_id=1, source_target_pairs={{0,16},{1,17},{2,18},{3,19},{4,20},{5,21},{6,22},{7,23},{8,24},{9,... | collective-permute-start | bytes 4730888 | tf_op jit(solution)/shard_map/ppermute | solution.py:257
  5.1 1.4 %collective-permute-start.1 = (f32[1544,128]{1,0:T(8,128)}, f32[1544,128]{1,0:T(8,128)S(1)}, u32[]{:S(2)}, u32[]{:S(2)}) collective-permute-start(f32[1544,128]{1,0:T(8,128)} %get-tuple-element.14.c1m), channel_id=1, source_target_pairs={{0,112},{1,113},{2,114},{3,115},{4,116},{5,117},{6,118},{7,119},{8... | collective-permute-start | bytes 2371592 | tf_op jit(solution)/shard_map/ppermute | solution.py:257
  6.4 1.2 %collective-permute-start.3 = (f32[776,128]{1,0:T(8,128)S(1)}, f32[776,128]{1,0:T(8,128)S(1)}, u32[]{:S(2)}, u32[]{:S(2)}) collective-permute-start(f32[776,128]{1,0:T(8,128)S(1)} %get-tuple-element.19), channel_id=1, source_target_pairs={{0,1},{1,2},{2,3},{3,4},{4,5},{5,6},{6,7},{7,8},{8,9},{9,10},{10,1... | collective-permute-start | bytes 1191944 | tf_op jit(solution)/shard_map/ppermute | solution.py:257
  7.7 4.7 %collective-permute-start.4 = (f32[768,128]{1,0:T(8,128)}, f32[768,128]{1,0:T(8,128)S(1)}, u32[]{:S(2)}, u32[]{:S(2)}) collective-permute-start(f32[768,128]{1,0:T(8,128)} %get-tuple-element.20), channel_id=1, source_target_pairs={{0,15},{1,0},{2,1},{3,2},{4,3},{5,4},{6,5},{7,6},{8,7},{9,8},{10,9... | collective-permute-start | bytes 1179656 | tf_op jit(solution)/shard_map/ppermute | solution.py:257
  12.4 0.8 %collective-permute-start.2 = (f32[1536,128]{1,0:T(8,128)}, f32[1536,128]{1,0:T(8,128)}, u32[]{:S(2)}, u32[]{:S(2)}) collective-permute-start(f32[1536,128]{1,0:T(8,128)} %get-tuple-element.18), channel_id=1, source_target_pairs={{0,112},{1,113},{2,114},{3,115},{4,116},{5,117},{6,118},{7,119},{8... | collective-permute-start | bytes 2359304 | tf_op jit(solution)/shard_map/ppermute | solution.py:257
  14.5 0.0 collective-permute-done.tw
  14.5 5.5 %shard_map.60 = (f32[36,128,128]{2,1,0:T(8,128)}, bf16[32,128,128]{2,1,0:T(8,128)(2,1)}, f32[128,128]{1,0:T(8,128)S(1)}, f32[1168,128]{1,0:T(8,128)S(1)}) custom-call(f32[1,1]{1,0:T(1,128)} %bitcast.7.alpha, f32[1,1]{1,0:T(1,128)} %bitcast.8.beta, f32[1544,128]{1,0:T(8,128)} %get-tuple-element.14.c1m, f32[3080,128]{1,0:T(8,128)S(1)} %get-tuple-element.15.twm, ...), custom_call_target="tpu_custom_call" | custom-call | flops 1000 | bytes 1000 | tf_op jit(solution)/shard_map/pallas_call | solution.py:261
  20.0 0.0 collective-permute-done.4.we
  20.0 0.1 collective-permute-done.3.ea
  20.1 0.0 collective-permute-done.1.c1
  20.1 1.4 %shard_map.61 = (f32[1024,128]{1,0:T(8,128)}, f32[1024,128]{1,0:T(8,128)}, f32[128,128]{1,0:T(8,128)}) custom-call(f32[1,1]{1,0:T(1,128)} %bitcast.9.beta, f32[128,128]{1,0:T(8,128)S(1)} %get-tuple-element.21.pairs, f32[1168,128]{1,0:T(8,128)S(1)} %get-tuple-element.22.few, f32[1544,128]{1,0:T(8,128)S(1)} %collective-permute-done.1.c1, ...), custom_call_target="tpu_custom_call" | custom-call | flops 1000 | bytes 1000 | tf_op jit(solution)/shard_map/pallas_call | solution.py:261
  21.5 2.7 %collective-permute-start.5 = (f32[1024,128]{1,0:T(8,128)}, f32[1024,128]{1,0:T(8,128)S(1)}, u32[]{:S(2)}, u32[]{:S(2)}) collective-permute-start(f32[1024,128]{1,0:T(8,128)} %get-tuple-element.23), channel_id=1, source_target_pairs={{0,112},{1,113},{2,114},{3,115},{4,116},{5,117},{6,118},{7,119},{8... | collective-permute-start | bytes 1572872 | tf_op jit(solution)/shard_map/ppermute | solution.py:257
  24.2 1.6 %collective-permute-start.6 = (f32[1024,128]{1,0:T(8,128)}, f32[1024,128]{1,0:T(8,128)S(1)}, u32[]{:S(2)}, u32[]{:S(2)}) collective-permute-start(f32[1024,128]{1,0:T(8,128)} %get-tuple-element.24), channel_id=1, source_target_pairs={{0,16},{1,17},{2,18},{3,19},{4,20},{5,21},{6,22},{7,23},{8,24},{9,... | collective-permute-start | bytes 1572872 | tf_op jit(solution)/shard_map/ppermute | solution.py:257
  25.7 7.1 %all-to-all-start = ((f32[128,1,128]{2,1,0:T(1,128)}), f32[128,1,128]{2,1,0:T(1,128)S(1)}, u32[]{:S(2)}, u32[]{:S(2)}) async-start(f32[128,1,128]{2,1,0:T(1,128)} %bitcast.3), calls=%async_computation | async-start | bytes 131072 | tf_op jit(solution)/shard_map/all_to_all | solution.py:309
  32.8 0.0 collective-permute-done.2.c2
  32.8 0.0 collective-permute-done.5.cc
  32.8 0.0 collective-permute-done.6.tc
  32.9 4.7 %shard_map.62.after = f32[1,4,9,128,128]{4,3,2,1,0:T(8,128)} custom-call(s32[1,4,9]{2,1,0:T(4,128)} %pat.3, bf16[32,128,128]{2,1,0:T(8,128)(2,1)} %get-tuple-element.16.lefts, f32[36,128,128]{2,1,0:T(8,128)} %get-tuple-element.17.acc, f32[1544,128]{1,0:T(8,128)S(1)} %collective-permute-done.1.c1, f32[1536,128]{1,0:T(8,128)} %collective-permute-done.2.c2, ...), custom_call_target="tpu_custom_call" | custom-call | flops 1000 | bytes 1000 | tf_op jit(solution)/shard_map/pallas_call | solution.py:261
  37.6 5.0 %all-to-all-done = f32[128,1,128]{2,1,0:T(1,128)S(1)} async-done(((f32[128,1,128]{2,1,0:T(1,128)}), f32[128,1,128]{2,1,0:T(1,128)S(1)}, u32[]{:S(2)}, u32[]{:S(2)}) %all-to-all-start) | async-done | bytes 65568 | tf_op jit(solution)/shard_map/all_to_all | solution.py:309
  42.6 0.6 %shard_map.63 = f32[1,1]{1,0:T(1,128)} custom-call(f32[128,128]{1,0:T(8,128)S(1)} %bitcast.10, f32[1,4,9,128,128]{4,3,2,1,0:T(8,128)} %shard_map.62.after), custom_call_target="tpu_custom_call" | custom-call | flops 1000 | bytes 1000 | tf_op jit(solution)/shard_map/pallas_call | solution.py:261
Async XLA Ops:
  3.6 10.9 %collective-permute-start = (f32[3080,128]{1,0:T(8,128)S(1)}, f32[3080,128]{1,0:T(8,128)}, u32[]{:S(2)}, u32[]{:S(2)}) collective-permute-start(f32[3080,128]{1,0:T(8,128)S(1)} %get-tuple-element.15.twm), channel_id=1, source_target_pairs={{0,16},{1,17},{2,18},{3,19},{4,20},{5,21},{6,22},{7,23},{8,24},{9,... | collective-permute-start | bytes 4730888 | tf_op jit(solution)/shard_map/ppermute | solution.py:257
  5.1 15.0 %collective-permute-start.1 = (f32[1544,128]{1,0:T(8,128)}, f32[1544,128]{1,0:T(8,128)S(1)}, u32[]{:S(2)}, u32[]{:S(2)}) collective-permute-start(f32[1544,128]{1,0:T(8,128)} %get-tuple-element.14.c1m), channel_id=1, source_target_pairs={{0,112},{1,113},{2,114},{3,115},{4,116},{5,117},{6,118},{7,119},{8... | collective-permute-start | bytes 2371592 | tf_op jit(solution)/shard_map/ppermute | solution.py:257
  6.4 13.6 %collective-permute-start.3 = (f32[776,128]{1,0:T(8,128)S(1)}, f32[776,128]{1,0:T(8,128)S(1)}, u32[]{:S(2)}, u32[]{:S(2)}) collective-permute-start(f32[776,128]{1,0:T(8,128)S(1)} %get-tuple-element.19), channel_id=1, source_target_pairs={{0,1},{1,2},{2,3},{3,4},{4,5},{5,6},{6,7},{7,8},{8,9},{9,10},{10,1... | collective-permute-start | bytes 1191944 | tf_op jit(solution)/shard_map/ppermute | solution.py:257
  7.7 12.3 %collective-permute-start.4 = (f32[768,128]{1,0:T(8,128)}, f32[768,128]{1,0:T(8,128)S(1)}, u32[]{:S(2)}, u32[]{:S(2)}) collective-permute-start(f32[768,128]{1,0:T(8,128)} %get-tuple-element.20), channel_id=1, source_target_pairs={{0,15},{1,0},{2,1},{3,2},{4,3},{5,4},{6,5},{7,6},{8,7},{9,8},{10,9... | collective-permute-start | bytes 1179656 | tf_op jit(solution)/shard_map/ppermute | solution.py:257
  12.4 20.4 %collective-permute-start.2 = (f32[1536,128]{1,0:T(8,128)}, f32[1536,128]{1,0:T(8,128)}, u32[]{:S(2)}, u32[]{:S(2)}) collective-permute-start(f32[1536,128]{1,0:T(8,128)} %get-tuple-element.18), channel_id=1, source_target_pairs={{0,112},{1,113},{2,114},{3,115},{4,116},{5,117},{6,118},{7,119},{8... | collective-permute-start | bytes 2359304 | tf_op jit(solution)/shard_map/ppermute | solution.py:257
  21.5 11.4 %collective-permute-start.5 = (f32[1024,128]{1,0:T(8,128)}, f32[1024,128]{1,0:T(8,128)S(1)}, u32[]{:S(2)}, u32[]{:S(2)}) collective-permute-start(f32[1024,128]{1,0:T(8,128)} %get-tuple-element.23), channel_id=1, source_target_pairs={{0,112},{1,113},{2,114},{3,115},{4,116},{5,117},{6,118},{7,119},{8... | collective-permute-start | bytes 1572872 | tf_op jit(solution)/shard_map/ppermute | solution.py:257
  24.2 8.7 %collective-permute-start.6 = (f32[1024,128]{1,0:T(8,128)}, f32[1024,128]{1,0:T(8,128)S(1)}, u32[]{:S(2)}, u32[]{:S(2)}) collective-permute-start(f32[1024,128]{1,0:T(8,128)} %get-tuple-element.24), channel_id=1, source_target_pairs={{0,16},{1,17},{2,18},{3,19},{4,20},{5,21},{6,22},{7,23},{8,24},{9,... | collective-permute-start | bytes 1572872 | tf_op jit(solution)/shard_map/ppermute | solution.py:257
  25.7 16.9 %all-to-all-start = ((f32[128,1,128]{2,1,0:T(1,128)}), f32[128,1,128]{2,1,0:T(1,128)S(1)}, u32[]{:S(2)}, u32[]{:S(2)}) async-start(f32[128,1,128]{2,1,0:T(1,128)} %bitcast.3), calls=%async_computation | async-start | bytes 131072 | tf_op jit(solution)/shard_map/all_to_all | solution.py:309

commit v4 on v3

--- a/solution.py
+++ b/solution.py
@@ -22,6 +22,7 @@
     return kind * 12 + v * 3 + j + 1
 
 
+SIDE = {CR: 0, MID: 2, TW: 4}
 HEAD = 8
 
 
@@ -68,40 +69,53 @@
         return copy
 
 
-def pack_kernel(x, pat, c1, ea, tw, c2, we, stage, table, sems):
+def pack_kernel(x, pat, c1, ea, tw, c2, we, stage, toward, sides, table, sems):
     odd = lax.rem(lax.axis_index("row"), 2)
     dma = Copies(sems)
+    table_load = dma.start(pat, table)
     order = (0, 3, 1, 2)
-    table_load = dma.start(pat, table)
-    loads = {v: dma.start(x.at[0, v], stage.at[v]) for v in order}
+    loads = {}
+    for kind in (CR, MID, TW):
+        slots = pl.ds(slot(kind, -1, odd), 3)
+        for v in order:
+            loads[kind, v] = dma.start(x.at[0, v, slots], stage.at[v, slots])
     table_load.wait()
     rows = lax.broadcasted_iota(jnp.int32, (HEAD, B), 0)
     present = jnp.zeros((HEAD, B), F32)
     for v in range(4):
         present = jnp.where(rows == v, weight(table, v, 4), present)
-    for ref in (c1, ea, tw):
+    for ref in (toward, ea, tw):
         ref[pl.ds(0, HEAD), :] = present
 
-    for v in order:
-        loads[v].wait()
-        for kind in KINDS:
+    stores = []
+    for kind in (CR, MID, TW):
+        for v in order:
+            loads[kind, v].wait()
             for j in (-1, 0, 1):
                 s = slot(kind, j, odd)
                 block = stage[v, s] * weight(table, v, s)
                 i = at(kind, v, j)
                 if kind == CR:
-                    put(c1, i, block, HEAD)
+                    put(toward, i, block, HEAD)
                 else:
                     put(tw, i - 12, block, HEAD)
-                if kind == MID:
-                    put(c2, i - 24, block)
                 if v == 3 and j >= 0:
-                    put(ea, 2 * kind + j, block, HEAD)
+                    put(ea, SIDE[kind] + j, block, HEAD)
                 if v == 0 and j < 1:
-                    put(we, 2 * kind + j + 1, block)
-
-
-def near_kernel(alpha, beta, c1m, twm, tw, acc, lefts, pairs, few, lh, ll, sh, sl, rh, rl):
+                    put(sides, SIDE[kind] + j + 1, block)
+            if kind == TW and v == 0:
+                stores.append(dma.start(sides, we))
+        if kind == CR:
+            stores.append(dma.start(toward, c1))
+        if kind == MID:
+            stores.append(dma.start(tw.at[pl.ds(HEAD + 12 * B, 12 * B), :], c2))
+    for copy in stores:
+        copy.wait()
+
+
+def near_kernel(alpha, beta, c1m, twm, tw, acc, lefts, pairs, few, total, lefts_here, lh, ll, sh, sl, rh, rl, sems):
+    dma = Copies(sems)
+    stores = []
     def own(kind, v, j):
         i = at(kind, v, j)
         return get(c1m, i, HEAD) if kind == CR else get(twm, i - 12, HEAD)
@@ -114,13 +128,13 @@
             for j in (-1, 0, 1):
                 i = at(kind, v, j)
                 block = own(kind, v, j)
-                acc[v * 9 + kind * 3 + j + 1] = alpha[...] * block
+                total[v * 9 + kind * 3 + j + 1] = alpha[...] * block
                 rh[i], rl[i] = split(block)
                 high, low = split(beta[...] * block)
                 if kind != CR:
                     lh[i - 12], ll[i - 12] = high, low
                 if i in sources:
-                    lefts[sources[i]], lefts[16 + sources[i]] = high, low
+                    lefts_here[sources[i]], lefts_here[16 + sources[i]] = high, low
         for j in (-1, 0, 1):
             for kind in (TW, MID):
                 i = at(kind, v, j) - 12
@@ -131,10 +145,11 @@
     theirs = lambda kind, v, j: (sh[at(kind, v, j) - 12], sl[at(kind, v, j) - 12])
 
     def add(kind, v, sv, block):
-        acc[v * 9 + kind * 3 + sv + 1] += block
+        total[v * 9 + kind * 3 + sv + 1] += block
 
     for w in range(4):
         prepare(w)
+    stores.append(dma.start(lefts_here, lefts))
     for w in range(4):
         for t in (0, -1, 1):
             targets = [(w - a, a) for a in (-1, 0, 1) if 0 <= w - a < 4 and -1 <= a + t <= 1]
@@ -147,6 +162,9 @@
                 add(MID, v, a + t, both[rows, :B])
                 add(TW, v, a + t, both[rows, B:])
                 add(CR, v, a + t, only[rows])
+        for v in range(4):
+            if w == min(v + 1, 3):
+                stores.append(dma.start(total.at[pl.ds(v * 9, 9)], acc.at[pl.ds(v * 9, 9)]))
     present = lambda v: twm[pl.ds(v, 1), :]
     other = lambda v: tw[pl.ds(v, 1), :]
     listed = []
@@ -165,15 +183,15 @@
     kept = [own(CR, v, 0) for v in range(4)] + [own(CR, v, -1) for v in (1, 2, 3)] + [own(MID, 0, -1), get(tw, 0, HEAD)]
     for i, block in enumerate(kept):
         put(few, i, block, 2 * HEAD)
+    for copy in stores:
+        copy.wait()
 
 
 def middle_kernel(beta, pairs, few, c1, ea, we, cc, tc, shares):
-    for out, toward in ((cc, CR), (tc, TW)):
-        for i, k in enumerate((toward, MID)):
-            for n in (0, 1):
-                put(out, 2 * i + n, get(ea, 2 * k + n, HEAD))
-                put(out, 4 + 2 * i + n, get(we, 2 * k + n))
-
+    for out, kind, head in ((cc, CR, 0), (tc, MID, 0)):
+        for i in range(4):
+            put(out, i, get(ea, SIDE[kind] + i, HEAD), head)
+            put(out, 4 + i, get(we, SIDE[kind] + i), head)
     own = lambda v: few[pl.ds(v, 1), :]
     far = lambda v: c1[pl.ds(v, 1), :]
     west = ea[pl.ds(3, 1), :]
@@ -183,9 +201,9 @@
         listed.append((own(v), kept(v), get(c1, at(CR, v, 0), HEAD)))
     for v in range(3):
         listed.append((own(v + 1) + far(v), kept(4 + v), get(c1, at(CR, v, 1), HEAD)))
-    listed.append((west + own(0), get(ea, 2 * MID + 1, HEAD), kept(7)))
-    listed.append((west + far(0), get(ea, 2 * CR + 1, HEAD), get(c1, 0, HEAD)))
-    listed.append((west + few[pl.ds(HEAD, 1), :], get(ea, 2 * TW + 1, HEAD), kept(8)))
+    listed.append((west + own(0), get(ea, SIDE[MID] + 1, HEAD), kept(7)))
+    listed.append((west + far(0), get(ea, SIDE[CR] + 1, HEAD), get(c1, 0, HEAD)))
+    listed.append((west + few[pl.ds(HEAD, 1), :], get(ea, SIDE[TW] + 1, HEAD), kept(8)))
     value = pairs[...] + beta[...] * dot3([[split(a * w) for w, a, _ in listed]], [[split(b)] for _, _, b in listed])
     rows = lax.broadcasted_iota(jnp.int32, (B, B), 0)
     columns = lax.broadcasted_iota(jnp.int32, (B, B), 1)
@@ -213,10 +231,10 @@
         for n, (kind, v, sv) in enumerate(places):
             add(kind, v, sv, result[:, n * B : (n + 1) * B])
 
-    spread(14, [get(ea, i, HEAD) for i in range(6)], [(k, 0, s) for k in KINDS for s in (-1, 0)])
-    spread(15, [get(we, i) for i in range(6)], [(k, 3, s) for k in KINDS for s in (0, 1)])
-    spread(12, [get(tc, i) for i in range(4)], [(MID, 0, -1), (MID, 0, 0), (TW, 0, -1), (TW, 0, 0)])
-    spread(13, [get(tc, 4 + i) for i in range(4)], [(MID, 3, 0), (MID, 3, 1), (TW, 3, 0), (TW, 3, 1)])
+    spread(14, [get(ea, i, HEAD) for i in range(6)], [(k, 0, s) for k in SIDE for s in (-1, 0)])
+    spread(15, [get(we, i) for i in range(6)], [(k, 3, s) for k in SIDE for s in (0, 1)])
+    spread(12, [get(tc, i) for i in range(4)], [(TW, 0, -1), (TW, 0, 0), (MID, 0, -1), (MID, 0, 0)])
+    spread(13, [get(tc, 4 + i) for i in range(4)], [(TW, 3, 0), (TW, 3, 1), (MID, 3, 0), (MID, 3, 1)])
     spread(at(CR, 0, -1), [get(cc, i) for i in range(4)], [(MID, 0, -1), (MID, 0, 0), (CR, 0, -1), (CR, 0, 0)])
     spread(at(CR, 3, 1), [get(cc, 4 + i) for i in range(4)], [(MID, 3, 0), (MID, 3, 1), (CR, 3, 0), (CR, 3, 1)])
 
@@ -282,21 +300,21 @@
 
     messages = call(
         pack_kernel,
-        [(lines(12, HEAD), VMEM), (lines(6, HEAD), VMEM), (lines(24, HEAD), VMEM), (lines(12), VMEM), (lines(6), VMEM)],
+        [(lines(12, HEAD), ANY), (lines(6, HEAD), VMEM), (lines(24, HEAD), VMEM), (lines(12), ANY), (lines(6), ANY)],
         (x, pat),
         [ANY, ANY],
         10,
-        [vmem(4, 9, B, B), pltpu.SMEM(pat.shape, jnp.int32), sems(5)],
+        [vmem(4, 9, B, B), vmem(12 * B + HEAD, B), vmem(6 * B, B), pltpu.SMEM(pat.shape, jnp.int32), sems(16)],
     )
     c1, ea, tw, c2, we = [moved(m, s) for m, s in zip(messages, [cross, east, twin, cross, west])]
     c1m, _, twm = messages[:3]
     acc, lefts, pairs, few = call(
         near_kernel,
-        [(shape(36, B, B), FAR), (shape(32, B, B, dtype=BF16), FAR), (shape(B, B), VMEM), (lines(9, 2 * HEAD), VMEM)],
-        (alpha, beta, c1m, twm, tw),
+        [(shape(36, B, B), ANY), (shape(32, B, B, dtype=BF16), ANY), (shape(B, B), VMEM), (lines(9, 2 * HEAD), VMEM)],
+        (alpha, beta, far(c1m), twm, tw),
         [VMEM] * 5,
         14,
-        [vmem(n, B, B, dtype=BF16) for n in (24, 24, 24, 24, 36, 36)],
+        [vmem(36, B, B)] + [vmem(n, B, B, dtype=BF16) for n in (32, 24, 24, 24, 24, 36, 36)] + [sems(5)],
     )
     *corners, shares = call(
         middle_kernel,

time: 43.5 us -> 43.2 us (level)
  Pallas kernels: 15.2 us -> 14.6 us
    pallas_call x5, Pallas kernels: 15.2 us -> 14.6 us  [call(): pl.pallas_call(kernel, out_shape=[pltpu.HBM(o.shape, o.dtype) if s is ANY...]
  transfers between devices with their start and end apart: 8 -> 8, of which waited for: 2 -> 2; matrix products, arithmetic and copies ran while one was open for 0% -> 0% of each run, Pallas kernels for 27% -> 26%
where the time goes in v4:
time: 43.2 us; the launch traced here: 42.9 us
  starting transfers between devices  20.9 us (48%)
  Pallas kernels  14.6 us (34%)
  waiting for transfers between devices  5.38 us (12%)
  between operations  2 us (5%)
    pallas_call x5, Pallas kernels, call(): pl.pallas_call(kernel, out_shape=[pltpu.HBM(o.shape, o.dtype) if s is ANY...  14.6 us
    ppermute x7, starting transfers between devices, moved(): return lax.ppermute(message, AXES, pairs)  13.6 us
    all_to_all x1, starting transfers between devices, body(): gathered = lax.all_to_all(shares, AXES, 0, 0)  7.34 us
    all_to_all x1, waiting for transfers between devices, body(): gathered = lax.all_to_all(shares, AXES, 0, 0)  5 us
  transfers between devices with their start and end apart: 8, of which 2 were waited for; matrix products, arithmetic and copies ran while one was open for 0% of the time, Pallas kernels for 26%

profile of v4, /device:TPU:1, one launch (start us, length us, event | category | flops | bytes accessed | tf_op | source)
XLA Modules:
  0.0 42.9 jit_solution(17837776284629989298)
XLA Ops:
  0.6 2.7 %shard_map.59 = (f32[1544,128]{1,0:T(8,128)}, f32[776,128]{1,0:T(8,128)S(1)}, f32[3080,128]{1,0:T(8,128)S(1)}, f32[1536,128]{1,0:T(8,128)}, f32[768,128]{1,0:T(8,128)}) custom-call(f32[1,4,9,128,128]{4,3,2,1,0:T(8,128)} %x.1, s32[1,4,9]{2,1,0:T(4,128)} %pat.3), custom_call_target="tpu_custom_call" | custom-call | flops 1000 | bytes 1000 | tf_op jit(solution)/shard_map/pallas_call | solution.py:279
  3.3 1.5 %collective-permute-start = (f32[3080,128]{1,0:T(8,128)S(1)}, f32[3080,128]{1,0:T(8,128)}, u32[]{:S(2)}, u32[]{:S(2)}) collective-permute-start(f32[3080,128]{1,0:T(8,128)S(1)} %get-tuple-element.15.twm), channel_id=1, source_target_pairs={{0,16},{1,17},{2,18},{3,19},{4,20},{5,21},{6,22},{7,23},{8,24},{9,... | collective-permute-start | bytes 4730888 | tf_op jit(solution)/shard_map/ppermute | solution.py:275
  4.8 1.4 %collective-permute-start.1 = (f32[1544,128]{1,0:T(8,128)}, f32[1544,128]{1,0:T(8,128)S(1)}, u32[]{:S(2)}, u32[]{:S(2)}) collective-permute-start(f32[1544,128]{1,0:T(8,128)} %get-tuple-element.14.c1m), channel_id=1, source_target_pairs={{0,112},{1,113},{2,114},{3,115},{4,116},{5,117},{6,118},{7,119},{8... | collective-permute-start | bytes 2371592 | tf_op jit(solution)/shard_map/ppermute | solution.py:275
  6.2 1.2 %collective-permute-start.3 = (f32[776,128]{1,0:T(8,128)S(1)}, f32[776,128]{1,0:T(8,128)S(1)}, u32[]{:S(2)}, u32[]{:S(2)}) collective-permute-start(f32[776,128]{1,0:T(8,128)S(1)} %get-tuple-element.19), channel_id=1, source_target_pairs={{0,1},{1,2},{2,3},{3,4},{4,5},{5,6},{6,7},{7,8},{8,9},{9,10},{10,1... | collective-permute-start | bytes 1191944 | tf_op jit(solution)/shard_map/ppermute | solution.py:275
  7.4 4.7 %collective-permute-start.4 = (f32[768,128]{1,0:T(8,128)}, f32[768,128]{1,0:T(8,128)S(1)}, u32[]{:S(2)}, u32[]{:S(2)}) collective-permute-start(f32[768,128]{1,0:T(8,128)} %get-tuple-element.20), channel_id=1, source_target_pairs={{0,15},{1,0},{2,1},{3,2},{4,3},{5,4},{6,5},{7,6},{8,7},{9,8},{10,9... | collective-permute-start | bytes 1179656 | tf_op jit(solution)/shard_map/ppermute | solution.py:275
  12.1 0.8 %collective-permute-start.2 = (f32[1536,128]{1,0:T(8,128)}, f32[1536,128]{1,0:T(8,128)}, u32[]{:S(2)}, u32[]{:S(2)}) collective-permute-start(f32[1536,128]{1,0:T(8,128)} %get-tuple-element.18), channel_id=1, source_target_pairs={{0,112},{1,113},{2,114},{3,115},{4,116},{5,117},{6,118},{7,119},{8... | collective-permute-start | bytes 2359304 | tf_op jit(solution)/shard_map/ppermute | solution.py:275
  14.2 0.0 collective-permute-done.tw
  14.2 5.2 %shard_map.60 = (f32[36,128,128]{2,1,0:T(8,128)}, bf16[32,128,128]{2,1,0:T(8,128)(2,1)}, f32[128,128]{1,0:T(8,128)S(1)}, f32[1168,128]{1,0:T(8,128)S(1)}) custom-call(f32[1,1]{1,0:T(1,128)} %bitcast.7.alpha, f32[1,1]{1,0:T(1,128)} %bitcast.8.beta, f32[1544,128]{1,0:T(8,128)} %get-tuple-element.14.c1m, f32[3080,128]{1,0:T(8,128)S(1)} %get-tuple-element.15.twm, ...), custom_call_target="tpu_custom_call" | custom-call | flops 1000 | bytes 1000 | tf_op jit(solution)/shard_map/pallas_call | solution.py:279
  19.4 0.0 collective-permute-done.4.we
  19.4 0.4 collective-permute-done.3.ea
  19.8 0.0 collective-permute-done.1.c1
  19.8 1.4 %shard_map.61 = (f32[1024,128]{1,0:T(8,128)}, f32[1024,128]{1,0:T(8,128)}, f32[128,128]{1,0:T(8,128)}) custom-call(f32[1,1]{1,0:T(1,128)} %bitcast.9.beta, f32[128,128]{1,0:T(8,128)S(1)} %get-tuple-element.21.pairs, f32[1168,128]{1,0:T(8,128)S(1)} %get-tuple-element.22.few, f32[1544,128]{1,0:T(8,128)S(1)} %collective-permute-done.1.c1, ...), custom_call_target="tpu_custom_call" | custom-call | flops 1000 | bytes 1000 | tf_op jit(solution)/shard_map/pallas_call | solution.py:279
  21.2 2.7 %collective-permute-start.5 = (f32[1024,128]{1,0:T(8,128)}, f32[1024,128]{1,0:T(8,128)S(1)}, u32[]{:S(2)}, u32[]{:S(2)}) collective-permute-start(f32[1024,128]{1,0:T(8,128)} %get-tuple-element.23), channel_id=1, source_target_pairs={{0,112},{1,113},{2,114},{3,115},{4,116},{5,117},{6,118},{7,119},{8... | collective-permute-start | bytes 1572872 | tf_op jit(solution)/shard_map/ppermute | solution.py:275
  23.9 1.3 %collective-permute-start.6 = (f32[1024,128]{1,0:T(8,128)}, f32[1024,128]{1,0:T(8,128)S(1)}, u32[]{:S(2)}, u32[]{:S(2)}) collective-permute-start(f32[1024,128]{1,0:T(8,128)} %get-tuple-element.24), channel_id=1, source_target_pairs={{0,16},{1,17},{2,18},{3,19},{4,20},{5,21},{6,22},{7,23},{8,24},{9,... | collective-permute-start | bytes 1572872 | tf_op jit(solution)/shard_map/ppermute | solution.py:275
  25.2 7.3 %all-to-all-start = ((f32[128,1,128]{2,1,0:T(1,128)}), f32[128,1,128]{2,1,0:T(1,128)S(1)}, u32[]{:S(2)}, u32[]{:S(2)}) async-start(f32[128,1,128]{2,1,0:T(1,128)} %bitcast.3), calls=%async_computation | async-start | bytes 131072 | tf_op jit(solution)/shard_map/all_to_all | solution.py:327
  32.5 0.0 collective-permute-done.2.c2
  32.5 0.0 collective-permute-done.5.cc
  32.5 0.0 collective-permute-done.6.tc
  32.6 4.7 %shard_map.62.after = f32[1,4,9,128,128]{4,3,2,1,0:T(8,128)} custom-call(s32[1,4,9]{2,1,0:T(4,128)} %pat.3, bf16[32,128,128]{2,1,0:T(8,128)(2,1)} %get-tuple-element.16.lefts, f32[36,128,128]{2,1,0:T(8,128)} %get-tuple-element.17.acc, f32[1544,128]{1,0:T(8,128)S(1)} %collective-permute-done.1.c1, f32[1536,128]{1,0:T(8,128)} %collective-permute-done.2.c2, ...), custom_call_target="tpu_custom_call" | custom-call | flops 1000 | bytes 1000 | tf_op jit(solution)/shard_map/pallas_call | solution.py:279
  37.3 5.0 %all-to-all-done = f32[128,1,128]{2,1,0:T(1,128)S(1)} async-done(((f32[128,1,128]{2,1,0:T(1,128)}), f32[128,1,128]{2,1,0:T(1,128)S(1)}, u32[]{:S(2)}, u32[]{:S(2)}) %all-to-all-start) | async-done | bytes 65568 | tf_op jit(solution)/shard_map/all_to_all | solution.py:327
  42.3 0.6 %shard_map.63 = f32[1,1]{1,0:T(1,128)} custom-call(f32[128,128]{1,0:T(8,128)S(1)} %bitcast.10, f32[1,4,9,128,128]{4,3,2,1,0:T(8,128)} %shard_map.62.after), custom_call_target="tpu_custom_call" | custom-call | flops 1000 | bytes 1000 | tf_op jit(solution)/shard_map/pallas_call | solution.py:279
Async XLA Ops:
  3.3 10.9 %collective-permute-start = (f32[3080,128]{1,0:T(8,128)S(1)}, f32[3080,128]{1,0:T(8,128)}, u32[]{:S(2)}, u32[]{:S(2)}) collective-permute-start(f32[3080,128]{1,0:T(8,128)S(1)} %get-tuple-element.15.twm), channel_id=1, source_target_pairs={{0,16},{1,17},{2,18},{3,19},{4,20},{5,21},{6,22},{7,23},{8,24},{9,... | collective-permute-start | bytes 4730888 | tf_op jit(solution)/shard_map/ppermute | solution.py:275
  4.8 15.0 %collective-permute-start.1 = (f32[1544,128]{1,0:T(8,128)}, f32[1544,128]{1,0:T(8,128)S(1)}, u32[]{:S(2)}, u32[]{:S(2)}) collective-permute-start(f32[1544,128]{1,0:T(8,128)} %get-tuple-element.14.c1m), channel_id=1, source_target_pairs={{0,112},{1,113},{2,114},{3,115},{4,116},{5,117},{6,118},{7,119},{8... | collective-permute-start | bytes 2371592 | tf_op jit(solution)/shard_map/ppermute | solution.py:275
  6.2 13.6 %collective-permute-start.3 = (f32[776,128]{1,0:T(8,128)S(1)}, f32[776,128]{1,0:T(8,128)S(1)}, u32[]{:S(2)}, u32[]{:S(2)}) collective-permute-start(f32[776,128]{1,0:T(8,128)S(1)} %get-tuple-element.19), channel_id=1, source_target_pairs={{0,1},{1,2},{2,3},{3,4},{4,5},{5,6},{6,7},{7,8},{8,9},{9,10},{10,1... | collective-permute-start | bytes 1191944 | tf_op jit(solution)/shard_map/ppermute | solution.py:275
  7.4 12.0 %collective-permute-start.4 = (f32[768,128]{1,0:T(8,128)}, f32[768,128]{1,0:T(8,128)S(1)}, u32[]{:S(2)}, u32[]{:S(2)}) collective-permute-start(f32[768,128]{1,0:T(8,128)} %get-tuple-element.20), channel_id=1, source_target_pairs={{0,15},{1,0},{2,1},{3,2},{4,3},{5,4},{6,5},{7,6},{8,7},{9,8},{10,9... | collective-permute-start | bytes 1179656 | tf_op jit(solution)/shard_map/ppermute | solution.py:275
  12.1 20.4 %collective-permute-start.2 = (f32[1536,128]{1,0:T(8,128)}, f32[1536,128]{1,0:T(8,128)}, u32[]{:S(2)}, u32[]{:S(2)}) collective-permute-start(f32[1536,128]{1,0:T(8,128)} %get-tuple-element.18), channel_id=1, source_target_pairs={{0,112},{1,113},{2,114},{3,115},{4,116},{5,117},{6,118},{7,119},{8... | collective-permute-start | bytes 2359304 | tf_op jit(solution)/shard_map/ppermute | solution.py:275
  21.2 11.4 %collective-permute-start.5 = (f32[1024,128]{1,0:T(8,128)}, f32[1024,128]{1,0:T(8,128)S(1)}, u32[]{:S(2)}, u32[]{:S(2)}) collective-permute-start(f32[1024,128]{1,0:T(8,128)} %get-tuple-element.23), channel_id=1, source_target_pairs={{0,112},{1,113},{2,114},{3,115},{4,116},{5,117},{6,118},{7,119},{8... | collective-permute-start | bytes 1572872 | tf_op jit(solution)/shard_map/ppermute | solution.py:275
  23.9 8.7 %collective-permute-start.6 = (f32[1024,128]{1,0:T(8,128)}, f32[1024,128]{1,0:T(8,128)S(1)}, u32[]{:S(2)}, u32[]{:S(2)}) collective-permute-start(f32[1024,128]{1,0:T(8,128)} %get-tuple-element.24), channel_id=1, source_target_pairs={{0,16},{1,17},{2,18},{3,19},{4,20},{5,21},{6,22},{7,23},{8,24},{9,... | collective-permute-start | bytes 1572872 | tf_op jit(solution)/shard_map/ppermute | solution.py:275
  25.2 17.1 %all-to-all-start = ((f32[128,1,128]{2,1,0:T(1,128)}), f32[128,1,128]{2,1,0:T(1,128)S(1)}, u32[]{:S(2)}, u32[]{:S(2)}) async-start(f32[128,1,128]{2,1,0:T(1,128)} %bitcast.3), calls=%async_computation | async-start | bytes 131072 | tf_op jit(solution)/shard_map/all_to_all | solution.py:327

commit v5 on v4

--- a/solution.py
+++ b/solution.py
@@ -128,9 +128,9 @@
             for j in (-1, 0, 1):
                 i = at(kind, v, j)
                 block = own(kind, v, j)
-                total[v * 9 + kind * 3 + j + 1] = alpha[...] * block
+                total[v * 9 + kind * 3 + j + 1] = alpha[()] * block
                 rh[i], rl[i] = split(block)
-                high, low = split(beta[...] * block)
+                high, low = split(beta[()] * block)
                 if kind != CR:
                     lh[i - 12], ll[i - 12] = high, low
                 if i in sources:
@@ -174,9 +174,9 @@
     for v in range(3):
         listed.append((own(MID, v, 1) * (present(v) + present(v + 1)), mine(MID, v + 1, -1)))
         listed.append((own(TW, v + 1, -1) * (present(v + 1) + other(v)), theirs(TW, v, 1)))
-    value = beta[...] * dot3([[split(a) for a, _ in listed]], [[b] for _, b in listed])
+    value = beta[()] * dot3([[split(a) for a, _ in listed]], [[b] for _, b in listed])
     for v in range(4):
-        value += alpha[...] * own(MID, v, 0)
+        value += alpha[()] * own(MID, v, 0)
     pairs[...] = value
     few[pl.ds(0, HEAD), :] = twm[pl.ds(0, HEAD), :]
     few[pl.ds(HEAD, HEAD), :] = tw[pl.ds(0, HEAD), :]
@@ -204,7 +204,7 @@
     listed.append((west + own(0), get(ea, SIDE[MID] + 1, HEAD), kept(7)))
     listed.append((west + far(0), get(ea, SIDE[CR] + 1, HEAD), get(c1, 0, HEAD)))
     listed.append((west + few[pl.ds(HEAD, 1), :], get(ea, SIDE[TW] + 1, HEAD), kept(8)))
-    value = pairs[...] + beta[...] * dot3([[split(a * w) for w, a, _ in listed]], [[split(b)] for _, _, b in listed])
+    value = pairs[...] + beta[()] * dot3([[split(a * w) for w, a, _ in listed]], [[split(b)] for _, _, b in listed])
     rows = lax.broadcasted_iota(jnp.int32, (B, B), 0)
     columns = lax.broadcasted_iota(jnp.int32, (B, B), 1)
     line = jnp.sum(jnp.where(rows == columns, value, 0.0), axis=0, keepdims=True)
@@ -296,7 +296,6 @@
     twin = lambda r, c: (r ^ 1, c)
     east = lambda r, c: (r, c + 1)
     west = lambda r, c: (r, c - 1)
-    alpha, beta = alpha.reshape(1, 1), beta.reshape(1, 1)
 
     messages = call(
         pack_kernel,
@@ -312,7 +311,7 @@
         near_kernel,
         [(shape(36, B, B), ANY), (shape(32, B, B, dtype=BF16), ANY), (shape(B, B), VMEM), (lines(9, 2 * HEAD), VMEM)],
         (alpha, beta, far(c1m), twm, tw),
-        [VMEM] * 5,
+        [SMEM, SMEM] + [VMEM] * 3,
         14,
         [vmem(36, B, B)] + [vmem(n, B, B, dtype=BF16) for n in (32, 24, 24, 24, 24, 36, 36)] + [sems(5)],
     )
@@ -320,7 +319,7 @@
         middle_kernel,
         [(lines(8), VMEM), (lines(8), VMEM), (shape(B, B), VMEM)],
         (beta, pairs, few, c1, ea, we),
-        [VMEM] * 6,
+        [SMEM] + [VMEM] * 5,
         4,
     )
     cc, tc = moved(corners[0], cross), moved(corners[1], twin)

time: 43.2 us -> 43.2 us (level)
  no operation moved by 1% of the time
where the time goes in v5:
time: 43.2 us; the launch traced here: 42.9 us
  starting transfers between devices  20.9 us (48%)
  Pallas kernels  14.5 us (34%)
  waiting for transfers between devices  5.53 us (13%)
  between operations  2 us (5%)
    pallas_call x5, Pallas kernels, call(): pl.pallas_call(kernel, out_shape=[pltpu.HBM(o.shape, o.dtype) if s is ANY...  14.5 us
    ppermute x7, starting transfers between devices, moved(): return lax.ppermute(message, AXES, pairs)  13.4 us
    all_to_all x1, starting transfers between devices, body(): gathered = lax.all_to_all(shares, AXES, 0, 0)  7.5 us
    all_to_all x1, waiting for transfers between devices, body(): gathered = lax.all_to_all(shares, AXES, 0, 0)  5 us
  transfers between devices with their start and end apart: 8, of which 2 were waited for; matrix products, arithmetic and copies ran while one was open for 0% of the time, Pallas kernels for 26%

profile of v5, /device:TPU:1, one launch (start us, length us, event | category | flops | bytes accessed | tf_op | source)
XLA Modules:
  0.0 42.9 jit_solution(15272034861576045055)
XLA Ops:
  0.6 2.7 %shard_map.59 = (f32[1544,128]{1,0:T(8,128)}, f32[776,128]{1,0:T(8,128)S(1)}, f32[3080,128]{1,0:T(8,128)S(1)}, f32[1536,128]{1,0:T(8,128)}, f32[768,128]{1,0:T(8,128)}) custom-call(f32[1,4,9,128,128]{4,3,2,1,0:T(8,128)} %x.1, s32[1,4,9]{2,1,0:T(4,128)} %pat.3), custom_call_target="tpu_custom_call" | custom-call | flops 1000 | bytes 1000 | tf_op jit(solution)/shard_map/pallas_call | solution.py:279
  3.3 1.5 %collective-permute-start = (f32[3080,128]{1,0:T(8,128)S(1)}, f32[3080,128]{1,0:T(8,128)}, u32[]{:S(2)}, u32[]{:S(2)}) collective-permute-start(f32[3080,128]{1,0:T(8,128)S(1)} %get-tuple-element.15.twm), channel_id=1, source_target_pairs={{0,16},{1,17},{2,18},{3,19},{4,20},{5,21},{6,22},{7,23},{8,24},{9,... | collective-permute-start | bytes 4730888 | tf_op jit(solution)/shard_map/ppermute | solution.py:275
  4.8 1.4 %collective-permute-start.1 = (f32[1544,128]{1,0:T(8,128)}, f32[1544,128]{1,0:T(8,128)S(1)}, u32[]{:S(2)}, u32[]{:S(2)}) collective-permute-start(f32[1544,128]{1,0:T(8,128)} %get-tuple-element.14.c1m), channel_id=1, source_target_pairs={{0,112},{1,113},{2,114},{3,115},{4,116},{5,117},{6,118},{7,119},{8... | collective-permute-start | bytes 2371592 | tf_op jit(solution)/shard_map/ppermute | solution.py:275
  6.2 1.2 %collective-permute-start.3 = (f32[776,128]{1,0:T(8,128)S(1)}, f32[776,128]{1,0:T(8,128)S(1)}, u32[]{:S(2)}, u32[]{:S(2)}) collective-permute-start(f32[776,128]{1,0:T(8,128)S(1)} %get-tuple-element.19), channel_id=1, source_target_pairs={{0,1},{1,2},{2,3},{3,4},{4,5},{5,6},{6,7},{7,8},{8,9},{9,10},{10,1... | collective-permute-start | bytes 1191944 | tf_op jit(solution)/shard_map/ppermute | solution.py:275
  7.4 4.7 %collective-permute-start.4 = (f32[768,128]{1,0:T(8,128)}, f32[768,128]{1,0:T(8,128)S(1)}, u32[]{:S(2)}, u32[]{:S(2)}) collective-permute-start(f32[768,128]{1,0:T(8,128)} %get-tuple-element.20), channel_id=1, source_target_pairs={{0,15},{1,0},{2,1},{3,2},{4,3},{5,4},{6,5},{7,6},{8,7},{9,8},{10,9... | collective-permute-start | bytes 1179656 | tf_op jit(solution)/shard_map/ppermute | solution.py:275
  12.1 0.8 %collective-permute-start.2 = (f32[1536,128]{1,0:T(8,128)}, f32[1536,128]{1,0:T(8,128)}, u32[]{:S(2)}, u32[]{:S(2)}) collective-permute-start(f32[1536,128]{1,0:T(8,128)} %get-tuple-element.18), channel_id=1, source_target_pairs={{0,112},{1,113},{2,114},{3,115},{4,116},{5,117},{6,118},{7,119},{8... | collective-permute-start | bytes 2359304 | tf_op jit(solution)/shard_map/ppermute | solution.py:275
  14.2 0.0 collective-permute-done.tw
  14.2 5.1 %shard_map.60 = (f32[36,128,128]{2,1,0:T(8,128)}, bf16[32,128,128]{2,1,0:T(8,128)(2,1)}, f32[128,128]{1,0:T(8,128)S(1)}, f32[1168,128]{1,0:T(8,128)S(1)}) custom-call(f32[]{:T(128)S(6)} %copy.7.alpha, f32[]{:T(128)S(6)} %copy.8.beta, f32[1544,128]{1,0:T(8,128)} %get-tuple-element.14.c1m, f32[3080,128]{1,0:T(8,128)S(1)} %get-tuple-element.15.twm, ...), custom_call_target="tpu_custom_call" | custom-call | flops 1000 | bytes 1000 | tf_op jit(solution)/shard_map/pallas_call | solution.py:279
  19.3 0.0 collective-permute-done.4.we
  19.3 0.5 %collective-permute-done.3.ea = f32[776,128]{1,0:T(8,128)S(1)} collective-permute-done((f32[776,128]{1,0:T(8,128)S(1)}, f32[776,128]{1,0:T(8,128)S(1)}, u32[]{:S(2)}, u32[]{:S(2)}) %collective-permute-start.3) | collective-permute-done | bytes 397344 | tf_op jit(solution)/shard_map/ppermute | solution.py:275
  19.8 0.0 collective-permute-done.1.c1
  19.8 1.4 %shard_map.61 = (f32[1024,128]{1,0:T(8,128)}, f32[1024,128]{1,0:T(8,128)}, f32[128,128]{1,0:T(8,128)}) custom-call(f32[]{:T(128)S(6)} %copy.8.beta, f32[128,128]{1,0:T(8,128)S(1)} %get-tuple-element.21.pairs, f32[1168,128]{1,0:T(8,128)S(1)} %get-tuple-element.22.few, f32[1544,128]{1,0:T(8,128)S(1)} %collective-permute-done.1.c1, ...), custom_call_target="tpu_custom_call" | custom-call | flops 1000 | bytes 1000 | tf_op jit(solution)/shard_map/pallas_call | solution.py:279
  21.2 2.7 %collective-permute-start.5 = (f32[1024,128]{1,0:T(8,128)}, f32[1024,128]{1,0:T(8,128)S(1)}, u32[]{:S(2)}, u32[]{:S(2)}) collective-permute-start(f32[1024,128]{1,0:T(8,128)} %get-tuple-element.23), channel_id=1, source_target_pairs={{0,112},{1,113},{2,114},{3,115},{4,116},{5,117},{6,118},{7,119},{8... | collective-permute-start | bytes 1572872 | tf_op jit(solution)/shard_map/ppermute | solution.py:275
  23.9 1.2 %collective-permute-start.6 = (f32[1024,128]{1,0:T(8,128)}, f32[1024,128]{1,0:T(8,128)S(1)}, u32[]{:S(2)}, u32[]{:S(2)}) collective-permute-start(f32[1024,128]{1,0:T(8,128)} %get-tuple-element.24), channel_id=1, source_target_pairs={{0,16},{1,17},{2,18},{3,19},{4,20},{5,21},{6,22},{7,23},{8,24},{9,... | collective-permute-start | bytes 1572872 | tf_op jit(solution)/shard_map/ppermute | solution.py:275
  25.0 7.5 %all-to-all-start = ((f32[128,1,128]{2,1,0:T(1,128)}), f32[128,1,128]{2,1,0:T(1,128)S(1)}, u32[]{:S(2)}, u32[]{:S(2)}) async-start(f32[128,1,128]{2,1,0:T(1,128)} %bitcast.1), calls=%async_computation | async-start | bytes 131072 | tf_op jit(solution)/shard_map/all_to_all | solution.py:326
  32.5 0.0 collective-permute-done.2.c2
  32.5 0.0 collective-permute-done.5.cc
  32.5 0.0 collective-permute-done.6.tc
  32.6 4.7 %shard_map.62.after = f32[1,4,9,128,128]{4,3,2,1,0:T(8,128)} custom-call(s32[1,4,9]{2,1,0:T(4,128)} %pat.3, bf16[32,128,128]{2,1,0:T(8,128)(2,1)} %get-tuple-element.16.lefts, f32[36,128,128]{2,1,0:T(8,128)} %get-tuple-element.17.acc, f32[1544,128]{1,0:T(8,128)S(1)} %collective-permute-done.1.c1, f32[1536,128]{1,0:T(8,128)} %collective-permute-done.2.c2, ...), custom_call_target="tpu_custom_call" | custom-call | flops 1000 | bytes 1000 | tf_op jit(solution)/shard_map/pallas_call | solution.py:279
  37.3 5.0 %all-to-all-done = f32[128,1,128]{2,1,0:T(1,128)S(1)} async-done(((f32[128,1,128]{2,1,0:T(1,128)}), f32[128,1,128]{2,1,0:T(1,128)S(1)}, u32[]{:S(2)}, u32[]{:S(2)}) %all-to-all-start) | async-done | bytes 65568 | tf_op jit(solution)/shard_map/all_to_all | solution.py:326
  42.3 0.6 %shard_map.63 = f32[1,1]{1,0:T(1,128)} custom-call(f32[128,128]{1,0:T(8,128)S(1)} %bitcast.5, f32[1,4,9,128,128]{4,3,2,1,0:T(8,128)} %shard_map.62.after), custom_call_target="tpu_custom_call" | custom-call | flops 1000 | bytes 1000 | tf_op jit(solution)/shard_map/pallas_call | solution.py:279
Async XLA Ops:
  3.3 10.9 %collective-permute-start = (f32[3080,128]{1,0:T(8,128)S(1)}, f32[3080,128]{1,0:T(8,128)}, u32[]{:S(2)}, u32[]{:S(2)}) collective-permute-start(f32[3080,128]{1,0:T(8,128)S(1)} %get-tuple-element.15.twm), channel_id=1, source_target_pairs={{0,16},{1,17},{2,18},{3,19},{4,20},{5,21},{6,22},{7,23},{8,24},{9,... | collective-permute-start | bytes 4730888 | tf_op jit(solution)/shard_map/ppermute | solution.py:275
  4.8 15.0 %collective-permute-start.1 = (f32[1544,128]{1,0:T(8,128)}, f32[1544,128]{1,0:T(8,128)S(1)}, u32[]{:S(2)}, u32[]{:S(2)}) collective-permute-start(f32[1544,128]{1,0:T(8,128)} %get-tuple-element.14.c1m), channel_id=1, source_target_pairs={{0,112},{1,113},{2,114},{3,115},{4,116},{5,117},{6,118},{7,119},{8... | collective-permute-start | bytes 2371592 | tf_op jit(solution)/shard_map/ppermute | solution.py:275
  6.2 13.6 %collective-permute-start.3 = (f32[776,128]{1,0:T(8,128)S(1)}, f32[776,128]{1,0:T(8,128)S(1)}, u32[]{:S(2)}, u32[]{:S(2)}) collective-permute-start(f32[776,128]{1,0:T(8,128)S(1)} %get-tuple-element.19), channel_id=1, source_target_pairs={{0,1},{1,2},{2,3},{3,4},{4,5},{5,6},{6,7},{7,8},{8,9},{9,10},{10,1... | collective-permute-start | bytes 1191944 | tf_op jit(solution)/shard_map/ppermute | solution.py:275
  7.4 11.9 %collective-permute-start.4 = (f32[768,128]{1,0:T(8,128)}, f32[768,128]{1,0:T(8,128)S(1)}, u32[]{:S(2)}, u32[]{:S(2)}) collective-permute-start(f32[768,128]{1,0:T(8,128)} %get-tuple-element.20), channel_id=1, source_target_pairs={{0,15},{1,0},{2,1},{3,2},{4,3},{5,4},{6,5},{7,6},{8,7},{9,8},{10,9... | collective-permute-start | bytes 1179656 | tf_op jit(solution)/shard_map/ppermute | solution.py:275
  12.1 20.4 %collective-permute-start.2 = (f32[1536,128]{1,0:T(8,128)}, f32[1536,128]{1,0:T(8,128)}, u32[]{:S(2)}, u32[]{:S(2)}) collective-permute-start(f32[1536,128]{1,0:T(8,128)} %get-tuple-element.18), channel_id=1, source_target_pairs={{0,112},{1,113},{2,114},{3,115},{4,116},{5,117},{6,118},{7,119},{8... | collective-permute-start | bytes 2359304 | tf_op jit(solution)/shard_map/ppermute | solution.py:275
  21.2 11.4 %collective-permute-start.5 = (f32[1024,128]{1,0:T(8,128)}, f32[1024,128]{1,0:T(8,128)S(1)}, u32[]{:S(2)}, u32[]{:S(2)}) collective-permute-start(f32[1024,128]{1,0:T(8,128)} %get-tuple-element.23), channel_id=1, source_target_pairs={{0,112},{1,113},{2,114},{3,115},{4,116},{5,117},{6,118},{7,119},{8... | collective-permute-start | bytes 1572872 | tf_op jit(solution)/shard_map/ppermute | solution.py:275
  23.9 8.7 %collective-permute-start.6 = (f32[1024,128]{1,0:T(8,128)}, f32[1024,128]{1,0:T(8,128)S(1)}, u32[]{:S(2)}, u32[]{:S(2)}) collective-permute-start(f32[1024,128]{1,0:T(8,128)} %get-tuple-element.24), channel_id=1, source_target_pairs={{0,16},{1,17},{2,18},{3,19},{4,20},{5,21},{6,22},{7,23},{8,24},{9,... | collective-permute-start | bytes 1572872 | tf_op jit(solution)/shard_map/ppermute | solution.py:275
  25.0 17.3 %all-to-all-start = ((f32[128,1,128]{2,1,0:T(1,128)}), f32[128,1,128]{2,1,0:T(1,128)S(1)}, u32[]{:S(2)}, u32[]{:S(2)}) async-start(f32[128,1,128]{2,1,0:T(1,128)} %bitcast.1), calls=%async_computation | async-start | bytes 131072 | tf_op jit(solution)/shard_map/all_to_all | solution.py:326

commit v6 on v5

--- a/solution.py
+++ b/solution.py
@@ -69,7 +69,7 @@
         return copy
 
 
-def pack_kernel(x, pat, c1, ea, tw, c2, we, stage, toward, sides, table, sems):
+def pack_kernel(x, pat, c1, ea, tw, c2, we, stage, toward, westward, table, sems):
     odd = lax.rem(lax.axis_index("row"), 2)
     dma = Copies(sems)
     table_load = dma.start(pat, table)
@@ -102,9 +102,9 @@
                 if v == 3 and j >= 0:
                     put(ea, SIDE[kind] + j, block, HEAD)
                 if v == 0 and j < 1:
-                    put(sides, SIDE[kind] + j + 1, block)
+                    put(westward, SIDE[kind] + j + 1, block)
             if kind == TW and v == 0:
-                stores.append(dma.start(sides, we))
+                stores.append(dma.start(westward, we))
         if kind == CR:
             stores.append(dma.start(toward, c1))
         if kind == MID:
@@ -187,11 +187,7 @@
         copy.wait()
 
 
-def middle_kernel(beta, pairs, few, c1, ea, we, cc, tc, shares):
-    for out, kind, head in ((cc, CR, 0), (tc, MID, 0)):
-        for i in range(4):
-            put(out, i, get(ea, SIDE[kind] + i, HEAD), head)
-            put(out, 4 + i, get(we, SIDE[kind] + i), head)
+def middle_kernel(beta, pairs, few, c1, ea, we, cc, tc, shares, lines, sem):
     own = lambda v: few[pl.ds(v, 1), :]
     far = lambda v: c1[pl.ds(v, 1), :]
     west = ea[pl.ds(3, 1), :]
@@ -208,14 +204,21 @@
     rows = lax.broadcasted_iota(jnp.int32, (B, B), 0)
     columns = lax.broadcasted_iota(jnp.int32, (B, B), 1)
     line = jnp.sum(jnp.where(rows == columns, value, 0.0), axis=0, keepdims=True)
-    shares[...] = jnp.broadcast_to(line, (B, B))
+    lines[...] = jnp.broadcast_to(line, (B, B))
+    copy = pltpu.make_async_copy(lines, shares, sem)
+    copy.start()
+    for out, kind in ((cc, CR), (tc, MID)):
+        for i in range(4):
+            put(out, i, get(ea, SIDE[kind] + i, HEAD))
+            put(out, 4 + i, get(we, SIDE[kind] + i))
+    copy.wait()
 
 
 def sum_kernel(scale, shares, after, out):
     out[0, 0] = jnp.sum(shares[...]) * scale
 
 
-def final_kernel(pat, lefts, acc, c1, c2, ea, we, cc, tc, out, total, stage, sems):
+def final_kernel(pat, lefts, acc, c1, c2, ccm, tcm, cc, tc, out, total, stage, sems):
     odd = lax.rem(lax.axis_index("row"), 2)
     dma = Copies(sems)
     left = lambda i: (lefts[i], lefts[16 + i])
@@ -231,8 +234,8 @@
         for n, (kind, v, sv) in enumerate(places):
             add(kind, v, sv, result[:, n * B : (n + 1) * B])
 
-    spread(14, [get(ea, i, HEAD) for i in range(6)], [(k, 0, s) for k in SIDE for s in (-1, 0)])
-    spread(15, [get(we, i) for i in range(6)], [(k, 3, s) for k in SIDE for s in (0, 1)])
+    spread(14, [get(ccm, i) for i in range(4)] + [get(tcm, i) for i in (2, 3)], [(k, 0, s) for k in SIDE for s in (-1, 0)])
+    spread(15, [get(ccm, 4 + i) for i in range(4)] + [get(tcm, i) for i in (6, 7)], [(k, 3, s) for k in SIDE for s in (0, 1)])
     spread(12, [get(tc, i) for i in range(4)], [(TW, 0, -1), (TW, 0, 0), (MID, 0, -1), (MID, 0, 0)])
     spread(13, [get(tc, 4 + i) for i in range(4)], [(TW, 3, 0), (TW, 3, 1), (MID, 3, 0), (MID, 3, 1)])
     spread(at(CR, 0, -1), [get(cc, i) for i in range(4)], [(MID, 0, -1), (MID, 0, 0), (CR, 0, -1), (CR, 0, 0)])
@@ -303,7 +306,7 @@
         (x, pat),
         [ANY, ANY],
         10,
-        [vmem(4, 9, B, B), vmem(12 * B + HEAD, B), vmem(6 * B, B), pltpu.SMEM(pat.shape, jnp.int32), sems(16)],
+        [vmem(4, 9, B, B), vmem(12 * B + HEAD, B), vmem(6 * B, B), pltpu.SMEM(pat.shape, jnp.int32), sems(17)],
     )
     c1, ea, tw, c2, we = [moved(m, s) for m, s in zip(messages, [cross, east, twin, cross, west])]
     c1m, _, twm = messages[:3]
@@ -317,17 +320,18 @@
     )
     *corners, shares = call(
         middle_kernel,
-        [(lines(8), VMEM), (lines(8), VMEM), (shape(B, B), VMEM)],
+        [(lines(8), VMEM), (lines(8), VMEM), (shape(B, B), ANY)],
         (beta, pairs, few, c1, ea, we),
         [SMEM] + [VMEM] * 5,
         4,
+        [vmem(B, B), pltpu.SemaphoreType.DMA(())],
     )
     cc, tc = moved(corners[0], cross), moved(corners[1], twin)
     gathered = lax.all_to_all(shares, AXES, 0, 0)
     (updated,) = call(
         final_kernel,
         [(shape(*x.shape), ANY)],
-        (pat, far(lefts), far(acc), c1, c2, ea, we, cc, tc),
+        (pat, far(lefts), far(acc), c1, far(c2), *corners, cc, tc),
         [SMEM] + [VMEM] * 8,
         14,
         [vmem(36, B, B), vmem(4, 9, B, B), sems(4)],

time: 43.2 us -> 42.9 us (level)
  transfers between devices with their start and end apart: 8 -> 8, of which waited for: 2 -> 2; matrix products, arithmetic and copies ran while one was open for 0% -> 0% of each run, Pallas kernels for 26% -> 25%
where the time goes in v6:
time: 42.9 us; the launch traced here: 42.7 us
  starting transfers between devices  21 us (49%)
  Pallas kernels  14.2 us (33%)
  waiting for transfers between devices  5.52 us (13%)
  between operations  2.01 us (5%)
    pallas_call x5, Pallas kernels, call(): pl.pallas_call(kernel, out_shape=[pltpu.HBM(o.shape, o.dtype) if s is ANY...  14.2 us
    ppermute x7, starting transfers between devices, moved(): return lax.ppermute(message, AXES, pairs)  13.5 us
    all_to_all x1, starting transfers between devices, body(): gathered = lax.all_to_all(shares, AXES, 0, 0)  7.49 us
    all_to_all x1, waiting for transfers between devices, body(): gathered = lax.all_to_all(shares, AXES, 0, 0)  5 us
  transfers between devices with their start and end apart: 8, of which 2 were waited for; matrix products, arithmetic and copies ran while one was open for 0% of the time, Pallas kernels for 25%

profile of v6, /device:TPU:1, one launch (start us, length us, event | category | flops | bytes accessed | tf_op | source)
XLA Modules:
  0.0 42.7 jit_solution(606702384760374445)
XLA Ops:
  0.6 2.7 %shard_map.59 = (f32[1544,128]{1,0:T(8,128)}, f32[776,128]{1,0:T(8,128)S(1)}, f32[3080,128]{1,0:T(8,128)S(1)}, f32[1536,128]{1,0:T(8,128)}, f32[768,128]{1,0:T(8,128)}) custom-call(f32[1,4,9,128,128]{4,3,2,1,0:T(8,128)} %x.1, s32[1,4,9]{2,1,0:T(4,128)} %pat.3), custom_call_target="tpu_custom_call" | custom-call | flops 1000 | bytes 1000 | tf_op jit(solution)/shard_map/pallas_call | solution.py:282
  3.3 1.5 %collective-permute-start = (f32[3080,128]{1,0:T(8,128)S(1)}, f32[3080,128]{1,0:T(8,128)}, u32[]{:S(2)}, u32[]{:S(2)}) collective-permute-start(f32[3080,128]{1,0:T(8,128)S(1)} %get-tuple-element.15.twm), channel_id=1, source_target_pairs={{0,16},{1,17},{2,18},{3,19},{4,20},{5,21},{6,22},{7,23},{8,24},{9,... | collective-permute-start | bytes 4730888 | tf_op jit(solution)/shard_map/ppermute | solution.py:278
  4.8 1.4 %collective-permute-start.1 = (f32[1544,128]{1,0:T(8,128)}, f32[1544,128]{1,0:T(8,128)S(1)}, u32[]{:S(2)}, u32[]{:S(2)}) collective-permute-start(f32[1544,128]{1,0:T(8,128)} %get-tuple-element.14.c1m), channel_id=1, source_target_pairs={{0,112},{1,113},{2,114},{3,115},{4,116},{5,117},{6,118},{7,119},{8... | collective-permute-start | bytes 2371592 | tf_op jit(solution)/shard_map/ppermute | solution.py:278
  6.2 1.2 %collective-permute-start.3 = (f32[776,128]{1,0:T(8,128)S(1)}, f32[776,128]{1,0:T(8,128)S(1)}, u32[]{:S(2)}, u32[]{:S(2)}) collective-permute-start(f32[776,128]{1,0:T(8,128)S(1)} %get-tuple-element.21), channel_id=1, source_target_pairs={{0,1},{1,2},{2,3},{3,4},{4,5},{5,6},{6,7},{7,8},{8,9},{9,10},{10,1... | collective-permute-start | bytes 1191944 | tf_op jit(solution)/shard_map/ppermute | solution.py:278
  7.4 4.7 %collective-permute-start.4 = (f32[768,128]{1,0:T(8,128)}, f32[768,128]{1,0:T(8,128)S(1)}, u32[]{:S(2)}, u32[]{:S(2)}) collective-permute-start(f32[768,128]{1,0:T(8,128)} %get-tuple-element.22), channel_id=1, source_target_pairs={{0,15},{1,0},{2,1},{3,2},{4,3},{5,4},{6,5},{7,6},{8,7},{9,8},{10,9... | collective-permute-start | bytes 1179656 | tf_op jit(solution)/shard_map/ppermute | solution.py:278
  12.1 0.8 %collective-permute-start.2 = (f32[1536,128]{1,0:T(8,128)}, f32[1536,128]{1,0:T(8,128)}, u32[]{:S(2)}, u32[]{:S(2)}) collective-permute-start(f32[1536,128]{1,0:T(8,128)} %get-tuple-element.18), channel_id=1, source_target_pairs={{0,112},{1,113},{2,114},{3,115},{4,116},{5,117},{6,118},{7,119},{8... | collective-permute-start | bytes 2359304 | tf_op jit(solution)/shard_map/ppermute | solution.py:278
  14.2 0.0 collective-permute-done.tw
  14.2 5.1 %shard_map.60 = (f32[36,128,128]{2,1,0:T(8,128)}, bf16[32,128,128]{2,1,0:T(8,128)(2,1)}, f32[128,128]{1,0:T(8,128)S(1)}, f32[1168,128]{1,0:T(8,128)S(1)}) custom-call(f32[]{:T(128)S(6)} %copy.7.alpha, f32[]{:T(128)S(6)} %copy.8.beta, f32[1544,128]{1,0:T(8,128)} %get-tuple-element.14.c1m, f32[3080,128]{1,0:T(8,128)S(1)} %get-tuple-element.15.twm, ...), custom_call_target="tpu_custom_call" | custom-call | flops 1000 | bytes 1000 | tf_op jit(solution)/shard_map/pallas_call | solution.py:282
  19.3 0.0 collective-permute-done.4.we
  19.3 0.5 %collective-permute-done.3.ea = f32[776,128]{1,0:T(8,128)S(1)} collective-permute-done((f32[776,128]{1,0:T(8,128)S(1)}, f32[776,128]{1,0:T(8,128)S(1)}, u32[]{:S(2)}, u32[]{:S(2)}) %collective-permute-start.3) | collective-permute-done | bytes 397344 | tf_op jit(solution)/shard_map/ppermute | solution.py:278
  19.8 0.0 collective-permute-done.1.c1
  19.8 1.1 %shard_map.61 = (f32[1024,128]{1,0:T(8,128)S(1)}, f32[1024,128]{1,0:T(8,128)S(1)}, f32[128,128]{1,0:T(8,128)}) custom-call(f32[]{:T(128)S(6)} %copy.8.beta, f32[128,128]{1,0:T(8,128)S(1)} %get-tuple-element.19.pairs, f32[1168,128]{1,0:T(8,128)S(1)} %get-tuple-element.20.few, f32[1544,128]{1,0:T(8,128)S(1)} %collective-permute-done.1.c1, ...), custom_call_target="tpu_custom_call" | custom-call | flops 1000 | bytes 1000 | tf_op jit(solution)/shard_map/pallas_call | solution.py:282
  20.9 2.8 %collective-permute-start.5 = (f32[1024,128]{1,0:T(8,128)S(1)}, f32[1024,128]{1,0:T(8,128)S(1)}, u32[]{:S(2)}, u32[]{:S(2)}) collective-permute-start(f32[1024,128]{1,0:T(8,128)S(1)} %get-tuple-element.23.ccm), channel_id=1, source_target_pairs={{0,112},{1,113},{2,114},{3,115},{4,116},{5,117},{6,118},{7,119},{8... | collective-permute-start | bytes 1572872 | tf_op jit(solution)/shard_map/ppermute | solution.py:278
  23.6 1.2 %collective-permute-start.6 = (f32[1024,128]{1,0:T(8,128)S(1)}, f32[1024,128]{1,0:T(8,128)S(1)}, u32[]{:S(2)}, u32[]{:S(2)}) collective-permute-start(f32[1024,128]{1,0:T(8,128)S(1)} %get-tuple-element.24.tcm), channel_id=1, source_target_pairs={{0,16},{1,17},{2,18},{3,19},{4,20},{5,21},{6,22},{7,23},{8,24},{9,... | collective-permute-start | bytes 1572872 | tf_op jit(solution)/shard_map/ppermute | solution.py:278
  24.8 7.5 %all-to-all-start = ((f32[128,1,128]{2,1,0:T(1,128)}), f32[128,1,128]{2,1,0:T(1,128)S(1)}, u32[]{:S(2)}, u32[]{:S(2)}) async-start(f32[128,1,128]{2,1,0:T(1,128)} %bitcast.6), calls=%async_computation | async-start | bytes 131072 | tf_op jit(solution)/shard_map/all_to_all | solution.py:330
  32.3 0.0 collective-permute-done.2.c2
  32.3 0.0 collective-permute-done.5.cc
  32.3 0.0 collective-permute-done.6.tc
  32.3 4.7 %shard_map.62.after = f32[1,4,9,128,128]{4,3,2,1,0:T(8,128)} custom-call(s32[1,4,9]{2,1,0:T(4,128)} %pat.3, bf16[32,128,128]{2,1,0:T(8,128)(2,1)} %get-tuple-element.16.lefts, f32[36,128,128]{2,1,0:T(8,128)} %get-tuple-element.17.acc, f32[1544,128]{1,0:T(8,128)S(1)} %collective-permute-done.1.c1, f32[1536,128]{1,0:T(8,128)} %collective-permute-done.2.c2, ...), custom_call_target="tpu_custom_call" | custom-call | flops 1000 | bytes 1000 | tf_op jit(solution)/shard_map/pallas_call | solution.py:282
  37.1 5.0 %all-to-all-done = f32[128,1,128]{2,1,0:T(1,128)S(1)} async-done(((f32[128,1,128]{2,1,0:T(1,128)}), f32[128,1,128]{2,1,0:T(1,128)S(1)}, u32[]{:S(2)}, u32[]{:S(2)}) %all-to-all-start) | async-done | bytes 65568 | tf_op jit(solution)/shard_map/all_to_all | solution.py:330
  42.1 0.6 %shard_map.63 = f32[1,1]{1,0:T(1,128)} custom-call(f32[128,128]{1,0:T(8,128)S(1)} %bitcast.5, f32[1,4,9,128,128]{4,3,2,1,0:T(8,128)} %shard_map.62.after), custom_call_target="tpu_custom_call" | custom-call | flops 1000 | bytes 1000 | tf_op jit(solution)/shard_map/pallas_call | solution.py:282
Async XLA Ops:
  3.3 10.9 %collective-permute-start = (f32[3080,128]{1,0:T(8,128)S(1)}, f32[3080,128]{1,0:T(8,128)}, u32[]{:S(2)}, u32[]{:S(2)}) collective-permute-start(f32[3080,128]{1,0:T(8,128)S(1)} %get-tuple-element.15.twm), channel_id=1, source_target_pairs={{0,16},{1,17},{2,18},{3,19},{4,20},{5,21},{6,22},{7,23},{8,24},{9,... | collective-permute-start | bytes 4730888 | tf_op jit(solution)/shard_map/ppermute | solution.py:278
  4.8 15.0 %collective-permute-start.1 = (f32[1544,128]{1,0:T(8,128)}, f32[1544,128]{1,0:T(8,128)S(1)}, u32[]{:S(2)}, u32[]{:S(2)}) collective-permute-start(f32[1544,128]{1,0:T(8,128)} %get-tuple-element.14.c1m), channel_id=1, source_target_pairs={{0,112},{1,113},{2,114},{3,115},{4,116},{5,117},{6,118},{7,119},{8... | collective-permute-start | bytes 2371592 | tf_op jit(solution)/shard_map/ppermute | solution.py:278
  6.2 13.6 %collective-permute-start.3 = (f32[776,128]{1,0:T(8,128)S(1)}, f32[776,128]{1,0:T(8,128)S(1)}, u32[]{:S(2)}, u32[]{:S(2)}) collective-permute-start(f32[776,128]{1,0:T(8,128)S(1)} %get-tuple-element.21), channel_id=1, source_target_pairs={{0,1},{1,2},{2,3},{3,4},{4,5},{5,6},{6,7},{7,8},{8,9},{9,10},{10,1... | collective-permute-start | bytes 1191944 | tf_op jit(solution)/shard_map/ppermute | solution.py:278
  7.4 11.9 %collective-permute-start.4 = (f32[768,128]{1,0:T(8,128)}, f32[768,128]{1,0:T(8,128)S(1)}, u32[]{:S(2)}, u32[]{:S(2)}) collective-permute-start(f32[768,128]{1,0:T(8,128)} %get-tuple-element.22), channel_id=1, source_target_pairs={{0,15},{1,0},{2,1},{3,2},{4,3},{5,4},{6,5},{7,6},{8,7},{9,8},{10,9... | collective-permute-start | bytes 1179656 | tf_op jit(solution)/shard_map/ppermute | solution.py:278
  12.1 20.2 %collective-permute-start.2 = (f32[1536,128]{1,0:T(8,128)}, f32[1536,128]{1,0:T(8,128)}, u32[]{:S(2)}, u32[]{:S(2)}) collective-permute-start(f32[1536,128]{1,0:T(8,128)} %get-tuple-element.18), channel_id=1, source_target_pairs={{0,112},{1,113},{2,114},{3,115},{4,116},{5,117},{6,118},{7,119},{8... | collective-permute-start | bytes 2359304 | tf_op jit(solution)/shard_map/ppermute | solution.py:278
  20.9 11.4 %collective-permute-start.5 = (f32[1024,128]{1,0:T(8,128)S(1)}, f32[1024,128]{1,0:T(8,128)S(1)}, u32[]{:S(2)}, u32[]{:S(2)}) collective-permute-start(f32[1024,128]{1,0:T(8,128)S(1)} %get-tuple-element.23.ccm), channel_id=1, source_target_pairs={{0,112},{1,113},{2,114},{3,115},{4,116},{5,117},{6,118},{7,119},{8... | collective-permute-start | bytes 1572872 | tf_op jit(solution)/shard_map/ppermute | solution.py:278
  23.6 8.7 %collective-permute-start.6 = (f32[1024,128]{1,0:T(8,128)S(1)}, f32[1024,128]{1,0:T(8,128)S(1)}, u32[]{:S(2)}, u32[]{:S(2)}) collective-permute-start(f32[1024,128]{1,0:T(8,128)S(1)} %get-tuple-element.24.tcm), channel_id=1, source_target_pairs={{0,16},{1,17},{2,18},{3,19},{4,20},{5,21},{6,22},{7,23},{8,24},{9,... | collective-permute-start | bytes 1572872 | tf_op jit(solution)/shard_map/ppermute | solution.py:278
  24.8 17.3 %all-to-all-start = ((f32[128,1,128]{2,1,0:T(1,128)}), f32[128,1,128]{2,1,0:T(1,128)S(1)}, u32[]{:S(2)}, u32[]{:S(2)}) async-start(f32[128,1,128]{2,1,0:T(1,128)} %bitcast.6), calls=%async_computation | async-start | bytes 131072 | tf_op jit(solution)/shard_map/all_to_all | solution.py:330

commit v7 on v6

--- a/solution.py
+++ b/solution.py
@@ -73,12 +73,11 @@
     odd = lax.rem(lax.axis_index("row"), 2)
     dma = Copies(sems)
     table_load = dma.start(pat, table)
-    order = (0, 3, 1, 2)
+    order = [(CR, v) for v in (0, 3, 1, 2)] + [(k, v) for v in (0, 3) for k in (MID, TW)] + [(k, v) for k in (MID, TW) for v in (1, 2)]
     loads = {}
-    for kind in (CR, MID, TW):
+    for kind, v in order:
         slots = pl.ds(slot(kind, -1, odd), 3)
-        for v in order:
-            loads[kind, v] = dma.start(x.at[0, v, slots], stage.at[v, slots])
+        loads[kind, v] = dma.start(x.at[0, v, slots], stage.at[v, slots])
     table_load.wait()
     rows = lax.broadcasted_iota(jnp.int32, (HEAD, B), 0)
     present = jnp.zeros((HEAD, B), F32)
@@ -88,27 +87,26 @@
         ref[pl.ds(0, HEAD), :] = present
 
     stores = []
-    for kind in (CR, MID, TW):
-        for v in order:
-            loads[kind, v].wait()
-            for j in (-1, 0, 1):
-                s = slot(kind, j, odd)
-                block = stage[v, s] * weight(table, v, s)
-                i = at(kind, v, j)
-                if kind == CR:
-                    put(toward, i, block, HEAD)
-                else:
-                    put(tw, i - 12, block, HEAD)
-                if v == 3 and j >= 0:
-                    put(ea, SIDE[kind] + j, block, HEAD)
-                if v == 0 and j < 1:
-                    put(westward, SIDE[kind] + j + 1, block)
-            if kind == TW and v == 0:
-                stores.append(dma.start(westward, we))
-        if kind == CR:
+    for kind, v in order:
+        loads[kind, v].wait()
+        for j in (-1, 0, 1):
+            s = slot(kind, j, odd)
+            block = stage[v, s] * weight(table, v, s)
+            i = at(kind, v, j)
+            if kind == CR:
+                put(toward, i, block, HEAD)
+            else:
+                put(tw, i - 12, block, HEAD)
+            if v == 3 and j >= 0:
+                put(ea, SIDE[kind] + j, block, HEAD)
+            if v == 0 and j < 1:
+                put(westward, SIDE[kind] + j + 1, block)
+        if (kind, v) == (CR, 2):
             stores.append(dma.start(toward, c1))
-        if kind == MID:
+        if (kind, v) == (MID, 2):
             stores.append(dma.start(tw.at[pl.ds(HEAD + 12 * B, 12 * B), :], c2))
+        if v == 0 and all((k, 0) in order[: order.index((kind, v)) + 1] for k in KINDS):
+            stores.append(dma.start(westward, we))
     for copy in stores:
         copy.wait()
 

time: 42.9 us -> 43 us (level)
  no operation moved by 1% of the time
where the time goes in v7:
time: 43 us; the launch traced here: 42.7 us
  starting transfers between devices  21 us (49%)
  Pallas kernels  14.2 us (33%)
  waiting for transfers between devices  5.52 us (13%)
  between operations  2.01 us (5%)
    pallas_call x5, Pallas kernels, call(): pl.pallas_call(kernel, out_shape=[pltpu.HBM(o.shape, o.dtype) if s is ANY...  14.2 us
    ppermute x7, starting transfers between devices, moved(): return lax.ppermute(message, AXES, pairs)  13.5 us
    all_to_all x1, starting transfers between devices, body(): gathered = lax.all_to_all(shares, AXES, 0, 0)  7.48 us
    all_to_all x1, waiting for transfers between devices, body(): gathered = lax.all_to_all(shares, AXES, 0, 0)  5 us
  transfers between devices with their start and end apart: 8, of which 2 were waited for; matrix products, arithmetic and copies ran while one was open for 0% of the time, Pallas kernels for 25%

profile of v7, /device:TPU:1, one launch (start us, length us, event | category | flops | bytes accessed | tf_op | source)
XLA Modules:
  0.0 42.7 jit_solution(11245599082158064469)
XLA Ops:
  0.6 2.7 %shard_map.59 = (f32[1544,128]{1,0:T(8,128)}, f32[776,128]{1,0:T(8,128)S(1)}, f32[3080,128]{1,0:T(8,128)S(1)}, f32[1536,128]{1,0:T(8,128)}, f32[768,128]{1,0:T(8,128)}) custom-call(f32[1,4,9,128,128]{4,3,2,1,0:T(8,128)} %x.1, s32[1,4,9]{2,1,0:T(4,128)} %pat.3), custom_call_target="tpu_custom_call" | custom-call | flops 1000 | bytes 1000 | tf_op jit(solution)/shard_map/pallas_call | solution.py:280
  3.3 1.5 %collective-permute-start = (f32[3080,128]{1,0:T(8,128)S(1)}, f32[3080,128]{1,0:T(8,128)}, u32[]{:S(2)}, u32[]{:S(2)}) collective-permute-start(f32[3080,128]{1,0:T(8,128)S(1)} %get-tuple-element.15.twm), channel_id=1, source_target_pairs={{0,16},{1,17},{2,18},{3,19},{4,20},{5,21},{6,22},{7,23},{8,24},{9,... | collective-permute-start | bytes 4730888 | tf_op jit(solution)/shard_map/ppermute | solution.py:276
  4.8 1.4 %collective-permute-start.1 = (f32[1544,128]{1,0:T(8,128)}, f32[1544,128]{1,0:T(8,128)S(1)}, u32[]{:S(2)}, u32[]{:S(2)}) collective-permute-start(f32[1544,128]{1,0:T(8,128)} %get-tuple-element.14.c1m), channel_id=1, source_target_pairs={{0,112},{1,113},{2,114},{3,115},{4,116},{5,117},{6,118},{7,119},{8... | collective-permute-start | bytes 2371592 | tf_op jit(solution)/shard_map/ppermute | solution.py:276
  6.2 1.2 %collective-permute-start.3 = (f32[776,128]{1,0:T(8,128)S(1)}, f32[776,128]{1,0:T(8,128)S(1)}, u32[]{:S(2)}, u32[]{:S(2)}) collective-permute-start(f32[776,128]{1,0:T(8,128)S(1)} %get-tuple-element.21), channel_id=1, source_target_pairs={{0,1},{1,2},{2,3},{3,4},{4,5},{5,6},{6,7},{7,8},{8,9},{9,10},{10,1... | collective-permute-start | bytes 1191944 | tf_op jit(solution)/shard_map/ppermute | solution.py:276
  7.4 4.7 %collective-permute-start.4 = (f32[768,128]{1,0:T(8,128)}, f32[768,128]{1,0:T(8,128)S(1)}, u32[]{:S(2)}, u32[]{:S(2)}) collective-permute-start(f32[768,128]{1,0:T(8,128)} %get-tuple-element.22), channel_id=1, source_target_pairs={{0,15},{1,0},{2,1},{3,2},{4,3},{5,4},{6,5},{7,6},{8,7},{9,8},{10,9... | collective-permute-start | bytes 1179656 | tf_op jit(solution)/shard_map/ppermute | solution.py:276
  12.1 0.8 %collective-permute-start.2 = (f32[1536,128]{1,0:T(8,128)}, f32[1536,128]{1,0:T(8,128)}, u32[]{:S(2)}, u32[]{:S(2)}) collective-permute-start(f32[1536,128]{1,0:T(8,128)} %get-tuple-element.18), channel_id=1, source_target_pairs={{0,112},{1,113},{2,114},{3,115},{4,116},{5,117},{6,118},{7,119},{8... | collective-permute-start | bytes 2359304 | tf_op jit(solution)/shard_map/ppermute | solution.py:276
  14.2 0.0 collective-permute-done.tw
  14.2 5.1 %shard_map.60 = (f32[36,128,128]{2,1,0:T(8,128)}, bf16[32,128,128]{2,1,0:T(8,128)(2,1)}, f32[128,128]{1,0:T(8,128)S(1)}, f32[1168,128]{1,0:T(8,128)S(1)}) custom-call(f32[]{:T(128)S(6)} %copy.7.alpha, f32[]{:T(128)S(6)} %copy.8.beta, f32[1544,128]{1,0:T(8,128)} %get-tuple-element.14.c1m, f32[3080,128]{1,0:T(8,128)S(1)} %get-tuple-element.15.twm, ...), custom_call_target="tpu_custom_call" | custom-call | flops 1000 | bytes 1000 | tf_op jit(solution)/shard_map/pallas_call | solution.py:280
  19.3 0.0 collective-permute-done.4.we
  19.3 0.5 %collective-permute-done.3.ea = f32[776,128]{1,0:T(8,128)S(1)} collective-permute-done((f32[776,128]{1,0:T(8,128)S(1)}, f32[776,128]{1,0:T(8,128)S(1)}, u32[]{:S(2)}, u32[]{:S(2)}) %collective-permute-start.3) | collective-permute-done | bytes 397344 | tf_op jit(solution)/shard_map/ppermute | solution.py:276
  19.8 0.0 collective-permute-done.1.c1
  19.8 1.1 %shard_map.61 = (f32[1024,128]{1,0:T(8,128)S(1)}, f32[1024,128]{1,0:T(8,128)S(1)}, f32[128,128]{1,0:T(8,128)}) custom-call(f32[]{:T(128)S(6)} %copy.8.beta, f32[128,128]{1,0:T(8,128)S(1)} %get-tuple-element.19.pairs, f32[1168,128]{1,0:T(8,128)S(1)} %get-tuple-element.20.few, f32[1544,128]{1,0:T(8,128)S(1)} %collective-permute-done.1.c1, ...), custom_call_target="tpu_custom_call" | custom-call | flops 1000 | bytes 1000 | tf_op jit(solution)/shard_map/pallas_call | solution.py:280
  20.9 2.8 %collective-permute-start.5 = (f32[1024,128]{1,0:T(8,128)S(1)}, f32[1024,128]{1,0:T(8,128)S(1)}, u32[]{:S(2)}, u32[]{:S(2)}) collective-permute-start(f32[1024,128]{1,0:T(8,128)S(1)} %get-tuple-element.23.ccm), channel_id=1, source_target_pairs={{0,112},{1,113},{2,114},{3,115},{4,116},{5,117},{6,118},{7,119},{8... | collective-permute-start | bytes 1572872 | tf_op jit(solution)/shard_map/ppermute | solution.py:276
  23.6 1.2 %collective-permute-start.6 = (f32[1024,128]{1,0:T(8,128)S(1)}, f32[1024,128]{1,0:T(8,128)S(1)}, u32[]{:S(2)}, u32[]{:S(2)}) collective-permute-start(f32[1024,128]{1,0:T(8,128)S(1)} %get-tuple-element.24.tcm), channel_id=1, source_target_pairs={{0,16},{1,17},{2,18},{3,19},{4,20},{5,21},{6,22},{7,23},{8,24},{9,... | collective-permute-start | bytes 1572872 | tf_op jit(solution)/shard_map/ppermute | solution.py:276
  24.8 7.5 %all-to-all-start = ((f32[128,1,128]{2,1,0:T(1,128)}), f32[128,1,128]{2,1,0:T(1,128)S(1)}, u32[]{:S(2)}, u32[]{:S(2)}) async-start(f32[128,1,128]{2,1,0:T(1,128)} %bitcast.6), calls=%async_computation | async-start | bytes 131072 | tf_op jit(solution)/shard_map/all_to_all | solution.py:328
  32.3 0.0 collective-permute-done.2.c2
  32.3 0.0 collective-permute-done.5.cc
  32.3 0.0 collective-permute-done.6.tc
  32.3 4.7 %shard_map.62.after = f32[1,4,9,128,128]{4,3,2,1,0:T(8,128)} custom-call(s32[1,4,9]{2,1,0:T(4,128)} %pat.3, bf16[32,128,128]{2,1,0:T(8,128)(2,1)} %get-tuple-element.16.lefts, f32[36,128,128]{2,1,0:T(8,128)} %get-tuple-element.17.acc, f32[1544,128]{1,0:T(8,128)S(1)} %collective-permute-done.1.c1, f32[1536,128]{1,0:T(8,128)} %collective-permute-done.2.c2, ...), custom_call_target="tpu_custom_call" | custom-call | flops 1000 | bytes 1000 | tf_op jit(solution)/shard_map/pallas_call | solution.py:280
  37.1 5.0 %all-to-all-done = f32[128,1,128]{2,1,0:T(1,128)S(1)} async-done(((f32[128,1,128]{2,1,0:T(1,128)}), f32[128,1,128]{2,1,0:T(1,128)S(1)}, u32[]{:S(2)}, u32[]{:S(2)}) %all-to-all-start) | async-done | bytes 65568 | tf_op jit(solution)/shard_map/all_to_all | solution.py:328
  42.1 0.6 %shard_map.63 = f32[1,1]{1,0:T(1,128)} custom-call(f32[128,128]{1,0:T(8,128)S(1)} %bitcast.5, f32[1,4,9,128,128]{4,3,2,1,0:T(8,128)} %shard_map.62.after), custom_call_target="tpu_custom_call" | custom-call | flops 1000 | bytes 1000 | tf_op jit(solution)/shard_map/pallas_call | solution.py:280
Async XLA Ops:
  3.3 10.9 %collective-permute-start = (f32[3080,128]{1,0:T(8,128)S(1)}, f32[3080,128]{1,0:T(8,128)}, u32[]{:S(2)}, u32[]{:S(2)}) collective-permute-start(f32[3080,128]{1,0:T(8,128)S(1)} %get-tuple-element.15.twm), channel_id=1, source_target_pairs={{0,16},{1,17},{2,18},{3,19},{4,20},{5,21},{6,22},{7,23},{8,24},{9,... | collective-permute-start | bytes 4730888 | tf_op jit(solution)/shard_map/ppermute | solution.py:276
  4.8 15.0 %collective-permute-start.1 = (f32[1544,128]{1,0:T(8,128)}, f32[1544,128]{1,0:T(8,128)S(1)}, u32[]{:S(2)}, u32[]{:S(2)}) collective-permute-start(f32[1544,128]{1,0:T(8,128)} %get-tuple-element.14.c1m), channel_id=1, source_target_pairs={{0,112},{1,113},{2,114},{3,115},{4,116},{5,117},{6,118},{7,119},{8... | collective-permute-start | bytes 2371592 | tf_op jit(solution)/shard_map/ppermute | solution.py:276
  6.2 13.6 %collective-permute-start.3 = (f32[776,128]{1,0:T(8,128)S(1)}, f32[776,128]{1,0:T(8,128)S(1)}, u32[]{:S(2)}, u32[]{:S(2)}) collective-permute-start(f32[776,128]{1,0:T(8,128)S(1)} %get-tuple-element.21), channel_id=1, source_target_pairs={{0,1},{1,2},{2,3},{3,4},{4,5},{5,6},{6,7},{7,8},{8,9},{9,10},{10,1... | collective-permute-start | bytes 1191944 | tf_op jit(solution)/shard_map/ppermute | solution.py:276
  7.4 11.9 %collective-permute-start.4 = (f32[768,128]{1,0:T(8,128)}, f32[768,128]{1,0:T(8,128)S(1)}, u32[]{:S(2)}, u32[]{:S(2)}) collective-permute-start(f32[768,128]{1,0:T(8,128)} %get-tuple-element.22), channel_id=1, source_target_pairs={{0,15},{1,0},{2,1},{3,2},{4,3},{5,4},{6,5},{7,6},{8,7},{9,8},{10,9... | collective-permute-start | bytes 1179656 | tf_op jit(solution)/shard_map/ppermute | solution.py:276
  12.1 20.2 %collective-permute-start.2 = (f32[1536,128]{1,0:T(8,128)}, f32[1536,128]{1,0:T(8,128)}, u32[]{:S(2)}, u32[]{:S(2)}) collective-permute-start(f32[1536,128]{1,0:T(8,128)} %get-tuple-element.18), channel_id=1, source_target_pairs={{0,112},{1,113},{2,114},{3,115},{4,116},{5,117},{6,118},{7,119},{8... | collective-permute-start | bytes 2359304 | tf_op jit(solution)/shard_map/ppermute | solution.py:276
  20.9 11.4 %collective-permute-start.5 = (f32[1024,128]{1,0:T(8,128)S(1)}, f32[1024,128]{1,0:T(8,128)S(1)}, u32[]{:S(2)}, u32[]{:S(2)}) collective-permute-start(f32[1024,128]{1,0:T(8,128)S(1)} %get-tuple-element.23.ccm), channel_id=1, source_target_pairs={{0,112},{1,113},{2,114},{3,115},{4,116},{5,117},{6,118},{7,119},{8... | collective-permute-start | bytes 1572872 | tf_op jit(solution)/shard_map/ppermute | solution.py:276
  23.6 8.7 %collective-permute-start.6 = (f32[1024,128]{1,0:T(8,128)S(1)}, f32[1024,128]{1,0:T(8,128)S(1)}, u32[]{:S(2)}, u32[]{:S(2)}) collective-permute-start(f32[1024,128]{1,0:T(8,128)S(1)} %get-tuple-element.24.tcm), channel_id=1, source_target_pairs={{0,16},{1,17},{2,18},{3,19},{4,20},{5,21},{6,22},{7,23},{8,24},{9,... | collective-permute-start | bytes 1572872 | tf_op jit(solution)/shard_map/ppermute | solution.py:276
  24.8 17.3 %all-to-all-start = ((f32[128,1,128]{2,1,0:T(1,128)}), f32[128,1,128]{2,1,0:T(1,128)S(1)}, u32[]{:S(2)}, u32[]{:S(2)}) async-start(f32[128,1,128]{2,1,0:T(1,128)} %bitcast.6), calls=%async_computation | async-start | bytes 131072 | tf_op jit(solution)/shard_map/all_to_all | solution.py:328

commit v8 on v7

--- a/solution.py
+++ b/solution.py
@@ -73,7 +73,7 @@
     odd = lax.rem(lax.axis_index("row"), 2)
     dma = Copies(sems)
     table_load = dma.start(pat, table)
-    order = [(CR, v) for v in (0, 3, 1, 2)] + [(k, v) for v in (0, 3) for k in (MID, TW)] + [(k, v) for k in (MID, TW) for v in (1, 2)]
+    order = [(CR, v) for v in (0, 3, 1, 2)] + [(MID, 0), (TW, 0)] + [(MID, v) for v in (3, 1, 2)] + [(TW, v) for v in (3, 1, 2)]
     loads = {}
     for kind, v in order:
         slots = pl.ds(slot(kind, -1, odd), 3)

time: 43 us -> 43 us (level)
  no operation moved by 1% of the time
where the time goes in v8:
time: 43 us; the launch traced here: 42.7 us
  starting transfers between devices  21 us (49%)
  Pallas kernels  14.2 us (33%)
  waiting for transfers between devices  5.52 us (13%)
  between operations  2.01 us (5%)
    pallas_call x5, Pallas kernels, call(): pl.pallas_call(kernel, out_shape=[pltpu.HBM(o.shape, o.dtype) if s is ANY...  14.2 us
    ppermute x7, starting transfers between devices, moved(): return lax.ppermute(message, AXES, pairs)  13.5 us
    all_to_all x1, starting transfers between devices, body(): gathered = lax.all_to_all(shares, AXES, 0, 0)  7.48 us
    all_to_all x1, waiting for transfers between devices, body(): gathered = lax.all_to_all(shares, AXES, 0, 0)  5 us
  transfers between devices with their start and end apart: 8, of which 2 were waited for; matrix products, arithmetic and copies ran while one was open for 0% of the time, Pallas kernels for 25%

profile of v8, /device:TPU:1, one launch (start us, length us, event | category | flops | bytes accessed | tf_op | source)
XLA Modules:
  0.0 42.7 jit_solution(16485405980759194068)
XLA Ops:
  0.6 2.7 %shard_map.59 = (f32[1544,128]{1,0:T(8,128)}, f32[776,128]{1,0:T(8,128)S(1)}, f32[3080,128]{1,0:T(8,128)S(1)}, f32[1536,128]{1,0:T(8,128)}, f32[768,128]{1,0:T(8,128)}) custom-call(f32[1,4,9,128,128]{4,3,2,1,0:T(8,128)} %x.1, s32[1,4,9]{2,1,0:T(4,128)} %pat.3), custom_call_target="tpu_custom_call" | custom-call | flops 1000 | bytes 1000 | tf_op jit(solution)/shard_map/pallas_call | solution.py:280
  3.3 1.5 %collective-permute-start = (f32[3080,128]{1,0:T(8,128)S(1)}, f32[3080,128]{1,0:T(8,128)}, u32[]{:S(2)}, u32[]{:S(2)}) collective-permute-start(f32[3080,128]{1,0:T(8,128)S(1)} %get-tuple-element.15.twm), channel_id=1, source_target_pairs={{0,16},{1,17},{2,18},{3,19},{4,20},{5,21},{6,22},{7,23},{8,24},{9,... | collective-permute-start | bytes 4730888 | tf_op jit(solution)/shard_map/ppermute | solution.py:276
  4.8 1.4 %collective-permute-start.1 = (f32[1544,128]{1,0:T(8,128)}, f32[1544,128]{1,0:T(8,128)S(1)}, u32[]{:S(2)}, u32[]{:S(2)}) collective-permute-start(f32[1544,128]{1,0:T(8,128)} %get-tuple-element.14.c1m), channel_id=1, source_target_pairs={{0,112},{1,113},{2,114},{3,115},{4,116},{5,117},{6,118},{7,119},{8... | collective-permute-start | bytes 2371592 | tf_op jit(solution)/shard_map/ppermute | solution.py:276
  6.2 1.2 %collective-permute-start.3 = (f32[776,128]{1,0:T(8,128)S(1)}, f32[776,128]{1,0:T(8,128)S(1)}, u32[]{:S(2)}, u32[]{:S(2)}) collective-permute-start(f32[776,128]{1,0:T(8,128)S(1)} %get-tuple-element.21), channel_id=1, source_target_pairs={{0,1},{1,2},{2,3},{3,4},{4,5},{5,6},{6,7},{7,8},{8,9},{9,10},{10,1... | collective-permute-start | bytes 1191944 | tf_op jit(solution)/shard_map/ppermute | solution.py:276
  7.4 4.7 %collective-permute-start.4 = (f32[768,128]{1,0:T(8,128)}, f32[768,128]{1,0:T(8,128)S(1)}, u32[]{:S(2)}, u32[]{:S(2)}) collective-permute-start(f32[768,128]{1,0:T(8,128)} %get-tuple-element.22), channel_id=1, source_target_pairs={{0,15},{1,0},{2,1},{3,2},{4,3},{5,4},{6,5},{7,6},{8,7},{9,8},{10,9... | collective-permute-start | bytes 1179656 | tf_op jit(solution)/shard_map/ppermute | solution.py:276
  12.1 0.8 %collective-permute-start.2 = (f32[1536,128]{1,0:T(8,128)}, f32[1536,128]{1,0:T(8,128)}, u32[]{:S(2)}, u32[]{:S(2)}) collective-permute-start(f32[1536,128]{1,0:T(8,128)} %get-tuple-element.18), channel_id=1, source_target_pairs={{0,112},{1,113},{2,114},{3,115},{4,116},{5,117},{6,118},{7,119},{8... | collective-permute-start | bytes 2359304 | tf_op jit(solution)/shard_map/ppermute | solution.py:276
  14.2 0.0 collective-permute-done.tw
  14.2 5.1 %shard_map.60 = (f32[36,128,128]{2,1,0:T(8,128)}, bf16[32,128,128]{2,1,0:T(8,128)(2,1)}, f32[128,128]{1,0:T(8,128)S(1)}, f32[1168,128]{1,0:T(8,128)S(1)}) custom-call(f32[]{:T(128)S(6)} %copy.7.alpha, f32[]{:T(128)S(6)} %copy.8.beta, f32[1544,128]{1,0:T(8,128)} %get-tuple-element.14.c1m, f32[3080,128]{1,0:T(8,128)S(1)} %get-tuple-element.15.twm, ...), custom_call_target="tpu_custom_call" | custom-call | flops 1000 | bytes 1000 | tf_op jit(solution)/shard_map/pallas_call | solution.py:280
  19.3 0.0 collective-permute-done.4.we
  19.3 0.5 %collective-permute-done.3.ea = f32[776,128]{1,0:T(8,128)S(1)} collective-permute-done((f32[776,128]{1,0:T(8,128)S(1)}, f32[776,128]{1,0:T(8,128)S(1)}, u32[]{:S(2)}, u32[]{:S(2)}) %collective-permute-start.3) | collective-permute-done | bytes 397344 | tf_op jit(solution)/shard_map/ppermute | solution.py:276
  19.8 0.0 collective-permute-done.1.c1
  19.8 1.1 %shard_map.61 = (f32[1024,128]{1,0:T(8,128)S(1)}, f32[1024,128]{1,0:T(8,128)S(1)}, f32[128,128]{1,0:T(8,128)}) custom-call(f32[]{:T(128)S(6)} %copy.8.beta, f32[128,128]{1,0:T(8,128)S(1)} %get-tuple-element.19.pairs, f32[1168,128]{1,0:T(8,128)S(1)} %get-tuple-element.20.few, f32[1544,128]{1,0:T(8,128)S(1)} %collective-permute-done.1.c1, ...), custom_call_target="tpu_custom_call" | custom-call | flops 1000 | bytes 1000 | tf_op jit(solution)/shard_map/pallas_call | solution.py:280
  20.9 2.8 %collective-permute-start.5 = (f32[1024,128]{1,0:T(8,128)S(1)}, f32[1024,128]{1,0:T(8,128)S(1)}, u32[]{:S(2)}, u32[]{:S(2)}) collective-permute-start(f32[1024,128]{1,0:T(8,128)S(1)} %get-tuple-element.23.ccm), channel_id=1, source_target_pairs={{0,112},{1,113},{2,114},{3,115},{4,116},{5,117},{6,118},{7,119},{8... | collective-permute-start | bytes 1572872 | tf_op jit(solution)/shard_map/ppermute | solution.py:276
  23.6 1.2 %collective-permute-start.6 = (f32[1024,128]{1,0:T(8,128)S(1)}, f32[1024,128]{1,0:T(8,128)S(1)}, u32[]{:S(2)}, u32[]{:S(2)}) collective-permute-start(f32[1024,128]{1,0:T(8,128)S(1)} %get-tuple-element.24.tcm), channel_id=1, source_target_pairs={{0,16},{1,17},{2,18},{3,19},{4,20},{5,21},{6,22},{7,23},{8,24},{9,... | collective-permute-start | bytes 1572872 | tf_op jit(solution)/shard_map/ppermute | solution.py:276
  24.8 7.5 %all-to-all-start = ((f32[128,1,128]{2,1,0:T(1,128)}), f32[128,1,128]{2,1,0:T(1,128)S(1)}, u32[]{:S(2)}, u32[]{:S(2)}) async-start(f32[128,1,128]{2,1,0:T(1,128)} %bitcast.6), calls=%async_computation | async-start | bytes 131072 | tf_op jit(solution)/shard_map/all_to_all | solution.py:328
  32.3 0.0 collective-permute-done.2.c2
  32.3 0.0 collective-permute-done.5.cc
  32.3 0.0 collective-permute-done.6.tc
  32.3 4.7 %shard_map.62.after = f32[1,4,9,128,128]{4,3,2,1,0:T(8,128)} custom-call(s32[1,4,9]{2,1,0:T(4,128)} %pat.3, bf16[32,128,128]{2,1,0:T(8,128)(2,1)} %get-tuple-element.16.lefts, f32[36,128,128]{2,1,0:T(8,128)} %get-tuple-element.17.acc, f32[1544,128]{1,0:T(8,128)S(1)} %collective-permute-done.1.c1, f32[1536,128]{1,0:T(8,128)} %collective-permute-done.2.c2, ...), custom_call_target="tpu_custom_call" | custom-call | flops 1000 | bytes 1000 | tf_op jit(solution)/shard_map/pallas_call | solution.py:280
  37.1 5.0 %all-to-all-done = f32[128,1,128]{2,1,0:T(1,128)S(1)} async-done(((f32[128,1,128]{2,1,0:T(1,128)}), f32[128,1,128]{2,1,0:T(1,128)S(1)}, u32[]{:S(2)}, u32[]{:S(2)}) %all-to-all-start) | async-done | bytes 65568 | tf_op jit(solution)/shard_map/all_to_all | solution.py:328
  42.1 0.6 %shard_map.63 = f32[1,1]{1,0:T(1,128)} custom-call(f32[128,128]{1,0:T(8,128)S(1)} %bitcast.5, f32[1,4,9,128,128]{4,3,2,1,0:T(8,128)} %shard_map.62.after), custom_call_target="tpu_custom_call" | custom-call | flops 1000 | bytes 1000 | tf_op jit(solution)/shard_map/pallas_call | solution.py:280
Async XLA Ops:
  3.3 10.9 %collective-permute-start = (f32[3080,128]{1,0:T(8,128)S(1)}, f32[3080,128]{1,0:T(8,128)}, u32[]{:S(2)}, u32[]{:S(2)}) collective-permute-start(f32[3080,128]{1,0:T(8,128)S(1)} %get-tuple-element.15.twm), channel_id=1, source_target_pairs={{0,16},{1,17},{2,18},{3,19},{4,20},{5,21},{6,22},{7,23},{8,24},{9,... | collective-permute-start | bytes 4730888 | tf_op jit(solution)/shard_map/ppermute | solution.py:276
  4.8 15.0 %collective-permute-start.1 = (f32[1544,128]{1,0:T(8,128)}, f32[1544,128]{1,0:T(8,128)S(1)}, u32[]{:S(2)}, u32[]{:S(2)}) collective-permute-start(f32[1544,128]{1,0:T(8,128)} %get-tuple-element.14.c1m), channel_id=1, source_target_pairs={{0,112},{1,113},{2,114},{3,115},{4,116},{5,117},{6,118},{7,119},{8... | collective-permute-start | bytes 2371592 | tf_op jit(solution)/shard_map/ppermute | solution.py:276
  6.2 13.6 %collective-permute-start.3 = (f32[776,128]{1,0:T(8,128)S(1)}, f32[776,128]{1,0:T(8,128)S(1)}, u32[]{:S(2)}, u32[]{:S(2)}) collective-permute-start(f32[776,128]{1,0:T(8,128)S(1)} %get-tuple-element.21), channel_id=1, source_target_pairs={{0,1},{1,2},{2,3},{3,4},{4,5},{5,6},{6,7},{7,8},{8,9},{9,10},{10,1... | collective-permute-start | bytes 1191944 | tf_op jit(solution)/shard_map/ppermute | solution.py:276
  7.4 11.9 %collective-permute-start.4 = (f32[768,128]{1,0:T(8,128)}, f32[768,128]{1,0:T(8,128)S(1)}, u32[]{:S(2)}, u32[]{:S(2)}) collective-permute-start(f32[768,128]{1,0:T(8,128)} %get-tuple-element.22), channel_id=1, source_target_pairs={{0,15},{1,0},{2,1},{3,2},{4,3},{5,4},{6,5},{7,6},{8,7},{9,8},{10,9... | collective-permute-start | bytes 1179656 | tf_op jit(solution)/shard_map/ppermute | solution.py:276
  12.1 20.2 %collective-permute-start.2 = (f32[1536,128]{1,0:T(8,128)}, f32[1536,128]{1,0:T(8,128)}, u32[]{:S(2)}, u32[]{:S(2)}) collective-permute-start(f32[1536,128]{1,0:T(8,128)} %get-tuple-element.18), channel_id=1, source_target_pairs={{0,112},{1,113},{2,114},{3,115},{4,116},{5,117},{6,118},{7,119},{8... | collective-permute-start | bytes 2359304 | tf_op jit(solution)/shard_map/ppermute | solution.py:276
  20.9 11.4 %collective-permute-start.5 = (f32[1024,128]{1,0:T(8,128)S(1)}, f32[1024,128]{1,0:T(8,128)S(1)}, u32[]{:S(2)}, u32[]{:S(2)}) collective-permute-start(f32[1024,128]{1,0:T(8,128)S(1)} %get-tuple-element.23.ccm), channel_id=1, source_target_pairs={{0,112},{1,113},{2,114},{3,115},{4,116},{5,117},{6,118},{7,119},{8... | collective-permute-start | bytes 1572872 | tf_op jit(solution)/shard_map/ppermute | solution.py:276
  23.6 8.7 %collective-permute-start.6 = (f32[1024,128]{1,0:T(8,128)S(1)}, f32[1024,128]{1,0:T(8,128)S(1)}, u32[]{:S(2)}, u32[]{:S(2)}) collective-permute-start(f32[1024,128]{1,0:T(8,128)S(1)} %get-tuple-element.24.tcm), channel_id=1, source_target_pairs={{0,16},{1,17},{2,18},{3,19},{4,20},{5,21},{6,22},{7,23},{8,24},{9,... | collective-permute-start | bytes 1572872 | tf_op jit(solution)/shard_map/ppermute | solution.py:276
  24.8 17.3 %all-to-all-start = ((f32[128,1,128]{2,1,0:T(1,128)}), f32[128,1,128]{2,1,0:T(1,128)S(1)}, u32[]{:S(2)}, u32[]{:S(2)}) async-start(f32[128,1,128]{2,1,0:T(1,128)} %bitcast.6), calls=%async_computation | async-start | bytes 131072 | tf_op jit(solution)/shard_map/all_to_all | solution.py:328
